TPU v7x, 32 devices: a whole 2x2x4 slice. The times are simulated.
32 devices in a mesh: dp: 8 (over z, y), fsdp: 4 (over x, core).
Axes of the slice: x: 2, y: 2, z: 4, core: 2. Of those that a mesh axis runs over, the one named last changes fastest.
Arguments:
- inputs: bfloat16 [2, 8, 1024, 1280], P(None, 'dp', 'fsdp'), may hold values from -6 to 6
- positions: int32 [2, 8, 1024], P(None, 'dp', 'fsdp'), may hold values from 0 to 799, as said below
- cotangent: bfloat16 [2, 8, 1024, 1280], P(None, 'dp', 'fsdp'), may hold values from -6 to 6
- attn_gain: bfloat16 [1280], P(('dp', 'fsdp')), may hold values from 0.5 to 1.5
- w_query: bfloat16 [1280, 1280], P(('dp', 'fsdp')), may hold values from -0.15625 to 0.15625
- key_matrix: bfloat16 [1280, 320], P(('dp', 'fsdp')), may hold values from -0.15625 to 0.15625
- value_matrix: bfloat16 [1280, 320], P(('dp', 'fsdp')), may hold values from -0.15625 to 0.15625
- w_out: bfloat16 [1280, 1280], P(('dp', 'fsdp')), may hold values from -1.5 to 1.5
- mlp_gain: bfloat16 [1280], P(('dp', 'fsdp')), may hold values from 0.5 to 1.5
- w_gate: bfloat16 [1280, 3584], P(('dp', 'fsdp')), may hold values from -0.15625 to 0.15625
- w_up: bfloat16 [1280, 3584], P(('dp', 'fsdp')), may hold values from -0.15625 to 0.15625
- w_down: bfloat16 [3584, 1280], P(('dp', 'fsdp')), may hold values from -0.09375 to 0.09375
Outputs:
- result: bfloat16 [2, 8, 1024, 1280], P(None, 'dp', 'fsdp')
- input_grad: bfloat16 [2, 8, 1024, 1280], P(None, 'dp', 'fsdp')
- grad_attn_gain: float32 [1280], P(('dp', 'fsdp'))
- grad_query: float32 [1280, 1280], P(('dp', 'fsdp'))
- grad_key: float32 [1280, 320], P(('dp', 'fsdp'))
- grad_value: float32 [1280, 320], P(('dp', 'fsdp'))
- grad_out: float32 [1280, 1280], P(('dp', 'fsdp'))
- grad_mlp_gain: float32 [1280], P(('dp', 'fsdp'))
- grad_gate: float32 [1280, 3584], P(('dp', 'fsdp'))
- grad_up: float32 [1280, 3584], P(('dp', 'fsdp'))
- grad_down: float32 [3584, 1280], P(('dp', 'fsdp'))
Inputs may be any that keep to these rules, and one draw needn't show every extreme that they name: `positions`: positions count 0, 1, 2, ... within each document and restart at 0 where a document begins; the first token of every sequence has position 0. Every sequence holds a document of exactly 800 tokens that starts within its first 65 tokens.
All inputs are finite; a program needn't handle non-finite values.
Results may differ from a plain program's by a relative error of at most 0.015.
Values may be sent and summed in bfloat16 or wider, within the bound.
A program may use at most 384 MiB of HBM per device.

v0:
```python
import jax
import jax.numpy as jnp
from jax import lax
from jax.sharding import PartitionSpec as P

MODEL_DIMENSION = 1280
HEADS = 20
KV_HEADS = 5
HD = 64
FF = 3584
HQ = 1280
KEY_FEATURES = 320
GROUP = 4


EPSILON = 1e-05
NEGATIVE = -1e30
ROPE_BASE = 10000.0


def rope_tables(places):
    half = HD // 2
    freqs = ROPE_BASE ** (-jnp.arange(half).astype(jnp.float32) / half)
    angles = places.astype(jnp.float32)[:, None] * freqs[None, :]
    return (jnp.cos(angles), jnp.sin(angles))


def split_heads(field, head_count):
    shaped = field.reshape(field.shape[0], head_count, HD)
    return (shaped[..., : HD // 2], shaped[..., HD // 2 :])


def rotate(field, cos_table, sin_table, head_count):
    first_half, second_half = split_heads(field, head_count)
    cos_heads = cos_table[:, None, :]
    sin_heads = sin_table[:, None, :]
    turned = jnp.concatenate(
        [
            first_half * cos_heads - second_half * sin_heads,
            second_half * cos_heads + first_half * sin_heads,
        ],
        -1,
    )
    return turned.reshape(field.shape[0], head_count * HD)


def rotate_back(field, cos_table, sin_table, head_count):
    first_half, second_half = split_heads(field, head_count)
    cos_heads = cos_table[:, None, :]
    sin_heads = sin_table[:, None, :]
    turned = jnp.concatenate(
        [
            first_half * cos_heads + second_half * sin_heads,
            second_half * cos_heads - first_half * sin_heads,
        ],
        -1,
    )
    return turned.reshape(field.shape[0], head_count * HD)


def plain_dot(left, right):
    return jnp.dot(left, right, preferred_element_type=jnp.float32)


def left_dot(left, right):
    return lax.dot_general(
        left, right, (((0,), (0,)), ((), ())), preferred_element_type=jnp.float32
    )


def right_dot(left, right):
    return lax.dot_general(
        left, right, (((1,), (1,)), ((), ())), preferred_element_type=jnp.float32
    )


def norm_back(grad_normed, inputs_float, inverse):
    return inverse * (
        grad_normed
        - inputs_float * inverse * inverse * jnp.mean(grad_normed * inputs_float, -1, keepdims=True)
    )


def flatten_all(grads):
    return tuple((g.reshape(-1) for g in grads))


def shape_like(flat_parts, shards):
    return tuple((f.reshape(s.shape) for f, s in zip(flat_parts, shards)))


def on_device(
    inputs,
    positions,
    cotangent,
    attn_gain,
    w_query,
    key_matrix,
    value_matrix,
    w_out,
    mlp_gain,
    w_gate,
    w_up,
    w_down,
):
    row_count = inputs.shape[2]
    model_width = inputs.shape[3]
    sequence_length = row_count * lax.axis_size("fsdp")
    first_row = lax.axis_index("fsdp") * row_count
    query_index = first_row + jnp.arange(row_count, dtype=jnp.int32)
    key_index = jnp.arange(sequence_length, dtype=jnp.int32)
    score_scale = HD ** (-0.5)
    shards = (attn_gain, w_query, key_matrix, value_matrix, w_out, mlp_gain, w_gate, w_up, w_down)

    def micro_step(totals, scan_items):
        x_block, place_block, cot_block = scan_items
        gathered = (
            lax.all_gather(attn_gain, ("dp", "fsdp"), axis=0, tiled=True),
            lax.all_gather(w_query, ("dp", "fsdp"), axis=0, tiled=True),
            lax.all_gather(key_matrix, ("dp", "fsdp"), axis=0, tiled=True),
            lax.all_gather(value_matrix, ("dp", "fsdp"), axis=0, tiled=True),
            lax.all_gather(w_out, ("dp", "fsdp"), axis=0, tiled=True),
            lax.all_gather(mlp_gain, ("dp", "fsdp"), axis=0, tiled=True),
            lax.all_gather(w_gate, ("dp", "fsdp"), axis=0, tiled=True),
            lax.all_gather(w_up, ("dp", "fsdp"), axis=0, tiled=True),
            lax.all_gather(w_down, ("dp", "fsdp"), axis=0, tiled=True),
        )
        (
            gain_one,
            query_full,
            key_full,
            value_full,
            out_full,
            gain_two,
            gate_full,
            up_full,
            down_full,
        ) = gathered
        x_float = x_block.reshape(row_count, model_width).astype(jnp.float32)
        places = place_block.reshape(row_count)
        cos_table, sin_table = rope_tables(places)
        doc_start = query_index - places
        allowed = (key_index[None, :] <= query_index[:, None]) & (
            key_index[None, :] >= doc_start[:, None]
        )
        attn_inverse = lax.rsqrt(jnp.mean(x_float * x_float, -1, keepdims=True) + EPSILON)
        attn_gain_f = gain_one.astype(jnp.float32)
        normed = (x_float * attn_inverse * attn_gain_f).astype(jnp.bfloat16)
        queries = (
            rotate(plain_dot(normed, query_full), cos_table, sin_table, HEADS) * score_scale
        ).astype(jnp.bfloat16)
        key_rows = rotate(plain_dot(normed, key_full), cos_table, sin_table, KV_HEADS).astype(
            jnp.bfloat16
        )
        value_rows = plain_dot(normed, value_full).astype(jnp.bfloat16)
        keys_all, values_all = (
            lax.all_gather(key_rows, "fsdp", axis=0, tiled=True),
            lax.all_gather(value_rows, "fsdp", axis=0, tiled=True),
        )
        grouped = queries.reshape(row_count, KV_HEADS, GROUP, HD)
        key_heads = keys_all.reshape(sequence_length, KV_HEADS, HD)
        value_heads = values_all.reshape(sequence_length, KV_HEADS, HD)
        scores = jnp.einsum(
            "qkgd,skd->kgqs", grouped, key_heads, preferred_element_type=jnp.float32
        )
        scores = jnp.where(allowed[None, None], scores, NEGATIVE)
        row_max = jnp.max(scores, -1, keepdims=True)
        row_total = jnp.sum(jnp.exp(scores - row_max), -1, keepdims=True)
        log_total = row_max + jnp.log(row_total)
        probs_low = jnp.exp(scores - log_total).astype(jnp.bfloat16)
        attended = jnp.einsum(
            "kgqs,skd->qkgd", probs_low, value_heads, preferred_element_type=jnp.float32
        )
        attended = attended.reshape(row_count, HQ).astype(jnp.bfloat16)
        mixed = x_float + plain_dot(attended, out_full)
        mlp_inverse = lax.rsqrt(jnp.mean(mixed * mixed, -1, keepdims=True) + EPSILON)
        mlp_gain_f = gain_two.astype(jnp.float32)
        normed_mlp = (mixed * mlp_inverse * mlp_gain_f).astype(jnp.bfloat16)
        gate_pre = plain_dot(normed_mlp, gate_full)
        up_proj = plain_dot(normed_mlp, up_full)
        gate_sig = jax.nn.sigmoid(gate_pre)
        hidden = (gate_pre * gate_sig * up_proj).astype(jnp.bfloat16)
        output = (mixed + plain_dot(hidden, down_full)).astype(jnp.bfloat16)
        gathered = (
            lax.all_gather(attn_gain, ("dp", "fsdp"), axis=0, tiled=True),
            lax.all_gather(w_query, ("dp", "fsdp"), axis=0, tiled=True),
            lax.all_gather(key_matrix, ("dp", "fsdp"), axis=0, tiled=True),
            lax.all_gather(value_matrix, ("dp", "fsdp"), axis=0, tiled=True),
            lax.all_gather(w_out, ("dp", "fsdp"), axis=0, tiled=True),
            lax.all_gather(mlp_gain, ("dp", "fsdp"), axis=0, tiled=True),
            lax.all_gather(w_gate, ("dp", "fsdp"), axis=0, tiled=True),
            lax.all_gather(w_up, ("dp", "fsdp"), axis=0, tiled=True),
            lax.all_gather(w_down, ("dp", "fsdp"), axis=0, tiled=True),
        )
        (
            gain_one,
            query_full,
            key_full,
            value_full,
            out_full,
            gain_two,
            gate_full,
            up_full,
            down_full,
        ) = gathered
        cot_low = cot_block.reshape(row_count, model_width)
        cot_float = cot_low.astype(jnp.float32)
        grad_down = left_dot(hidden, cot_low)
        grad_hidden = right_dot(cot_low, down_full)
        sig_slope = gate_sig * (1.0 + gate_pre * (1.0 - gate_sig))
        grad_gate_pre = (grad_hidden * up_proj * sig_slope).astype(jnp.bfloat16)
        grad_up_pre = (grad_hidden * gate_pre * gate_sig).astype(jnp.bfloat16)
        grad_gate = left_dot(normed_mlp, grad_gate_pre)
        grad_up = left_dot(normed_mlp, grad_up_pre)
        grad_normed_mlp = right_dot(grad_gate_pre, gate_full) + right_dot(grad_up_pre, up_full)
        grad_mlp_gain = jnp.sum(grad_normed_mlp * mixed * mlp_inverse, 0)
        grad_mixed = cot_float + norm_back(grad_normed_mlp * mlp_gain_f, mixed, mlp_inverse)
        grad_mixed_low = grad_mixed.astype(jnp.bfloat16)
        grad_out = left_dot(attended, grad_mixed_low)
        grad_attended = right_dot(grad_mixed_low, out_full).astype(jnp.bfloat16)
        grad_attended = grad_attended.reshape(row_count, KV_HEADS, GROUP, HD)
        scores_again = jnp.einsum(
            "qkgd,skd->kgqs", grouped, key_heads, preferred_element_type=jnp.float32
        )
        scores_again = jnp.where(allowed[None, None], scores_again, NEGATIVE)
        probabilities = jnp.exp(scores_again - log_total)
        grad_probs = jnp.einsum(
            "qkgd,skd->kgqs", grad_attended, value_heads, preferred_element_type=jnp.float32
        )
        row_dot = jnp.sum(probabilities * grad_probs, -1, keepdims=True)
        grad_scores = (probabilities * (grad_probs - row_dot)).astype(jnp.bfloat16)
        grad_query_rot = jnp.einsum(
            "kgqs,skd->qkgd", grad_scores, key_heads, preferred_element_type=jnp.float32
        )
        grad_query_rot = grad_query_rot.reshape(row_count, HQ)
        key_portion = jnp.einsum(
            "kgqs,qkgd->skd", grad_scores, grouped, preferred_element_type=jnp.float32
        )
        value_portion = jnp.einsum(
            "kgqs,qkgd->skd",
            probabilities.astype(jnp.bfloat16),
            grad_attended,
            preferred_element_type=jnp.float32,
        )
        key_sum, value_sum = (
            lax.psum_scatter(
                key_portion.reshape(sequence_length, KEY_FEATURES).astype(jnp.bfloat16),
                "fsdp",
                scatter_dimension=0,
                tiled=True,
            ).astype(jnp.float32),
            lax.psum_scatter(
                value_portion.reshape(sequence_length, KEY_FEATURES).astype(jnp.bfloat16),
                "fsdp",
                scatter_dimension=0,
                tiled=True,
            ).astype(jnp.float32),
        )
        grad_query_pre = rotate_back(
            grad_query_rot * score_scale, cos_table, sin_table, HEADS
        ).astype(jnp.bfloat16)
        grad_key_pre = rotate_back(key_sum, cos_table, sin_table, KV_HEADS).astype(jnp.bfloat16)
        grad_value_pre = value_sum.astype(jnp.bfloat16)
        grad_query = left_dot(normed, grad_query_pre)
        grad_key = left_dot(normed, grad_key_pre)
        grad_value = left_dot(normed, grad_value_pre)
        grad_normed = (
            right_dot(grad_query_pre, query_full)
            + right_dot(grad_key_pre, key_full)
            + right_dot(grad_value_pre, value_full)
        )
        grad_attn_gain = jnp.sum(grad_normed * x_float * attn_inverse, 0)
        grad_input = grad_mixed + norm_back(grad_normed * attn_gain_f, x_float, attn_inverse)
        fresh = (
            grad_attn_gain,
            grad_query,
            grad_key,
            grad_value,
            grad_out,
            grad_mlp_gain,
            grad_gate,
            grad_up,
            grad_down,
        )
        totals = tuple((acc + new for acc, new in zip(totals, fresh)))
        return (totals, (output, grad_input.astype(jnp.bfloat16)))

    initial = (
        jnp.zeros((MODEL_DIMENSION,), jnp.float32),
        jnp.zeros((MODEL_DIMENSION, HQ), jnp.float32),
        jnp.zeros((MODEL_DIMENSION, KEY_FEATURES), jnp.float32),
        jnp.zeros((MODEL_DIMENSION, KEY_FEATURES), jnp.float32),
        jnp.zeros((HQ, MODEL_DIMENSION), jnp.float32),
        jnp.zeros((MODEL_DIMENSION,), jnp.float32),
        jnp.zeros((MODEL_DIMENSION, FF), jnp.float32),
        jnp.zeros((MODEL_DIMENSION, FF), jnp.float32),
        jnp.zeros((FF, MODEL_DIMENSION), jnp.float32),
    )
    totals, (outputs, grad_inputs) = lax.scan(micro_step, initial, (inputs, positions, cotangent))
    flat = flatten_all(totals)
    summed_flat = (
        lax.psum_scatter(flat[0], ("dp", "fsdp"), scatter_dimension=0, tiled=True),
        lax.psum_scatter(flat[1], ("dp", "fsdp"), scatter_dimension=0, tiled=True),
        lax.psum_scatter(flat[2], ("dp", "fsdp"), scatter_dimension=0, tiled=True),
        lax.psum_scatter(flat[3], ("dp", "fsdp"), scatter_dimension=0, tiled=True),
        lax.psum_scatter(flat[4], ("dp", "fsdp"), scatter_dimension=0, tiled=True),
        lax.psum_scatter(flat[5], ("dp", "fsdp"), scatter_dimension=0, tiled=True),
        lax.psum_scatter(flat[6], ("dp", "fsdp"), scatter_dimension=0, tiled=True),
        lax.psum_scatter(flat[7], ("dp", "fsdp"), scatter_dimension=0, tiled=True),
        lax.psum_scatter(flat[8], ("dp", "fsdp"), scatter_dimension=0, tiled=True),
    )
    summed = shape_like(summed_flat, shards)
    return (
        outputs.reshape(inputs.shape),
        grad_inputs.reshape(inputs.shape),
        summed[0],
        summed[1],
        summed[2],
        summed[3],
        summed[4],
        summed[5],
        summed[6],
        summed[7],
        summed[8],
    )


def solution(mesh):
    in_specs = (
        P(None, "dp", "fsdp", None),
        P(None, "dp", "fsdp"),
        P(None, "dp", "fsdp", None),
        P(("dp", "fsdp")),
        P(("dp", "fsdp"), None),
        P(("dp", "fsdp"), None),
        P(("dp", "fsdp"), None),
        P(("dp", "fsdp"), None),
        P(("dp", "fsdp")),
        P(("dp", "fsdp"), None),
        P(("dp", "fsdp"), None),
        P(("dp", "fsdp"), None),
    )
    out_specs = (
        P(None, "dp", "fsdp", None),
        P(None, "dp", "fsdp", None),
        P(("dp", "fsdp")),
        P(("dp", "fsdp"), None),
        P(("dp", "fsdp"), None),
        P(("dp", "fsdp"), None),
        P(("dp", "fsdp"), None),
        P(("dp", "fsdp")),
        P(("dp", "fsdp"), None),
        P(("dp", "fsdp"), None),
        P(("dp", "fsdp"), None),
    )
    return jax.shard_map(
        on_device, mesh=mesh, in_specs=in_specs, out_specs=out_specs, check_vma=False
    )
```

profile of v0, /device:TPU:0, one launch (start us, length us, event | category | flops | bytes accessed | tf_op | source)
XLA Modules:
  0.0 2191.8 jit_solution(3636361592204793642)
XLA Ops:
  8.1 1049.5 %while.32 = (s32[]{:T(128)}, f32[1280]{0:T(1024)}, f32[1280,1280]{1,0:T(8,128)}, f32[1280,320]{0,1:T(8,128)}, f32[1280,320]{0,1:T(8,128)}, /*index=5*/f32[1280,1...) while((s32[]{:T(128)}, f32[1280]{0:T(1024)}, ...), condition=%wide.region_12.13_spmd.clone.clone, body=%wide.region_0.12_spmd.clone.clone.sunk | while | flops 31644293120 | bytes 1014841984 | solution.py:299
  14.4 42.1 %all-reduce.17 = (bf16[1280]{0:T(1024)(128)(2,1)S(1)}, bf16[1280]{0:T(1024)(128)(2,1)S(1)}) all-reduce(bf16[1280]{0:T(1024)(128)(2,1)S(1)} %dynamic-update-slice.6, bf16[1280]{0:T(1024)(128)(2,1)S(1)} %dynamic-update-slice.7), channel_id=1, replica_groups=mesh['dp'=8,'fsdp'=4] {'dp','fsdp'}, use_global_device_ids=true, to_apply=%add | all-reduce | flops 2560 | bytes 10240 | tf_op jit(solution)/shard_map/while
  56.5 44.3 %all_gather.69 = bf16[1280,320]{1,0:T(8,128)(2,1)S(1)} all-gather(bf16[40,320]{1,0:T(8,128)(2,1)} %get-tuple-element.727), channel_id=1, replica_groups=mesh['dp'=8,'fsdp'=4] {'dp','fsdp'}, dimensions={0}, use_global_device_ids=true | all-gather | bytes 844800 | tf_op jit(solution)/shard_map/while/body/eval_jaxpr/all_gather | solution.py:120
  103.5 40.9 %all_gather.72 = bf16[1280,320]{1,0:T(8,128)(2,1)S(1)} all-gather(bf16[40,320]{1,0:T(8,128)(2,1)S(1)} %copy-done.46), channel_id=1, replica_groups=mesh['dp'=8,'fsdp'=4] {'dp','fsdp'}, dimensions={0}, use_global_device_ids=true | all-gather | bytes 844800 | tf_op jit(solution)/shard_map/while/body/eval_jaxpr/all_gather | solution.py:121
  145.9 8.8 all_gather.73
  154.8 9.8 all_gather.70
  164.5 5.8 copy.61
  170.4 3.1 fusion.244
  177.7 3.9 exponential_reduce_fusion.2
  184.7 5.9 fusion.247
  190.5 3.4 multiply_reduce_fusion.5
  194.2 30.5 %all-gather.12.cloned.1.call-done = bf16[3584,1280]{1,0:T(8,128)(2,1)} async-done(((bf16[112,1280]{1,0:T(8,128)(2,1)}), bf16[3584,1280]{1,0:T(8,128)(2,1)}) %all-gather.12.cloned.1.call-update) | async-done | bytes 9175056 | tf_op jit(solution)/shard_map/while/body/eval_jaxpr/all_gather | solution.py:193
  224.7 8.0 fusion.249
  232.7 74.0 %all-gather.10.cloned.1.call-done = bf16[1280,3584]{1,0:T(8,128)(2,1)} async-done(((bf16[40,3584]{1,0:T(8,128)(2,1)}), bf16[1280,3584]{1,0:T(8,128)(2,1)}) %all-gather.10.cloned.1.call-update) | async-done | bytes 9175056 | tf_op jit(solution)/shard_map/while/body/eval_jaxpr/all_gather | solution.py:124
  306.7 8.0 fusion.248
  314.7 74.0 %all-gather.14.cloned.1.call-done = bf16[1280,3584]{1,0:T(8,128)(2,1)} async-done(((bf16[40,3584]{1,0:T(8,128)(2,1)}), bf16[1280,3584]{1,0:T(8,128)(2,1)}) %all-gather.14.cloned.1.call-update) | async-done | bytes 9175056 | tf_op jit(solution)/shard_map/while/body/eval_jaxpr/all_gather | solution.py:125
  388.7 10.0 multiply_convert_fusion.7
  398.8 3.7 fusion.250
  404.2 4.8 multiply_reduce_fusion.6
  414.3 16.4 fusion.251
  430.7 14.7 fusion.252
  445.4 4.1 fusion.254
  451.4 8.8 convolution_add_fusion.26
  460.2 8.9 convolution_add_fusion.25
  471.0 10.5 fusion.255
  481.6 10.8 convolution_add_fusion.27
  500.5 6.3 fusion.257
  507.9 3.7 convolution_add_fusion.24
  529.1 39.8 %all-reduce.17 = (bf16[1280]{0:T(1024)(128)(2,1)S(1)}, bf16[1280]{0:T(1024)(128)(2,1)S(1)}) all-reduce(bf16[1280]{0:T(1024)(128)(2,1)S(1)} %dynamic-update-slice.6, bf16[1280]{0:T(1024)(128)(2,1)S(1)} %dynamic-update-slice.7), channel_id=1, replica_groups=mesh['dp'=8,'fsdp'=4] {'dp','fsdp'}, use_global_device_ids=true, to_apply=%add | all-reduce | flops 2560 | bytes 10240 | tf_op jit(solution)/shard_map/while
  568.9 44.1 %all_gather.69 = bf16[1280,320]{1,0:T(8,128)(2,1)S(1)} all-gather(bf16[40,320]{1,0:T(8,128)(2,1)} %get-tuple-element.727), channel_id=1, replica_groups=mesh['dp'=8,'fsdp'=4] {'dp','fsdp'}, dimensions={0}, use_global_device_ids=true | all-gather | bytes 844800 | tf_op jit(solution)/shard_map/while/body/eval_jaxpr/all_gather | solution.py:120
  615.6 40.2 %all_gather.72 = bf16[1280,320]{1,0:T(8,128)(2,1)S(1)} all-gather(bf16[40,320]{1,0:T(8,128)(2,1)S(1)} %copy-done.46), channel_id=1, replica_groups=mesh['dp'=8,'fsdp'=4] {'dp','fsdp'}, dimensions={0}, use_global_device_ids=true | all-gather | bytes 844800 | tf_op jit(solution)/shard_map/while/body/eval_jaxpr/all_gather | solution.py:121
  657.4 11.5 all_gather.73
  668.9 8.7 all_gather.70
  677.5 6.1 copy.61
  683.7 3.1 fusion.244
  691.0 3.9 exponential_reduce_fusion.2
  698.0 5.8 fusion.247
  703.8 3.4 multiply_reduce_fusion.5
  707.5 26.4 %all-gather.12.cloned.1.call-done = bf16[3584,1280]{1,0:T(8,128)(2,1)} async-done(((bf16[112,1280]{1,0:T(8,128)(2,1)}), bf16[3584,1280]{1,0:T(8,128)(2,1)}) %all-gather.12.cloned.1.call-update) | async-done | bytes 9175056 | tf_op jit(solution)/shard_map/while/body/eval_jaxpr/all_gather | solution.py:193
  733.8 8.0 fusion.249
  741.9 74.1 %all-gather.10.cloned.1.call-done = bf16[1280,3584]{1,0:T(8,128)(2,1)} async-done(((bf16[40,3584]{1,0:T(8,128)(2,1)}), bf16[1280,3584]{1,0:T(8,128)(2,1)}) %all-gather.10.cloned.1.call-update) | async-done | bytes 9175056 | tf_op jit(solution)/shard_map/while/body/eval_jaxpr/all_gather | solution.py:124
  816.0 8.0 fusion.248
  824.0 74.1 %all-gather.14.cloned.1.call-done = bf16[1280,3584]{1,0:T(8,128)(2,1)} async-done(((bf16[40,3584]{1,0:T(8,128)(2,1)}), bf16[1280,3584]{1,0:T(8,128)(2,1)}) %all-gather.14.cloned.1.call-update) | async-done | bytes 9175056 | tf_op jit(solution)/shard_map/while/body/eval_jaxpr/all_gather | solution.py:125
  898.1 10.0 multiply_convert_fusion.7
  908.1 3.7 fusion.250
  913.4 4.8 multiply_reduce_fusion.6
  923.5 16.4 fusion.251
  939.9 14.5 fusion.252
  954.5 4.1 fusion.254
  960.5 15.1 convolution_add_fusion.26
  975.6 15.1 convolution_add_fusion.25
  992.7 10.7 fusion.255
  1003.5 16.2 convolution_add_fusion.27
  1027.8 6.3 fusion.257
  1035.2 6.7 convolution_add_fusion.24
  1060.5 3.3 reshape.351
  1065.5 3.2 reshape.353
  1068.7 7.4 reshape.349
  1076.1 7.4 reshape.355
  1083.5 18.3 reshape.357
  1101.8 18.3 reshape.359
  1120.1 19.5 reshape.361
  1140.3 41.5 %all-reduce.14 = (f32[1280]{0:T(1024)S(1)}, f32[1280]{0:T(1024)S(1)}) all-reduce(f32[1280]{0:T(1024)S(1)} %copy-done.52, f32[1280]{0:T(1024)S(1)} %copy-done.49), channel_id=4, replica_groups=mesh['dp'=8,'fsdp'=4] {'dp','fsdp'}, use_global_device_ids=true, to_apply=%region_13.14.clone | all-reduce | flops 2560 | bytes 20480
  1183.0 988.9 %all-reduce.20.cloned.1.call-done = (f32[1638400]{0:T(1024)}, f32[409600]{0:T(1024)}, f32[409600]{0:T(1024)}, f32[1638400]{0:T(1024)}, f32[4587520]{0:T(1024)}, /*index=5*/f32[4587520]{0:T(1024)}, f32[4587520]{0:T(1024)}) async-done(((f32[1638400]{0:T(1024)}, f32[409600]{0:T(1024)}, f32[409600]{0:T(1024)}, f32[1638400]{0:T(1024)}, f32[4587520]{0:T(1024)}, /*index=5*/f32[4587520]{0:T(1024)}, ...) | async-done | bytes 71434256
  (405 shorter events, 115.8 us)
Async XLA Ops:
  8.6 156.0 %all-gather.6.cloned.1.call-start = ((), (), s32[]{:S(2)}) async-start(), calls=%async_computation.3 | async-start | bytes 3379200 | tf_op jit(solution)/shard_map/while/body/eval_jaxpr/all_gather | solution.py:119
  9.3 181.2 %all-gather.8.cloned.1.call-start = ((), (), s32[]{:S(2)}) async-start(), calls=%async_computation.4 | async-start | bytes 3379200 | tf_op jit(solution)/shard_map/while/body/eval_jaxpr/all_gather | solution.py:122
  10.1 214.6 %all-gather.12.cloned.1.call-start = ((), (), s32[]{:S(2)}) async-start(), calls=%async_computation.6 | async-start | bytes 9461760 | tf_op jit(solution)/shard_map/while/body/eval_jaxpr/all_gather | solution.py:193
  10.1 91.3 %copy-start.3 = (bf16[2,1,256,1280]{3,2,1,0:T(8,128)(2,1)S(1)}, bf16[2,1,256,1280]{3,2,1,0:T(8,128)(2,1)}, u32[]{:S(2)}) copy-start(bf16[2,1,256,1280]{3,2,1,0:T(8,128)(2,1)} %get-tuple-element.725) | copy-start | bytes 3932164 | tf_op jit(solution)/shard_map/while
  10.8 295.9 %all-gather.10.cloned.1.call-start = ((), (), s32[]{:S(2)}) async-start(), calls=%async_computation.5 | async-start | bytes 9461760 | tf_op jit(solution)/shard_map/while/body/eval_jaxpr/all_gather | solution.py:124
  11.4 377.3 %all-gather.14.cloned.1.call-start = ((), (), s32[]{:S(2)}) async-start(), calls=%async_computation.7 | async-start | bytes 9461760 | tf_op jit(solution)/shard_map/while/body/eval_jaxpr/all_gather | solution.py:125
  12.0 499.6 %reduce-scatter.3.cloned.1.call-start = ((), (), s32[]{:S(2)}) async-start(), calls=%async_computation.8 | async-start | bytes 819200 | tf_op jit(solution)/shard_map/while/body/eval_jaxpr/reduce_scatter | solution.py:246
  56.5 113.8 %copy-start.39 = (f32[1280]{0:T(1024)}, f32[1280]{0:T(1024)S(1)}, u32[]{:S(2)}) copy-start(f32[1280]{0:T(1024)S(1)} %convert_element_type.399) | copy-start | bytes 15364 | tf_op jit(solution)/shard_map/while
  101.7 68.7 %copy-start.44 = (f32[256]{0:T(256)}, f32[256]{0:T(256)S(1)}, u32[]{:S(2)}) copy-start(f32[256]{0:T(256)S(1)} %add_rsqrt_fusion.4) | copy-start | bytes 3076 | tf_op jit(solution)/shard_map/while
  101.9 71.6 %copy-start.33 = (f32[256,32]{0,1:T(8,128)}, f32[256,32]{0,1:T(8,128)S(1)}, u32[]{:S(2)}) copy-start(f32[256,32]{0,1:T(8,128)S(1)} %get-tuple-element.626) | copy-start | bytes 98308 | tf_op jit(solution)/shard_map/while
  101.9 71.6 %copy-start.35 = (f32[256,32]{0,1:T(8,128)}, f32[256,32]{0,1:T(8,128)S(1)}, u32[]{:S(2)}) copy-start(f32[256,32]{0,1:T(8,128)S(1)} %get-tuple-element.625) | copy-start | bytes 98308 | tf_op jit(solution)/shard_map/while
  177.6 7.0 copy-start
  181.6 8.9 copy-start.41
  193.9 215.0 %copy-start.12 = (f32[256,1280]{1,0:T(8,128)}, f32[256,1280]{1,0:T(8,128)S(1)}, u32[]{:S(2)}) copy-start(f32[256,1280]{1,0:T(8,128)S(1)} %get-tuple-element.635) | copy-start | bytes 3932164 | tf_op jit(solution)/shard_map/while
  193.9 30.7 %copy-start.29 = (bf16[2,1,256,1280]{3,2,1,0:T(8,128)(2,1)S(1)}, bf16[2,1,256,1280]{3,2,1,0:T(8,128)(2,1)}, u32[]{:S(2)}) copy-start(bf16[2,1,256,1280]{3,2,1,0:T(8,128)(2,1)} %get-tuple-element.731) | copy-start | bytes 3932164 | tf_op jit(solution)/shard_map/while
  388.7 10.0 copy-start.54
  414.2 16.4 copy-start.16
  414.2 16.4 copy-start.42
  430.7 14.7 copy-start.9
  451.4 8.8 copy-start.26
  469.1 46.8 %reduce-scatter.5.cloned.1.call-start = ((), (), s32[]{:S(2)}) async-start(), calls=%async_computation.9 | async-start | bytes 819200 | tf_op jit(solution)/shard_map/while/body/eval_jaxpr/reduce_scatter | solution.py:252
  481.6 10.9 slice-start
  481.6 10.8 copy-start.31
  481.6 10.8 copy-start.32
  481.6 10.9 copy-start.4
  481.6 10.9 slice-start.1
  481.6 10.9 copy-start.40
  481.6 10.9 copy-start.45
  495.4 11.4 copy-start.5
  500.5 7.3 copy-start.37
  523.3 154.3 %all-gather.6.cloned.1.call-start = ((), (), s32[]{:S(2)}) async-start(), calls=%async_computation.3 | async-start | bytes 3379200 | tf_op jit(solution)/shard_map/while/body/eval_jaxpr/all_gather | solution.py:119
  524.0 179.8 %all-gather.8.cloned.1.call-start = ((), (), s32[]{:S(2)}) async-start(), calls=%async_computation.4 | async-start | bytes 3379200 | tf_op jit(solution)/shard_map/while/body/eval_jaxpr/all_gather | solution.py:122
  524.8 209.1 %all-gather.12.cloned.1.call-start = ((), (), s32[]{:S(2)}) async-start(), calls=%async_computation.6 | async-start | bytes 9461760 | tf_op jit(solution)/shard_map/while/body/eval_jaxpr/all_gather | solution.py:193
  524.8 88.8 %copy-start.3 = (bf16[2,1,256,1280]{3,2,1,0:T(8,128)(2,1)S(1)}, bf16[2,1,256,1280]{3,2,1,0:T(8,128)(2,1)}, u32[]{:S(2)}) copy-start(bf16[2,1,256,1280]{3,2,1,0:T(8,128)(2,1)} %get-tuple-element.725) | copy-start | bytes 3932164 | tf_op jit(solution)/shard_map/while
  525.4 290.7 %all-gather.10.cloned.1.call-start = ((), (), s32[]{:S(2)}) async-start(), calls=%async_computation.5 | async-start | bytes 9461760 | tf_op jit(solution)/shard_map/while/body/eval_jaxpr/all_gather | solution.py:124
  526.1 372.0 %all-gather.14.cloned.1.call-start = ((), (), s32[]{:S(2)}) async-start(), calls=%async_computation.7 | async-start | bytes 9461760 | tf_op jit(solution)/shard_map/while/body/eval_jaxpr/all_gather | solution.py:125
  526.7 515.2 %reduce-scatter.3.cloned.1.call-start = ((), (), s32[]{:S(2)}) async-start(), calls=%async_computation.8 | async-start | bytes 819200 | tf_op jit(solution)/shard_map/while/body/eval_jaxpr/reduce_scatter | solution.py:246
  568.9 114.8 %copy-start.39 = (f32[1280]{0:T(1024)}, f32[1280]{0:T(1024)S(1)}, u32[]{:S(2)}) copy-start(f32[1280]{0:T(1024)S(1)} %convert_element_type.399) | copy-start | bytes 15364 | tf_op jit(solution)/shard_map/while
  613.8 69.9 %copy-start.44 = (f32[256]{0:T(256)}, f32[256]{0:T(256)S(1)}, u32[]{:S(2)}) copy-start(f32[256]{0:T(256)S(1)} %add_rsqrt_fusion.4) | copy-start | bytes 3076 | tf_op jit(solution)/shard_map/while
  614.0 72.8 %copy-start.33 = (f32[256,32]{0,1:T(8,128)}, f32[256,32]{0,1:T(8,128)S(1)}, u32[]{:S(2)}) copy-start(f32[256,32]{0,1:T(8,128)S(1)} %get-tuple-element.626) | copy-start | bytes 98308 | tf_op jit(solution)/shard_map/while
  614.0 72.8 %copy-start.35 = (f32[256,32]{0,1:T(8,128)}, f32[256,32]{0,1:T(8,128)S(1)}, u32[]{:S(2)}) copy-start(f32[256,32]{0,1:T(8,128)S(1)} %get-tuple-element.625) | copy-start | bytes 98308 | tf_op jit(solution)/shard_map/while
  691.0 7.0 copy-start
  694.9 8.9 copy-start.41
  707.2 211.0 %copy-start.12 = (f32[256,1280]{1,0:T(8,128)}, f32[256,1280]{1,0:T(8,128)S(1)}, u32[]{:S(2)}) copy-start(f32[256,1280]{1,0:T(8,128)S(1)} %get-tuple-element.635) | copy-start | bytes 3932164 | tf_op jit(solution)/shard_map/while
  707.2 26.6 %copy-start.29 = (bf16[2,1,256,1280]{3,2,1,0:T(8,128)(2,1)S(1)}, bf16[2,1,256,1280]{3,2,1,0:T(8,128)(2,1)}, u32[]{:S(2)}) copy-start(bf16[2,1,256,1280]{3,2,1,0:T(8,128)(2,1)} %get-tuple-element.731) | copy-start | bytes 3932164 | tf_op jit(solution)/shard_map/while
  898.1 10.0 copy-start.54
  923.5 16.4 copy-start.16
  923.5 16.4 copy-start.42
  939.9 14.5 copy-start.9
  960.5 15.1 copy-start.26
  990.8 55.4 %reduce-scatter.5.cloned.1.call-start = ((), (), s32[]{:S(2)}) async-start(), calls=%async_computation.9 | async-start | bytes 819200 | tf_op jit(solution)/shard_map/while/body/eval_jaxpr/reduce_scatter | solution.py:252
  1003.4 16.4 slice-start
  1003.5 16.3 copy-start.31
  1003.5 16.3 copy-start.32
  1003.5 16.3 copy-start.4
  1003.5 16.3 slice-start.1
  1003.5 16.3 copy-start.40
  1003.5 16.3 copy-start.45
  1022.7 11.4 copy-start.5
  1027.8 7.4 copy-start.37
  1035.2 6.7 copy-start.48
  1035.2 7.7 copy-start.34
  1035.2 7.7 copy-start.36
  1057.6 1114.3 %all-reduce.20.cloned.1.call-start = ((), (), s32[]{:S(2)}) async-start(), calls=%async_computation.2 | async-start | bytes 142868480
  (74 other events, 190.3 us)
Sparse Core Ops, SparseCore 0:
  12.3 64.0 all-gather.5
  79.2 62.3 all-gather.7
  144.5 80.0 all-gather.11
  227.4 79.3 all-gather.9
  309.4 79.2 all-gather.13
  469.2 21.0 reduce-scatter.2
  492.8 22.4 reduce-scatter.4
  527.0 60.9 all-gather.5
  590.8 60.7 all-gather.7
  654.4 79.3 all-gather.11
  736.7 79.2 all-gather.9
  818.7 79.3 all-gather.13
  990.9 21.0 reduce-scatter.2
  1014.4 22.4 reduce-scatter.4
Sparse Core Ops, SparseCore 1:
  1139.7 1032.1 all-reduce.19
where the time goes:
time: 2200 us; the launch traced here: 2190 us
  waiting for transfers between devices  1350 us (61%)
  blocking collectives  332 us (15%)
  matrix products  293 us (13%)
  local copies, waits for them, and re-layouts  147 us (7%)
  other arithmetic  48.8 us (2%)
    unnamed x2, waiting for transfers between devices  989 us
    all_gather x2, waiting for transfers between devices, micro_step(): lax.all_gather(w_gate, ('dp', 'fsdp'), axis=0, tiled=True)  148 us
    all_gather x2, waiting for transfers between devices, micro_step(): lax.all_gather(w_up, ('dp', 'fsdp'), axis=0, tiled=True)  148 us
    dot_general x14, matrix products, left_dot(): lax.dot_general(left, right, (((0,), (0,)), ((), ())), preferred_element_...  93.6 us
    all_gather x2, blocking collectives, micro_step(): lax.all_gather(key_matrix, ('dp', 'fsdp'), axis=0, tiled=True)  88.4 us
    while x2, blocking collectives  81.9 us
    all_gather x2, blocking collectives, micro_step(): lax.all_gather(value_matrix, ('dp', 'fsdp'), axis=0, tiled=True)  81.1 us
    reshape x7, local copies, waits for them, and re-layouts, flatten_all(): return tuple((g.reshape(-1) for g in grads))  77.4 us
  transfers between devices with their start and end apart: 15, of which 7 were waited for; matrix products, arithmetic and copies ran while one was open for 9% of the time, Pallas kernels for 0%

commit v1 on v0

v1 whole, which is shorter than its diff:
```python
import jax
import jax.numpy as jnp
from jax import lax
from jax.sharding import PartitionSpec as P

HD = 64
EPSILON = 1e-05
NEGATIVE = -1e30
ROPE_BASE = 10000.0
BOTH = ("dp", "fsdp")


def rope_tables(places):
    half = HD // 2
    freqs = ROPE_BASE ** (-jnp.arange(half).astype(jnp.float32) / half)
    angles = places.astype(jnp.float32)[:, None] * freqs[None, :]
    return (jnp.cos(angles), jnp.sin(angles))


def rotate(field, cos_table, sin_table, sign):
    shaped = field.reshape(field.shape[0], -1, HD)
    first_half = shaped[..., : HD // 2]
    second_half = shaped[..., HD // 2 :]
    cos_heads = cos_table[:, None, :]
    sin_heads = sin_table[:, None, :] * sign
    turned = jnp.concatenate(
        [
            first_half * cos_heads - second_half * sin_heads,
            second_half * cos_heads + first_half * sin_heads,
        ],
        -1,
    )
    return turned.reshape(field.shape)


def plain_dot(left, right):
    return jnp.dot(left, right, preferred_element_type=jnp.float32)


def left_dot(left, right):
    return lax.dot_general(
        left, right, (((0,), (0,)), ((), ())), preferred_element_type=jnp.float32
    )


def right_dot(left, right):
    return lax.dot_general(
        left, right, (((1,), (1,)), ((), ())), preferred_element_type=jnp.float32
    )


def norm_back(grad_normed, inputs_float, inverse):
    return inverse * (
        grad_normed
        - inputs_float * inverse * inverse * jnp.mean(grad_normed * inputs_float, -1, keepdims=True)
    )


def einsum32(spec, a, b):
    return jnp.einsum(spec, a, b, preferred_element_type=jnp.float32)


def gather_rows(shard):
    return lax.all_gather(shard, BOTH, axis=0, tiled=True)


def scatter_rows(full):
    return lax.psum_scatter(
        full.astype(jnp.bfloat16), BOTH, scatter_dimension=0, tiled=True
    ).astype(jnp.float32)


def on_device(
    inputs,
    positions,
    cotangent,
    attn_gain,
    w_query,
    key_matrix,
    value_matrix,
    w_out,
    mlp_gain,
    w_gate,
    w_up,
    w_down,
):
    batches, _, rows, width = inputs.shape
    shard = w_query.shape[0]
    query_features = w_query.shape[1]
    key_features = key_matrix.shape[1]
    kv_heads = key_features // HD
    group = query_features // key_features
    tokens = batches * rows
    length = rows * lax.axis_size("fsdp")
    first_row = lax.axis_index("fsdp") * rows
    query_index = first_row + jnp.arange(rows, dtype=jnp.int32)
    key_index = jnp.arange(length, dtype=jnp.int32)
    score_scale = HD ** (-0.5)

    extras = jnp.zeros((shard, 128), jnp.bfloat16)
    extras = extras.at[:, 0].set(attn_gain).at[:, 1].set(mlp_gain)
    first_pack = gather_rows(
        jnp.concatenate([w_query, key_matrix, value_matrix, extras], axis=1)
    )
    projection = first_pack[:, : query_features + 2 * key_features]
    gains = first_pack[:, query_features + 2 * key_features :][:, :2].astype(jnp.float32).T
    out_full = gather_rows(w_out)
    gate_full = gather_rows(w_gate)
    up_full = gather_rows(w_up)
    down_full = gather_rows(w_down)

    x_float = inputs.reshape(tokens, width).astype(jnp.float32)
    places = positions.reshape(batches, rows)
    cos_table, sin_table = rope_tables(places.reshape(tokens))
    doc_start = query_index[None, :] - places
    allowed = (key_index[None, None, :] <= query_index[None, :, None]) & (
        key_index[None, None, :] >= doc_start[:, :, None]
    )
    attn_inverse = lax.rsqrt(jnp.mean(x_float * x_float, -1, keepdims=True) + EPSILON)
    attn_gain_f = gains[0]
    mlp_gain_f = gains[1]
    normed = (x_float * attn_inverse * attn_gain_f).astype(jnp.bfloat16)
    projected = plain_dot(normed, projection)
    queries = (
        rotate(projected[:, :query_features], cos_table, sin_table, 1.0) * score_scale
    ).astype(jnp.bfloat16)
    key_rows = rotate(
        projected[:, query_features : query_features + key_features], cos_table, sin_table, 1.0
    ).astype(jnp.bfloat16)
    value_rows = projected[:, query_features + key_features :].astype(jnp.bfloat16)
    both_rows = jnp.concatenate([key_rows, value_rows], -1).reshape(batches, rows, -1)
    both_all = lax.all_gather(both_rows, "fsdp", axis=1, tiled=True)
    key_heads = both_all[..., :key_features].reshape(batches, length, kv_heads, HD)
    value_heads = both_all[..., key_features:].reshape(batches, length, kv_heads, HD)
    grouped = queries.reshape(batches, rows, kv_heads, group, HD)
    mask = allowed[:, None, None]
    scores = einsum32("bqkgd,bskd->bkgqs", grouped, key_heads)
    scores = jnp.where(mask, scores, NEGATIVE)
    row_max = jnp.max(scores, -1, keepdims=True)
    row_total = jnp.sum(jnp.exp(scores - row_max), -1, keepdims=True)
    log_total = row_max + jnp.log(row_total)
    probs_low = jnp.exp(scores - log_total).astype(jnp.bfloat16)
    attended = einsum32("bkgqs,bskd->bqkgd", probs_low, value_heads)
    attended = attended.reshape(tokens, query_features).astype(jnp.bfloat16)

    mixed = x_float + plain_dot(attended, out_full)
    mlp_inverse = lax.rsqrt(jnp.mean(mixed * mixed, -1, keepdims=True) + EPSILON)
    normed_mlp = (mixed * mlp_inverse * mlp_gain_f).astype(jnp.bfloat16)
    gate_pre = plain_dot(normed_mlp, gate_full)
    up_proj = plain_dot(normed_mlp, up_full)
    gate_sig = jax.nn.sigmoid(gate_pre)
    hidden = (gate_pre * gate_sig * up_proj).astype(jnp.bfloat16)
    output = (mixed + plain_dot(hidden, down_full)).astype(jnp.bfloat16)

    cot_low = cotangent.reshape(tokens, width)
    cot_float = cot_low.astype(jnp.float32)
    grad_down = scatter_rows(left_dot(hidden, cot_low))
    grad_hidden = right_dot(cot_low, down_full)
    sig_slope = gate_sig * (1.0 + gate_pre * (1.0 - gate_sig))
    grad_gate_pre = (grad_hidden * up_proj * sig_slope).astype(jnp.bfloat16)
    grad_up_pre = (grad_hidden * gate_pre * gate_sig).astype(jnp.bfloat16)
    grad_gate = scatter_rows(left_dot(normed_mlp, grad_gate_pre))
    grad_up = scatter_rows(left_dot(normed_mlp, grad_up_pre))
    grad_normed_mlp = right_dot(grad_gate_pre, gate_full) + right_dot(grad_up_pre, up_full)
    grad_mlp_gain = jnp.sum(grad_normed_mlp * mixed * mlp_inverse, 0)
    grad_mixed = cot_float + norm_back(grad_normed_mlp * mlp_gain_f, mixed, mlp_inverse)
    grad_mixed_low = grad_mixed.astype(jnp.bfloat16)
    grad_out = scatter_rows(left_dot(attended, grad_mixed_low))
    grad_attended = right_dot(grad_mixed_low, out_full).astype(jnp.bfloat16)
    grad_attended = grad_attended.reshape(batches, rows, kv_heads, group, HD)

    scores_again = einsum32("bqkgd,bskd->bkgqs", grouped, key_heads)
    scores_again = jnp.where(mask, scores_again, NEGATIVE)
    probabilities = jnp.exp(scores_again - log_total)
    grad_probs = einsum32("bqkgd,bskd->bkgqs", grad_attended, value_heads)
    row_dot = jnp.sum(probabilities * grad_probs, -1, keepdims=True)
    grad_scores = (probabilities * (grad_probs - row_dot)).astype(jnp.bfloat16)
    grad_query_rot = einsum32("bkgqs,bskd->bqkgd", grad_scores, key_heads)
    key_portion = einsum32("bkgqs,bqkgd->bskd", grad_scores, grouped)
    value_portion = einsum32(
        "bkgqs,bqkgd->bskd", probabilities.astype(jnp.bfloat16), grad_attended
    )
    portions = jnp.concatenate(
        [
            key_portion.reshape(batches, length, key_features),
            value_portion.reshape(batches, length, key_features),
        ],
        -1,
    ).astype(jnp.bfloat16)
    sums = lax.psum_scatter(portions, "fsdp", scatter_dimension=1, tiled=True)
    sums = sums.astype(jnp.float32).reshape(tokens, 2 * key_features)
    grad_query_pre = rotate(
        grad_query_rot.reshape(tokens, query_features) * score_scale, cos_table, sin_table, -1.0
    ).astype(jnp.bfloat16)
    grad_key_pre = rotate(sums[:, :key_features], cos_table, sin_table, -1.0).astype(jnp.bfloat16)
    grad_value_pre = sums[:, key_features:].astype(jnp.bfloat16)
    grad_pre = jnp.concatenate([grad_query_pre, grad_key_pre, grad_value_pre], -1)
    grad_projection = left_dot(normed, grad_pre)
    grad_normed = right_dot(grad_pre, projection)
    grad_attn_gain = jnp.sum(grad_normed * x_float * attn_inverse, 0)
    grad_input = grad_mixed + norm_back(grad_normed * attn_gain_f, x_float, attn_inverse)
    gain_columns = jnp.stack([grad_attn_gain, grad_mlp_gain], -1)
    gain_columns = jnp.pad(gain_columns, ((0, 0), (0, 126)))
    last = scatter_rows(jnp.concatenate([grad_projection, gain_columns], 1))
    split = query_features + key_features
    return (
        output.reshape(inputs.shape),
        grad_input.astype(jnp.bfloat16).reshape(inputs.shape),
        last[:, split + key_features],
        last[:, :query_features],
        last[:, query_features:split],
        last[:, split : split + key_features],
        grad_out,
        last[:, split + key_features + 1],
        grad_gate,
        grad_up,
        grad_down,
    )


def solution(mesh):
    tokens = P(None, "dp", "fsdp", None)
    vector = P(BOTH)
    matrix = P(BOTH, None)
    weights = (vector, matrix, matrix, matrix, matrix, vector, matrix, matrix, matrix)
    return jax.shard_map(
        on_device,
        mesh=mesh,
        in_specs=(tokens, P(None, "dp", "fsdp"), tokens) + weights,
        out_specs=(tokens, tokens) + weights,
        check_vma=False,
    )
```

time: 2200 us -> 1350 us (0.61)
  waiting for transfers between devices: 1350 us -> 958 us
  blocking collectives: 332 us -> 0 us
  local copies, waits for them, and re-layouts: 147 us -> 55.8 us
  matrix products: 293 us -> 227 us
  other arithmetic: 48.8 us -> 83.5 us
    unnamed x2 -> x12, waiting for transfers between devices: 989 us -> 2.39 us
    reduce_scatter x4 -> x6, waiting for transfers between devices: 0.01 us -> 661 us  [the longest x5 654 us: scatter_rows(): lax.psum_scatter(full.astype(jnp.bfloat16), BOTH, scatter_dimension=0, ti...]
    all_gather x8 -> x0, blocking collectives: 208 us -> none  [the longest x2 88.4 us: micro_step(): lax.all_gather(key_matrix, ('dp', 'fsdp'), axis=0, tiled=True)]
    while x2 -> x0, blocking collectives: 81.9 us -> none
    reshape x14 -> x4, local copies, waits for them, and re-layouts: 82.9 us -> 10.3 us  [the longest x2 7.14 us: on_device(): grad_attended = grad_attended.reshape(batches, rows, kv_heads, group, HD)]
    all_gather x10 -> x6, waiting for transfers between devices: 353 us -> 294 us  [the longest x5 280 us: gather_rows(): return lax.all_gather(shard, BOTH, axis=0, tiled=True)]
    dot_general x14 -> x5, matrix products: 93.6 us -> 38.4 us  [left_dot(): lax.dot_general(left, right, (((0,), (0,)), ((), ())), preferred_element_...]
    unnamed x1 -> x0, blocking collectives: 41.5 us -> none
  transfers between devices with their start and end apart: 15 -> 12, of which waited for: 7 -> 11; matrix products, arithmetic and copies ran while one was open for 9% -> 15% of each run, Pallas kernels for 0% -> 0%
where the time goes in v1:
time: 1350 us; the launch traced here: 1340 us
  waiting for transfers between devices  958 us (71%)
  matrix products  227 us (17%)
  other arithmetic  83.5 us (6%)
  local copies, waits for them, and re-layouts  55.8 us (4%)
  between operations  15 us (1%)
    reduce_scatter x5, waiting for transfers between devices, scatter_rows(): lax.psum_scatter(full.astype(jnp.bfloat16), BOTH, scatter_dimension=0, ti...  654 us
    all_gather x5, waiting for transfers between devices, gather_rows(): return lax.all_gather(shard, BOTH, axis=0, tiled=True)  280 us
    dot_general x6, matrix products, einsum32(): return jnp.einsum(spec, a, b, preferred_element_type=jnp.float32)  98.5 us
    dot_general x5, matrix products, right_dot(): lax.dot_general(left, right, (((1,), (1,)), ((), ())), preferred_element_...  45.2 us
    dot_general x5, matrix products, plain_dot(): return jnp.dot(left, right, preferred_element_type=jnp.float32)  44.6 us
    dot_general x5, matrix products, left_dot(): lax.dot_general(left, right, (((0,), (0,)), ((), ())), preferred_element_...  38.4 us
    convert_element_type x1, other arithmetic, on_device(): grad_scores = (probabilities * (grad_probs - row_dot)).astype(jnp.bfloat16)  34.2 us
  transfers between devices with their start and end apart: 12, of which 11 were waited for; matrix products, arithmetic and copies ran while one was open for 15% of the time, Pallas kernels for 0%

profile of v1, /device:TPU:0, one launch (start us, length us, event | category | flops | bytes accessed | tf_op | source)
XLA Modules:
  0.0 1339.4 jit_solution(2188818021657015678)
XLA Ops:
  11.2 1.7 concatenate.36
  13.7 1.6 fusion.28
  16.4 64.7 %all-gather.7.cloned.1.call-done = bf16[1280,2048]{1,0:T(8,128)(2,1)} async-done(((bf16[40,2048]{1,0:T(8,128)(2,1)}), bf16[1280,2048]{1,0:T(8,128)(2,1)}) %all-gather.7.cloned.1.call-update) | async-done | bytes 5242896 | tf_op jit(solution)/shard_map/all_gather | solution.py:64
  83.7 5.3 fusion.9
  89.3 1.7 copy-done.17
  96.1 3.5 slice.139
  99.6 2.3 copy.88
  103.0 14.3 %all-gather.9.cloned.1.call-done = bf16[2,1024,640]{2,1,0:T(8,128)(2,1)} async-done(((bf16[2,256,640]{2,1,0:T(8,128)(2,1)}), bf16[2,1024,640]{2,1,0:T(8,128)(2,1)}) %all-gather.9.cloned.1.call-update) | async-done | bytes 2621456 | tf_op jit(solution)/shard_map/all_gather | solution.py:132
  117.3 4.4 fusion.49
  121.7 1.7 copy.87
  123.3 3.0 copy.86
  126.3 16.2 %fusion.3 = (f32[2,5,4,256]{3,2,1,0:T(4,128)S(1)}, f32[2,5,1024,256,4]{3,2,4,1,0:T(8,128)}) fusion(pred[2,256,1024]{1,2,0:T(8,128)(4,1)S(1)} %fusion.29, bf16[2,1024,5,64,1]{1,3,4,2,0:T(8,128)(2,1)S(1)} %bitcast.155, bf16[2,256,5,4,64]{1,0,4,3,2:T(2,128)(2,1)S(1)} %convert_element_type.135), kind=kOutput, calls=%fused_computation.8 | convolution fusion | flops 1363138560 | bytes 45129728 | tf_op jit(solution)/shard_map/bqkgd,bskd->bkgqs/dot_general | solution.py:60
  142.6 17.2 %exponential_reduce_fusion = f32[2,5,4,256]{3,2,1,0:T(4,128)S(1)} fusion(f32[2,5,1024,256,4]{3,2,4,1,0:T(8,128)} %get-tuple-element.108, f32[2,5,4,256]{3,2,1,0:T(4,128)S(1)} %get-tuple-element.107, pred[2,256,1024]{1,2,0:T(8,128)(4,1)S(1)} %fusion.29), kind=kLoop, calls=%fused_computation.7 | loop fusion | flops 31447040 | bytes 42549248 | tf_op jit(solution)/shard_map/reduce_sum | solution.py:140
  159.8 18.1 %fusion.35 = bf16[2,256,5,4,64]{1,4,3,2,0:T(8,128)(2,1)S(1)} fusion(bf16[2,1024,5,64,1]{1,3,4,2,0:T(8,128)(2,1)S(1)} %bitcast.161, f32[2,5,1024,256,4]{3,2,4,1,0:T(8,128)} %get-tuple-element.108, f32[2,5,4,256]{3,2,1,0:T(4,128)S(1)} %log_add_fusion, pred[2,256,1024]{1,2,0:T(8,128)(4,1)S(1)} %fusion.29), kind=kOutput, calls=%fused_computation.64 | convolution fusion | flops 1374289920 | bytes 45129728 | tf_op jit(solution)/shard_map/bkgqs,bskd->bqkgd/dot_general | solution.py:60
  179.3 1.4 copy.121
  180.7 4.8 multiply_reduce_fusion.2
  185.4 1.6 multiply_convert_fusion.3
  187.0 74.7 %all-gather.15.cloned.1.call-done = bf16[1280,3584]{1,0:T(8,128)(2,1)} async-done(((bf16[40,3584]{1,0:T(8,128)(2,1)}), bf16[1280,3584]{1,0:T(8,128)(2,1)}) %all-gather.15.cloned.1.call-update) | async-done | bytes 9175056 | tf_op jit(solution)/shard_map/all_gather | solution.py:64
  261.7 11.8 fusion.53
  273.5 70.2 %all-gather.13.cloned.1.call-done = bf16[1280,3584]{1,0:T(8,128)(2,1)} async-done(((bf16[40,3584]{1,0:T(8,128)(2,1)}), bf16[1280,3584]{1,0:T(8,128)(2,1)}) %all-gather.13.cloned.1.call-update) | async-done | bytes 9175056 | tf_op jit(solution)/shard_map/all_gather | solution.py:64
  343.8 11.8 fusion.52
  355.6 70.2 %all-gather.17.cloned.1.call-done = bf16[3584,1280]{1,0:T(8,128)(2,1)} async-done(((bf16[112,1280]{1,0:T(8,128)(2,1)}), bf16[3584,1280]{1,0:T(8,128)(2,1)}) %all-gather.17.cloned.1.call-update) | async-done | bytes 9175056 | tf_op jit(solution)/shard_map/all_gather | solution.py:64
  425.8 15.8 %multiply_convert_fusion = (bf16[512,3584]{1,0:T(8,128)(2,1)}, bf16[512,3584]{1,0:T(8,128)(2,1)}, bf16[512,3584]{1,0:T(8,128)(2,1)}) fusion(f32[512,3584]{1,0:T(8,128)} %fusion.52, f32[512,3584]{1,0:T(8,128)} %fusion.53, bf16[512,1280]{1,0:T(8,128)(2,1)} %bitcast.166, bf16[3584,1280]{1,0:T(8,128)(2,1)} %all-gather.17.cloned.1.call-done), kind=kOutput, calls=%fused_computation.17 | convolution fusion | flops 4726980608 | bytes 36175872 | tf_op jit(solution)/shard_map/dot_general | solution.py:47
  441.6 9.8 fusion.54
  451.4 9.0 multiply_reduce_fusion
  461.3 1.5 copy-done.10
  462.8 3.0 convolution_convert_fusion.5
  465.8 3.8 reshape.351
  469.6 3.3 copy.93
  472.9 16.5 %bitcast_convert_fusion = bf16[2,5,64,1024]{3,2,1,0:T(8,128)(2,1)S(1)} fusion(bf16[2,256,5,4,64]{1,4,3,2,0:T(8,128)(2,1)} %copy.93, f32[2,5,1024,256,4]{3,2,4,1,0:T(8,128)} %get-tuple-element.108, f32[2,5,4,256]{3,2,1,0:T(4,128)S(1)} %log_add_fusion, pred[2,256,1024]{1,2,0:T(8,128)(4,1)S(1)} %fusion.29), kind=kOutput, calls=%fused_computation.36 | convolution fusion | flops 1374289920 | bytes 45129728 | tf_op jit(solution)/shard_map/bkgqs,bqkgd->bskd/dot_general | solution.py:60
  489.4 28.0 %fusion = (f32[2,5,4,256]{3,2,1,0:T(4,128)S(1)}, f32[2,5,1024,256,4]{3,2,4,1,0:T(8,128)}) fusion(f32[2,5,1024,256,4]{3,2,4,1,0:T(8,128)} %get-tuple-element.108, f32[2,5,4,256]{3,2,1,0:T(4,128)S(1)} %log_add_fusion, pred[2,256,1024]{1,2,0:T(8,128)(4,1)S(1)} %fusion.29, bf16[2,1024,5,64,1]{1,3,4,2,0:T(8,128)(2,1)S(1)} %bitcast.162, ...), kind=kOutput, calls=%fused_computation.2 | convolution fusion | flops 1384110080 | bytes 87113728 | tf_op jit(solution)/shard_map/bqkgd,bskd->bkgqs/dot_general | solution.py:60
  517.5 1.6 copy.101
  519.0 34.2 %fusion.2 = bf16[2,5,4,256,1024]{3,4,2,1,0:T(8,128)(2,1)} fusion(f32[2,5,1024,256,4]{3,2,4,1,0:T(8,128)} %get-tuple-element.113, f32[2,5,1024,256,4]{3,2,4,1,0:T(8,128)} %get-tuple-element.108, f32[2,5,4,256]{3,2,1,0:T(4,128)S(1)} %get-tuple-element.112, f32[2,5,4,256]{3,2,1,0:T(4,128)S(1)} %log_add_fusion, pred[2,256,1024]{1,2,0:T(8,128)(4,1)S(1)} %fusion.29), kind=kLoop, calls=%fused_computation.4 | loop fusion | flops 52428800 | bytes 105463808 | tf_op jit(solution)/shard_map/convert_element_type | solution.py:177
  553.3 10.6 bitcast_convert_fusion.1
  563.9 1.6 copy.100
  565.5 3.8 pad_maximum_fusion
  569.4 1.7 copy-done.11
  571.1 4.9 convolution_convert_fusion.3
  576.0 1.4 copy-done.6
  577.4 9.0 multiply_bitcast_fusion
  586.4 3.6 copy.95
  590.0 4.0 mul.362
  595.6 7.2 reduce-scatter.7.cloned.1.call-done
  602.8 1.4 fusion.50
  604.9 7.7 fusion.19
  612.8 4.2 convolution_convert_fusion.4
  617.1 3.1 fusion.6
  621.5 9.4 convolution_convert_fusion
  630.9 9.5 convolution_convert_fusion.1
  641.7 10.5 convolution_convert_fusion.2
  652.2 1.7 copy-done.1
  653.9 10.8 fusion.11
  664.8 1.9 fusion.27
  666.6 77.7 %reduce-scatter.11.cloned.1.call-done = bf16[40,1280]{1,0:T(8,128)(2,1)} async-done(((bf16[1280,1280]{1,0:T(8,128)(2,1)}), bf16[40,1280]{1,0:T(8,128)(2,1)}) %reduce-scatter.11.cloned.1.call-update) | async-done | bytes 102416 | tf_op jit(solution)/shard_map/reduce_scatter | solution.py:68
  744.3 1.6 convert_element_type.154
  745.9 139.2 %reduce-scatter.9.cloned.1.call-done = bf16[40,2048]{1,0:T(8,128)(2,1)} async-done(((bf16[1280,2048]{1,0:T(8,128)(2,1)}), bf16[40,2048]{1,0:T(8,128)(2,1)}) %reduce-scatter.9.cloned.1.call-update) | async-done | bytes 163856 | tf_op jit(solution)/shard_map/reduce_scatter | solution.py:68
  885.1 1.6 slice.150
  888.3 1.5 fusion.51
  889.9 143.7 %reduce-scatter.15.cloned.1.call-done = bf16[40,3584]{1,0:T(8,128)(2,1)} async-done(((bf16[1280,3584]{1,0:T(8,128)(2,1)}), bf16[40,3584]{1,0:T(8,128)(2,1)}) %reduce-scatter.15.cloned.1.call-update) | async-done | bytes 286736 | tf_op jit(solution)/shard_map/reduce_scatter | solution.py:68
  1033.5 1.8 convert_element_type.158
  1035.3 146.8 %reduce-scatter.13.cloned.1.call-done = bf16[40,3584]{1,0:T(8,128)(2,1)} async-done(((bf16[1280,3584]{1,0:T(8,128)(2,1)}), bf16[40,3584]{1,0:T(8,128)(2,1)}) %reduce-scatter.13.cloned.1.call-update) | async-done | bytes 286736 | tf_op jit(solution)/shard_map/reduce_scatter | solution.py:68
  1182.1 1.8 convert_element_type.156
  1183.9 146.7 %reduce-scatter.17.cloned.1.call-done = bf16[112,1280]{1,0:T(8,128)(2,1)} async-done(((bf16[3584,1280]{1,0:T(8,128)(2,1)}), bf16[112,1280]{1,0:T(8,128)(2,1)}) %reduce-scatter.17.cloned.1.call-update) | async-done | bytes 286736 | tf_op jit(solution)/shard_map/reduce_scatter | solution.py:68
  1330.6 1.8 convert_element_type.160
  (134 shorter events, 23.8 us)
Async XLA Ops:
  7.2 76.1 %copy-start.2 = (bf16[2,1,256,1280]{3,2,1,0:T(8,128)(2,1)S(1)}, bf16[2,1,256,1280]{3,2,1,0:T(8,128)(2,1)}, u32[]{:S(2)}) copy-start(bf16[2,1,256,1280]{3,2,1,0:T(8,128)(2,1)} %param.16) | copy-start | bytes 3932164
  7.2 73.9 %all-gather.7.cloned.1.call-start = ((), (), s32[]{:S(2)}) async-start(), calls=%async_computation.6 | async-start | bytes 5406720 | tf_op jit(solution)/shard_map/all_gather | solution.py:64
  13.0 104.3 %all-gather.9.cloned.1.call-start = ((), (), s32[]{:S(2)}) async-start(), calls=%async_computation.7 | async-start | bytes 3276800 | tf_op jit(solution)/shard_map/all_gather | solution.py:132
  15.4 73.7 %copy-start.29 = (f32[1,2,2,128]{3,1,2,0:T(2,128)}, f32[1,2,2,128]{3,1,2,0:T(2,128)S(1)}, u32[]{:S(2)}) copy-start(f32[1,2,2,128]{3,1,2,0:T(2,128)S(1)} %copy.120) | copy-start | bytes 6148
  16.4 85.5 %copy-start.19 = (f32[512,32]{0,1:T(8,128)}, f32[512,32]{0,1:T(8,128)S(1)}, u32[]{:S(2)}) copy-start(f32[512,32]{0,1:T(8,128)S(1)} %get-tuple-element.106) | copy-start | bytes 196612
  82.7 0.6 copy-start.27
  83.7 5.4 copy-start.25
  89.1 1.9 copy-start.17
  91.2 4.2 copy-start.31
  92.7 88.0 %all-gather.11.cloned.1.call-start = ((), (), s32[]{:S(2)}) async-start(), calls=%async_computation.8 | async-start | bytes 3379200 | tf_op jit(solution)/shard_map/all_gather | solution.py:64
  93.4 168.3 %all-gather.15.cloned.1.call-start = ((), (), s32[]{:S(2)}) async-start(), calls=%async_computation.10 | async-start | bytes 9461760 | tf_op jit(solution)/shard_map/all_gather | solution.py:64
  94.0 249.7 %all-gather.13.cloned.1.call-start = ((), (), s32[]{:S(2)}) async-start(), calls=%async_computation.9 | async-start | bytes 9461760 | tf_op jit(solution)/shard_map/all_gather | solution.py:64
  94.6 331.2 %all-gather.17.cloned.1.call-start = ((), (), s32[]{:S(2)}) async-start(), calls=%async_computation.11 | async-start | bytes 9461760 | tf_op jit(solution)/shard_map/all_gather | solution.py:64
  95.2 507.7 %reduce-scatter.7.cloned.1.call-start = ((), (), s32[]{:S(2)}) async-start(), calls=%async_computation.12 | async-start | bytes 3276800 | tf_op jit(solution)/shard_map/reduce_scatter | solution.py:190
  103.0 23.3 %copy-start.7 = (bf16[2,256,5,4,64]{1,0,4,3,2:T(2,128)(2,1)}, bf16[2,256,5,4,64]{1,0,4,3,2:T(2,128)(2,1)S(1)}, u32[]{:S(2)}) copy-start(bf16[2,256,5,4,64]{1,0,4,3,2:T(2,128)(2,1)S(1)} %convert_element_type.135) | copy-start | bytes 3932164
  123.3 19.2 %copy-start.5 = (bf16[2,1024,320]{1,2,0:T(8,128)(2,1)}, bf16[2,1024,320]{1,2,0:T(8,128)(2,1)S(1)}, u32[]{:S(2)}) copy-start(bf16[2,1024,320]{1,2,0:T(8,128)(2,1)S(1)} %copy.87) | copy-start | bytes 3932164
  142.6 17.2 %copy-start.13 = (bf16[2,1024,320]{1,2,0:T(8,128)(2,1)S(1)}, bf16[2,1024,320]{1,2,0:T(8,128)(2,1)}, u32[]{:S(2)}) copy-start(bf16[2,1024,320]{1,2,0:T(8,128)(2,1)} %copy.86) | copy-start | bytes 3932164
  185.4 275.0 %copy-start = (f32[512,1280]{1,0:T(8,128)}, f32[512,1280]{1,0:T(8,128)S(1)}, u32[]{:S(2)}) copy-start(f32[512,1280]{1,0:T(8,128)S(1)} %get-tuple-element.110) | copy-start | bytes 7864324
  441.6 9.8 copy-start.32
  451.4 9.1 copy-start.21
  460.5 2.3 copy-start.9
  461.3 1.5 copy-start.10
  472.9 16.5 %copy-start.14 = (bf16[2,1024,320]{1,2,0:T(8,128)(2,1)S(1)}, bf16[2,1024,320]{1,2,0:T(8,128)(2,1)}, u32[]{:S(2)}) copy-start(bf16[2,1024,320]{1,2,0:T(8,128)(2,1)} %copy.86) | copy-start | bytes 3932164
  472.9 16.5 %copy-start.15 = (bf16[2,256,5,4,64]{1,4,3,2,0:T(8,128)(2,1)S(1)}, bf16[2,256,5,4,64]{1,4,3,2,0:T(8,128)(2,1)}, u32[]{:S(2)}) copy-start(bf16[2,256,5,4,64]{1,4,3,2,0:T(8,128)(2,1)} %copy.93) | copy-start | bytes 3932164
  519.0 34.2 %copy-start.8 = (bf16[2,256,5,4,64]{1,0,4,3,2:T(2,128)(2,1)S(1)}, bf16[2,256,5,4,64]{1,0,4,3,2:T(2,128)(2,1)}, u32[]{:S(2)}) copy-start(bf16[2,256,5,4,64]{1,0,4,3,2:T(2,128)(2,1)} %copy-done.7) | copy-start | bytes 3932164
  563.9 1.6 copy-start.16
  569.3 1.7 copy-start.11
  569.3 175.0 %reduce-scatter.11.cloned.1.call-start = ((), (), s32[]{:S(2)}) async-start(), calls=%async_computation.14 | async-start | bytes 3379200 | tf_op jit(solution)/shard_map/reduce_scatter | solution.py:68
  575.9 1.5 copy-start.6
  576.0 309.1 %reduce-scatter.9.cloned.1.call-start = ((), (), s32[]{:S(2)}) async-start(), calls=%async_computation.13 | async-start | bytes 5406720 | tf_op jit(solution)/shard_map/reduce_scatter | solution.py:68
  589.9 4.0 copy-start.20
  590.0 4.0 copy-start.26
  602.8 2.0 copy-start.3
  602.8 2.0 copy-start.28
  602.8 2.0 copy-start.30
  604.9 7.9 copy-start.24
  620.1 1.3 copy-start.23
  620.2 413.3 %reduce-scatter.15.cloned.1.call-start = ((), (), s32[]{:S(2)}) async-start(), calls=%async_computation.16 | async-start | bytes 9461760 | tf_op jit(solution)/shard_map/reduce_scatter | solution.py:68
  630.8 551.2 %reduce-scatter.13.cloned.1.call-start = ((), (), s32[]{:S(2)}) async-start(), calls=%async_computation.15 | async-start | bytes 9461760 | tf_op jit(solution)/shard_map/reduce_scatter | solution.py:68
  640.4 1.3 copy-start.22
  640.4 690.2 %reduce-scatter.17.cloned.1.call-start = ((), (), s32[]{:S(2)}) async-start(), calls=%async_computation.17 | async-start | bytes 9461760 | tf_op jit(solution)/shard_map/reduce_scatter | solution.py:68
  652.2 1.8 copy-start.1
  653.9 10.8 copy-start.4
  653.9 10.8 copy-start.12
  653.9 10.8 copy-start.18
Sparse Core Ops, SparseCore 0:
  13.1 67.9 all-gather.6
  92.8 24.4 all-gather.8
  120.1 59.2 all-gather.10
  182.1 79.4 all-gather.14
  264.4 79.3 all-gather.12
  346.5 79.3 all-gather.16
  569.5 33.3 reduce-scatter.6
  605.2 139.0 reduce-scatter.10
  746.6 138.4 reduce-scatter.8
  887.2 146.2 reduce-scatter.14
  1035.8 146.2 reduce-scatter.12
  1184.3 146.2 reduce-scatter.16

commit v2 on v1

--- a/solution.py
+++ b/solution.py
@@ -1,6 +1,10 @@
+import functools
+
 import jax
 import jax.numpy as jnp
 from jax import lax
+from jax.experimental import pallas as pl
+from jax.experimental.pallas import tpu as pltpu
 from jax.sharding import PartitionSpec as P
 
 HD = 64
@@ -60,14 +64,190 @@
     return jnp.einsum(spec, a, b, preferred_element_type=jnp.float32)
 
 
-def gather_rows(shard):
-    return lax.all_gather(shard, BOTH, axis=0, tiled=True)
-
-
-def scatter_rows(full):
-    return lax.psum_scatter(
-        full.astype(jnp.bfloat16), BOTH, scatter_dimension=0, tiled=True
-    ).astype(jnp.float32)
+class Place:
+    def __init__(self):
+        self.Z=lax.axis_size("dp")//2; self.X=lax.axis_size("fsdp")//2
+        dp=lax.axis_index("dp"); fs=lax.axis_index("fsdp")
+        self.z=dp//2; self.y=dp%2; self.x=fs//2; self.c=fs%2
+    def device(self,s=0,dy=0,dx=0,dc=0):
+        return (lax.rem(self.z+s,self.Z)*2+lax.rem(self.y+dy,2), lax.rem(self.x+dx,self.X)*2+lax.rem(self.c+dc,2))
+    def slot(self,s,dy,dx,dc):
+        return ((lax.rem(self.z+self.Z-s,self.Z)*2+lax.rem(self.y+dy,2))*self.X+lax.rem(self.x+dx,self.X))*2+lax.rem(self.c+dc,2)
+
+MESH = pl.DeviceIdType.MESH
+
+def greet(me):
+    barrier=pltpu.get_barrier_semaphore()
+    friends=[me.device(s=s) for s in range(1,me.Z)]+[me.device(dy=1),me.device(dx=1),me.device(dc=1)]
+    for f in friends:
+        pl.semaphore_signal(barrier,inc=1,device_id=f,device_id_type=MESH)
+    pl.semaphore_wait(barrier,len(friends))
+
+def gather_kernel(Z, orders, ahead, *refs):
+    K=len(orders)
+    shards=refs[:K]; outs=refs[K:2*K]; local,send,recv=refs[2*K:]
+    me=Place()
+    greet(me)
+    dims={"y":1,"x":2,"c":3}
+    def sem(rel):
+        return ((rel[0]*2+rel[1])*2+rel[2])*2+rel[3]
+    started=[]
+    def start(k,rel,to):
+        if isinstance(to,int):
+            target=me.device(s=to); landed=(to,0,0,0)
+        else:
+            landed=list(rel); landed[dims[to]]=1; landed=tuple(landed)
+            target=me.device(**{"d"+to:1})
+        slot=me.slot(*rel)
+        src=shards[k] if rel==(0,0,0,0) else outs[k].at[slot]
+        cp=pltpu.make_async_remote_copy(src_ref=src,dst_ref=outs[k].at[slot],send_sem=send.at[k,sem(landed)],recv_sem=recv.at[k,sem(landed)],device_id=target,device_id_type=MESH)
+        cp.start()
+        table[(k,landed)]=cp
+    table={}
+    own=[]
+    def first(k):
+        cp=pltpu.make_async_copy(shards[k],outs[k].at[me.slot(0,0,0,0)],local.at[k]); cp.start(); own.append(cp)
+        for s in range(1,Z): start(k,(0,0,0,0),s)
+        for d in orders[k]: start(k,(0,0,0,0),d)
+    def arrive(k,rel,rest):
+        table[(k,rel)].wait_recv()
+        for d in rest: start(k,rel,d)
+    def rel_of(s,o,a,b=0,c=0):
+        r=[s,0,0,0]; r[dims[o[0]]]=a; r[dims[o[1]]]=b; r[dims[o[2]]]=c
+        return tuple(r)
+    for k in range(min(ahead,K)): first(k)
+    for t in range(K+3):
+        if t+ahead<K: first(t+ahead)
+        k=t
+        if k<K:
+            o=orders[k]
+            for s in range(1,Z): arrive(k,rel_of(s,o,0),o)
+        k=t-1
+        if 0<=k<K:
+            o=orders[k]
+            for s in range(Z): arrive(k,rel_of(s,o,1),o[1:])
+        k=t-2
+        if 0<=k<K:
+            o=orders[k]
+            for s in range(Z):
+                for a in range(2): arrive(k,rel_of(s,o,a,1),o[2:])
+        k=t-3
+        if 0<=k<K:
+            o=orders[k]
+            for s in range(Z):
+                for a in range(2):
+                    for b in range(2): arrive(k,rel_of(s,o,a,b,1),"")
+    for cp in own: cp.wait()
+    for cp in table.values(): cp.wait_send()
+
+def gather(shards, orders, cid, ahead=2):
+    n=lax.axis_size("dp")*lax.axis_size("fsdp"); Z=lax.axis_size("dp")//2; K=len(shards)
+    return pl.pallas_call(functools.partial(gather_kernel,Z,orders,ahead),
+        out_shape=[jax.ShapeDtypeStruct((n,)+s.shape,s.dtype) for s in shards],
+        in_specs=[pl.BlockSpec(memory_space=pl.ANY)]*K,
+        out_specs=[pl.BlockSpec(memory_space=pl.ANY)]*K,
+        scratch_shapes=[pltpu.SemaphoreType.DMA((K,)),pltpu.SemaphoreType.DMA((K,8*Z)),pltpu.SemaphoreType.DMA((K,8*Z))],
+        compiler_params=pltpu.CompilerParams(collective_id=cid,has_side_effects=True))(*shards)
+
+
+def tile_of(N):
+    for t in (512,384,256,128):
+        if N%t==0: return t
+    return N
+
+def scatter_kernel(Z, orders, ahead, dims_, *refs):
+    K=len(orders)
+    parts=refs[:K]; outs=refs[K:2*K]
+    sc=refs[2*K:]
+    first_buf=sc[:K]; one_buf=sc[K:2*K]; two_buf=sc[2*K:3*K]; last_buf=sc[3*K:4*K]
+    shapes=sorted(set(dims_))
+    stage=[sc[4*K+shapes.index(d)] for d in dims_]
+    local,send,recv=sc[4*K+len(shapes):]
+    me=Place()
+    greet(me)
+    copies={}
+    def ship(k,name,index,src,dst,target):
+        cp=pltpu.make_async_remote_copy(src_ref=src,dst_ref=dst,send_sem=send.at[k,index],recv_sem=recv.at[k,index],device_id=target,device_id_type=MESH)
+        cp.start(); copies[(k,name)]=cp
+    def part(k,a,b,other):
+        o=orders[k]
+        rel={o[0]:a,o[1]:b}
+        y=lax.rem(me.y+rel["y"],2); x=lax.rem(me.x+rel["x"],me.X); c=lax.rem(me.c+other,2)
+        return parts[k].at[:,y,x,c]
+    order4=((1,1),(1,0),(0,1),(0,0))
+    locals_={}
+    def first(k):
+        for i,(a,b) in enumerate(order4):
+            ship(k,("c",a,b),i,part(k,a,b,1),first_buf[k].at[a,b],me.device(dc=1))
+    def bring(k,i):
+        a,b=order4[i]
+        cp=pltpu.make_async_copy(part(k,a,b,0),stage[k].at[i%2],local.at[k,i%2]); cp.start(); locals_[(k,i)]=cp
+    def add(dst,src,k):
+        _,r,N=dims_[k]
+        t=tile_of(N)
+        def body(i,_):
+            zi=i//(N//t); j=i%(N//t)
+            cols=pl.ds(pl.multiple_of(j*t,128),t)
+            dst[zi,:,cols]=dst[zi,:,cols]+src[zi,:,cols]
+            return 0
+        lax.fori_loop(0,Z*(N//t),body,0)
+    def step_c(k):
+        bring(k,0); bring(k,1)
+        for i,(a,b) in enumerate(order4):
+            copies[(k,("c",a,b))].wait_recv()
+            locals_[(k,i)].wait()
+            add(first_buf[k].at[a,b],stage[k].at[i%2],k)
+            if i+2<4: bring(k,i+2)
+            if a==1:
+                ship(k,("1",b),4+b,first_buf[k].at[1,b],one_buf[k].at[b],me.device(**{"d"+orders[k][0]:1}))
+    def step_1(k):
+        for b in (1,0):
+            copies[(k,("1",b))].wait_recv()
+            add(first_buf[k].at[0,b],one_buf[k].at[b],k)
+            if b==1:
+                ship(k,"2",6,first_buf[k].at[0,1],two_buf[k],me.device(**{"d"+orders[k][1]:1}))
+    def step_2(k):
+        copies[(k,"2")].wait_recv()
+        add(first_buf[k].at[0,0],two_buf[k],k)
+        for s in range(1,Z):
+            ship(k,("z",s),6+s,first_buf[k].at[0,0,lax.rem(me.z+s,Z)],last_buf[k].at[s-1],me.device(s=s))
+    def step_z(k):
+        _,r,N=dims_[k]
+        for s in range(1,Z): copies[(k,("z",s))].wait_recv()
+        t=tile_of(N)
+        mine=first_buf[k].at[0,0,me.z]
+        def body(j,_):
+            cols=pl.ds(pl.multiple_of(j*t,128),t)
+            total=mine[:,cols].astype(jnp.float32)
+            for s in range(1,Z): total=total+last_buf[k][s-1,:,cols].astype(jnp.float32)
+            outs[k][:,cols]=total
+            return 0
+        lax.fori_loop(0,N//t,body,0)
+    for k in range(min(ahead,K)): first(k)
+    for t in range(K+3):
+        if t+ahead<K: first(t+ahead)
+        if t<K: step_c(t)
+        if 0<=t-1<K: step_1(t-1)
+        if 0<=t-2<K: step_2(t-2)
+        if 0<=t-3<K: step_z(t-3)
+    for cp in copies.values(): cp.wait_send()
+
+def scatter(parts, orders, cid, ahead=2):
+    n=lax.axis_size("dp")*lax.axis_size("fsdp"); Z=lax.axis_size("dp")//2; X=lax.axis_size("fsdp")//2; K=len(parts)
+    dims_=[(n,p.shape[0]//n,p.shape[1]) for p in parts]
+    parts=[p.reshape(Z,2,X,2,p.shape[0]//n,p.shape[1]) for p in parts]
+    bf=jnp.bfloat16
+    sc=[pltpu.VMEM((2,2,Z,r,N),bf) for _,r,N in dims_]+[pltpu.VMEM((2,Z,r,N),bf) for _,r,N in dims_]+[pltpu.VMEM((Z,r,N),bf) for _,r,N in dims_]+[pltpu.VMEM((Z-1,r,N),bf) for _,r,N in dims_]+[pltpu.VMEM((2,Z,r,N),bf) for _,r,N in sorted(set(dims_))]
+    return pl.pallas_call(functools.partial(scatter_kernel,Z,orders,ahead,dims_),
+        out_shape=[jax.ShapeDtypeStruct((r,N),jnp.float32) for _,r,N in dims_],
+        in_specs=[pl.BlockSpec(memory_space=pl.ANY)]*K,
+        out_specs=[pl.BlockSpec(memory_space=pltpu.VMEM)]*K,
+        scratch_shapes=sc+[pltpu.SemaphoreType.DMA((K,2)),pltpu.SemaphoreType.DMA((K,6+Z)),pltpu.SemaphoreType.DMA((K,6+Z))],
+        compiler_params=pltpu.CompilerParams(collective_id=cid,has_side_effects=True,vmem_limit_bytes=63*2**20))(*parts)
+
+
+def half_of(full):
+    return full.astype(jnp.bfloat16)
 
 
 def on_device(
@@ -99,15 +279,15 @@
 
     extras = jnp.zeros((shard, 128), jnp.bfloat16)
     extras = extras.at[:, 0].set(attn_gain).at[:, 1].set(mlp_gain)
-    first_pack = gather_rows(
-        jnp.concatenate([w_query, key_matrix, value_matrix, extras], axis=1)
+    first_shard = jnp.concatenate([w_query, key_matrix, value_matrix, extras], axis=1)
+    fulls = gather(
+        (first_shard, w_out, w_gate, w_up, w_down), ("yxc", "xyc", "yxc", "xyc", "yxc"), 1, 5
+    )
+    first_pack, out_full, gate_full, up_full, down_full = (
+        f.reshape(-1, f.shape[-1]) for f in fulls
     )
     projection = first_pack[:, : query_features + 2 * key_features]
     gains = first_pack[:, query_features + 2 * key_features :][:, :2].astype(jnp.float32).T
-    out_full = gather_rows(w_out)
-    gate_full = gather_rows(w_gate)
-    up_full = gather_rows(w_up)
-    down_full = gather_rows(w_down)
 
     x_float = inputs.reshape(tokens, width).astype(jnp.float32)
     places = positions.reshape(batches, rows)
@@ -154,18 +334,18 @@
 
     cot_low = cotangent.reshape(tokens, width)
     cot_float = cot_low.astype(jnp.float32)
-    grad_down = scatter_rows(left_dot(hidden, cot_low))
+    grad_down = half_of(left_dot(hidden, cot_low))
     grad_hidden = right_dot(cot_low, down_full)
     sig_slope = gate_sig * (1.0 + gate_pre * (1.0 - gate_sig))
     grad_gate_pre = (grad_hidden * up_proj * sig_slope).astype(jnp.bfloat16)
     grad_up_pre = (grad_hidden * gate_pre * gate_sig).astype(jnp.bfloat16)
-    grad_gate = scatter_rows(left_dot(normed_mlp, grad_gate_pre))
-    grad_up = scatter_rows(left_dot(normed_mlp, grad_up_pre))
+    grad_gate = half_of(left_dot(normed_mlp, grad_gate_pre))
+    grad_up = half_of(left_dot(normed_mlp, grad_up_pre))
     grad_normed_mlp = right_dot(grad_gate_pre, gate_full) + right_dot(grad_up_pre, up_full)
     grad_mlp_gain = jnp.sum(grad_normed_mlp * mixed * mlp_inverse, 0)
     grad_mixed = cot_float + norm_back(grad_normed_mlp * mlp_gain_f, mixed, mlp_inverse)
     grad_mixed_low = grad_mixed.astype(jnp.bfloat16)
-    grad_out = scatter_rows(left_dot(attended, grad_mixed_low))
+    grad_out = half_of(left_dot(attended, grad_mixed_low))
     grad_attended = right_dot(grad_mixed_low, out_full).astype(jnp.bfloat16)
     grad_attended = grad_attended.reshape(batches, rows, kv_heads, group, HD)
 
@@ -201,7 +381,10 @@
     grad_input = grad_mixed + norm_back(grad_normed * attn_gain_f, x_float, attn_inverse)
     gain_columns = jnp.stack([grad_attn_gain, grad_mlp_gain], -1)
     gain_columns = jnp.pad(gain_columns, ((0, 0), (0, 126)))
-    last = scatter_rows(jnp.concatenate([grad_projection, gain_columns], 1))
+    grad_first = half_of(jnp.concatenate([grad_projection, gain_columns], 1))
+    grad_down, grad_gate, grad_up, grad_out, last = scatter(
+        (grad_down, grad_gate, grad_up, grad_out, grad_first), ("xy", "yx", "xy", "yx", "xy"), 2
+    )
     split = query_features + key_features
     return (
         output.reshape(inputs.shape),

time: 1350 us -> 1270 us (0.941)
  waiting for transfers between devices: 958 us -> 2.6 us
  local copies, waits for them, and re-layouts: 55.8 us -> 562 us
  Pallas kernels: 0 us -> 382 us
    reduce_scatter x6 -> x0, waiting for transfers between devices: 661 us -> none  [the longest x5 654 us: scatter_rows(): lax.psum_scatter(full.astype(jnp.bfloat16), BOTH, scatter_dimension=0, ti...]
    unnamed x70 -> x97, local copies, waits for them, and re-layouts: 12.8 us -> 504 us
    pallas_call x0 -> x2, Pallas kernels: none -> 382 us  [the longest x1 211 us: scatter(): pl.pallas_call(functools.partial(scatter_kernel, Z, orders, ahead, dims_)...]
    all_gather x5 -> x0, waiting for transfers between devices: 280 us -> none  [gather_rows(): return lax.all_gather(shard, BOTH, axis=0, tiled=True)]
  transfers between devices with their start and end apart: 12 -> 2, of which waited for: 11 -> 2; matrix products, arithmetic and copies ran while one was open for 15% -> 5% of each run, Pallas kernels for 0% -> 0%
where the time goes in v2:
time: 1270 us; the launch traced here: 1260 us
  local copies, waits for them, and re-layouts  562 us (44%)
  Pallas kernels  382 us (30%)
  matrix products  220 us (17%)
  other arithmetic  79.8 us (6%)
  between operations  15 us (1%)
    unnamed x97, local copies, waits for them, and re-layouts  504 us
    pallas_call x1, Pallas kernels, scatter(): pl.pallas_call(functools.partial(scatter_kernel, Z, orders, ahead, dims_)...  211 us
    pallas_call x1, Pallas kernels, gather(): pl.pallas_call(functools.partial(gather_kernel, Z, orders, ahead), out_sh...  172 us
    dot_general x6, matrix products, einsum32(): return jnp.einsum(spec, a, b, preferred_element_type=jnp.float32)  103 us
    dot_general x5, matrix products, right_dot(): lax.dot_general(left, right, (((1,), (1,)), ((), ())), preferred_element_...  45.3 us
    dot_general x5, matrix products, left_dot(): lax.dot_general(left, right, (((0,), (0,)), ((), ())), preferred_element_...  36.4 us
    dot_general x5, matrix products, plain_dot(): return jnp.dot(left, right, preferred_element_type=jnp.float32)  35.1 us
    convert_element_type x1, other arithmetic, on_device(): grad_scores = (probabilities * (grad_probs - row_dot)).astype(jnp.bfloat16)  34.2 us
  transfers between devices with their start and end apart: 2, of which 2 were waited for; matrix products, arithmetic and copies ran while one was open for 5% of the time, Pallas kernels for 0%

profile of v2, /device:TPU:0, one launch (start us, length us, event | category | flops | bytes accessed | tf_op | source)
XLA Modules:
  0.0 1261.6 jit_solution(12678011585802991052)
XLA Ops:
  8.5 1.3 fusion.46
  9.9 1.3 fusion.47
  11.5 1.7 concatenate.39.refs_0_
  13.2 171.6 %shard_map.203 = (bf16[32,40,2048]{2,1,0:T(8,128)(2,1)}, bf16[32,40,1280]{2,1,0:T(8,128)(2,1)}, bf16[32,40,3584]{2,1,0:T(8,128)(2,1)}, bf16[32,40,3584]{2,1,0:T(8,128)(2,1)}, bf16[32,112,1280]{2,1,0:T(8,128)(2,1)}) custom-call(bf16[40,2048]{1,0:T(8,128)(2,1)} %concatenate.39.refs_0_, bf16[40,1280]{1,0:T(8,128)(2,1)} %refs_1_.1, bf16[40,3584]{1,0:T(8,128)(2,1)} %refs_2_.1, ...), custom_call_target="tpu_custom_call" | custom-call | tf_op jit(solution)/shard_map/pallas_call | solution.py:145
  186.8 4.9 fusion.11
  192.0 1.6 copy-done.15
  194.5 2.2 copy.98
  197.7 1.2 subtract_convert_fusion.2
  199.6 1.2 copy.99
  200.8 1.1 pad_maximum_fusion.3
  202.5 3.4 slice.139
  205.9 3.2 copy.102
  209.1 2.1 multiply_subtract_fusion
  211.3 1.4 fusion.18
  212.7 4.1 convert_element_type.123
  216.8 1.5 copy.120
  218.9 11.8 fusion.54
  230.7 1.3 all-gather.2.cloned.1.call-done
  232.0 3.9 fusion.50
  235.9 1.5 copy.100
  237.4 1.7 copy.101
  239.1 18.0 %fusion.3 = (f32[2,5,4,256]{3,2,1,0:T(4,128)S(1)}, f32[2,5,1024,256,4]{3,2,4,1,0:T(8,128)}) fusion(pred[2,256,1024]{1,2,0:T(8,128)(4,1)S(1)} %fusion.31, bf16[2,1024,5,64,1]{1,3,4,2,0:T(8,128)(2,1)S(1)} %bitcast.190, bf16[2,256,5,4,64]{1,0,4,3,2:T(2,128)(2,1)} %convert_element_type.123), kind=kOutput, calls=%fused_computation.8 | convolution fusion | flops 1363138560 | bytes 45129728 | tf_op jit(solution)/shard_map/bqkgd,bskd->bkgqs/dot_general | solution.py:64
  257.1 17.1 %exponential_reduce_fusion = f32[2,5,4,256]{3,2,1,0:T(4,128)S(1)} fusion(f32[2,5,1024,256,4]{3,2,4,1,0:T(8,128)} %get-tuple-element.128, f32[2,5,4,256]{3,2,1,0:T(4,128)S(1)} %get-tuple-element.127, pred[2,256,1024]{1,2,0:T(8,128)(4,1)S(1)} %fusion.31), kind=kLoop, calls=%fused_computation.7 | loop fusion | flops 31447040 | bytes 42549248 | tf_op jit(solution)/shard_map/reduce_sum | solution.py:320
  274.2 18.4 %fusion.38 = bf16[2,256,5,4,64]{1,4,3,2,0:T(8,128)(2,1)} fusion(bf16[2,1024,5,64,1]{1,3,4,2,0:T(8,128)(2,1)S(1)} %bitcast.202, f32[2,5,1024,256,4]{3,2,4,1,0:T(8,128)} %get-tuple-element.128, f32[2,5,4,256]{3,2,1,0:T(4,128)S(1)} %log_add_fusion, pred[2,256,1024]{1,2,0:T(8,128)(4,1)S(1)} %fusion.31), kind=kOutput, calls=%fused_computation.66 | convolution fusion | flops 1374289920 | bytes 45129728 | tf_op jit(solution)/shard_map/bkgqs,bskd->bqkgd/dot_general | solution.py:64
  292.7 2.8 copy.105
  295.8 2.1 multiply_reduce_fusion.2
  298.7 6.9 fusion.53
  305.6 15.3 %fusion.8 = (bf16[512,3584]{1,0:T(8,128)(2,1)S(1)}, bf16[512,3584]{1,0:T(8,128)(2,1)}, bf16[512,3584]{1,0:T(8,128)(2,1)}) fusion(f32[3584,512]{0,1:T(8,128)} %fusion.54, f32[512,3584]{1,0:T(8,128)} %fusion.53, bf16[512,1280]{1,0:T(8,128)(2,1)S(1)} %multiply_convert_fusion.1, bf16[1280,3584]{1,0:T(8,128)(2,1)} %bitcast.236), kind=kOutput, calls=%fused_computation.19 | convolution fusion | flops 4726980608 | bytes 36175872 | tf_op jit(solution)/shard_map/dot_general | solution.py:41
  320.9 12.4 fusion.55
  333.4 10.3 multiply_reduce_fusion
  344.5 1.5 copy-done.8
  346.0 3.0 convolution_convert_fusion.5
  349.0 3.8 reshape.396
  352.8 3.7 copy.108
  356.5 28.5 %fusion = (f32[2,5,4,256]{3,2,1,0:T(4,128)S(1)}, f32[2,5,1024,256,4]{3,2,4,1,0:T(8,128)}) fusion(f32[2,5,1024,256,4]{3,2,4,1,0:T(8,128)} %get-tuple-element.128, f32[2,5,4,256]{3,2,1,0:T(4,128)S(1)} %log_add_fusion, pred[2,256,1024]{1,2,0:T(8,128)(4,1)S(1)} %fusion.31, bf16[2,1024,5,64,1]{1,3,4,2,0:T(8,128)(2,1)} %bitcast.201, ...), kind=kOutput, calls=%fused_computation.2 | convolution fusion | flops 1384110080 | bytes 87113728 | tf_op jit(solution)/shard_map/bqkgd,bskd->bkgqs/dot_general | solution.py:64
  385.0 16.9 %bitcast_convert_fusion = bf16[2,5,64,1024]{3,2,1,0:T(8,128)(2,1)} fusion(bf16[2,256,5,4,64]{1,4,3,2,0:T(8,128)(2,1)S(1)} %copy-done.14, f32[2,5,1024,256,4]{3,2,4,1,0:T(8,128)} %get-tuple-element.128, f32[2,5,4,256]{3,2,1,0:T(4,128)S(1)} %log_add_fusion, pred[2,256,1024]{1,2,0:T(8,128)(4,1)S(1)} %fusion.31), kind=kOutput, calls=%fused_computation.38 | convolution fusion | flops 1374289920 | bytes 45129728 | tf_op jit(solution)/shard_map/bkgqs,bqkgd->bskd/dot_general | solution.py:64
  402.0 34.2 %fusion.2 = bf16[2,5,4,256,1024]{3,4,2,1,0:T(8,128)(2,1)} fusion(f32[2,5,1024,256,4]{3,2,4,1,0:T(8,128)} %get-tuple-element.133, f32[2,5,1024,256,4]{3,2,4,1,0:T(8,128)} %get-tuple-element.128, f32[2,5,4,256]{3,2,1,0:T(4,128)S(1)} %get-tuple-element.132, f32[2,5,4,256]{3,2,1,0:T(4,128)S(1)} %log_add_fusion, pred[2,256,1024]{1,2,0:T(8,128)(4,1)S(1)} %fusion.31), kind=kLoop, calls=%fused_computation.4 | loop fusion | flops 52428800 | bytes 105463808 | tf_op jit(solution)/shard_map/convert_element_type | solution.py:357
  436.2 9.0 multiply_bitcast_fusion
  445.2 12.1 bitcast_convert_fusion.1
  457.3 3.5 convolution_convert_fusion.3
  460.9 3.6 copy.110
  464.4 3.6 mul.362
  468.0 2.8 copy.116
  470.8 1.3 copy.115
  472.1 4.9 pad_maximum_fusion.1
  477.1 113.9 %copy.134 = bf16[2,1024,640]{0,2,1:T(8,128)(2,1)} copy(bf16[2,1024,640]{1,0,2:T(2,128)(2,1)} %pad_maximum_fusion.1) | data formatting | bytes 5242880
  590.9 257.2 %reshape.394 = bf16[1024,1280]{1,0:T(8,128)(2,1)} reshape(bf16[1024,640,2]{2,1,0:T(8,128)(2,1)} %bitcast.56) | data formatting | bytes 5242880
  850.2 11.5 convolution_convert_fusion.1
  861.7 9.9 convolution_convert_fusion
  871.7 6.0 fusion.13
  877.6 7.3 convolution_convert_fusion.2
  884.9 1.3 reduce-scatter.4.cloned.1.call-done
  886.2 88.1 %reshape.395 = bf16[256,640,2]{2,1,0:T(8,128)(2,1)} reshape(bf16[256,1280]{1,0:T(8,128)(2,1)} %reduce-scatter.4.cloned.1.call-done) | data formatting | bytes 1310720
  974.3 36.5 %copy.135 = bf16[2,256,640]{1,0,2:T(2,128)(2,1)S(1)} copy(bf16[2,256,640]{0,2,1:T(8,128)(2,1)} %bitcast.188) | data formatting | bytes 1310720
  1012.2 1.3 copy.119
  1013.5 2.3 concatenate.46
  1015.8 7.8 fusion.21
  1024.0 4.2 convolution_convert_fusion.4
  1028.2 3.1 pad_maximum_fusion.refs_4_
  1031.3 210.5 %shard_map.204 = (f32[112,1280]{1,0:T(8,128)}, f32[40,3584]{1,0:T(8,128)}, f32[40,3584]{1,0:T(8,128)}, f32[40,1280]{1,0:T(8,128)}, f32[40,2048]{1,0:T(8,128)}) custom-call(bf16[4,2,2,2,112,1280]{5,4,3,2,1,0:T(8,128)(2,1)} %bitcast.199, bf16[4,2,2,2,40,3584]{5,4,3,2,1,0:T(8,128)(2,1)} %bitcast.197, bf16[4,2,2,2,40,3584]{5,4,3,2,1,0:T(8,128)(2,1)} %bitcast.198, ...), custom_call_target="tpu_custom_call" | custom-call | tf_op jit(solution)/shard_map/pallas_call | solution.py:241
  1241.8 1.5 slice_reduce_fusion
  1243.3 1.6 slice.126
  1245.0 1.6 fusion.52
  1246.6 4.9 fusion.29
  (136 shorter events, 16.5 us)
Async XLA Ops:
  7.2 178.9 %copy-start.2 = (bf16[2,1,256,1280]{3,2,1,0:T(8,128)(2,1)S(1)}, bf16[2,1,256,1280]{3,2,1,0:T(8,128)(2,1)}, u32[]{:S(2)}) copy-start(bf16[2,1,256,1280]{3,2,1,0:T(8,128)(2,1)} %param.16) | copy-start | bytes 3932164
  7.2 224.8 %all-gather.2.cloned.1.call-start = ((), (), s32[]{:S(2)}) async-start(), calls=%async_computation.1 | async-start | bytes 3276800 | tf_op jit(solution)/shard_map/all_gather | solution.py:312
  186.1 5.6 copy-start.28
  186.4 5.3 copy-start.30
  191.7 1.9 copy-start.15
  191.7 5.0 copy-start.32
  197.7 11.4 copy-start.17
  201.9 684.3 %reduce-scatter.4.cloned.1.call-start = ((), (), s32[]{:S(2)}) async-start(), calls=%async_computation.2 | async-start | bytes 3276800
  239.1 18.0 %copy-start.4 = (bf16[2,1024,320]{1,2,0:T(8,128)(2,1)}, bf16[2,1024,320]{1,2,0:T(8,128)(2,1)S(1)}, u32[]{:S(2)}) copy-start(bf16[2,1024,320]{1,2,0:T(8,128)(2,1)S(1)} %copy.101) | copy-start | bytes 3932164
  257.1 17.1 %copy-start.13 = (bf16[2,1024,320]{1,2,0:T(8,128)(2,1)S(1)}, bf16[2,1024,320]{1,2,0:T(8,128)(2,1)}, u32[]{:S(2)}) copy-start(bf16[2,1024,320]{1,2,0:T(8,128)(2,1)} %copy.100) | copy-start | bytes 3932164
  292.7 3.1 copy-start.7
  292.7 5.5 slice-start.3
  295.8 2.1 copy-start.10
  295.8 2.8 slice-start.4
  295.8 2.9 slice-start.5
  297.9 45.8 %copy-start = (f32[512,1280]{1,0:T(8,128)}, f32[512,1280]{1,0:T(8,128)S(1)}, u32[]{:S(2)}) copy-start(f32[512,1280]{1,0:T(8,128)S(1)} %get-tuple-element.130) | copy-start | bytes 7864324
  298.2 7.4 copy-start.21
  320.9 12.4 copy-start.35
  333.4 10.3 copy-start.19
  344.5 1.5 copy-start.8
  356.5 28.5 %copy-start.14 = (bf16[2,256,5,4,64]{1,4,3,2,0:T(8,128)(2,1)S(1)}, bf16[2,256,5,4,64]{1,4,3,2,0:T(8,128)(2,1)}, u32[]{:S(2)}) copy-start(bf16[2,256,5,4,64]{1,4,3,2,0:T(8,128)(2,1)} %copy.108) | copy-start | bytes 3932164
  402.0 34.2 %copy-start.5 = (bf16[2,1024,320]{1,2,0:T(8,128)(2,1)S(1)}, bf16[2,1024,320]{1,2,0:T(8,128)(2,1)}, u32[]{:S(2)}) copy-start(bf16[2,1024,320]{1,2,0:T(8,128)(2,1)} %copy-done.4) | copy-start | bytes 3932164
  436.2 9.0 copy-start.6
  445.2 12.1 copy-start.9
  445.2 12.1 copy-start.11
  468.0 2.8 copy-start.12
  848.1 0.8 copy-start.18
  848.1 0.9 copy-start.23
  849.4 0.8 copy-start.33
  850.2 11.5 copy-start.22
  850.2 21.4 %slice-start = ((s8[9175040]{0:T(1024)(128)(4,1)}), s8[4194304]{0:T(1024)(128)(4,1)S(1)}, s32[]{:S(2)}) async-start(s8[9175040]{0:T(1024)(128)(4,1)} %bitcast.229), calls=%async_computation.3 | async-start | bytes 8388608
  850.2 21.4 %slice-start.1 = ((s8[9175040]{0:T(1024)(128)(4,1)}), s8[4194304]{0:T(1024)(128)(4,1)S(1)}, s32[]{:S(2)}) async-start(s8[9175040]{0:T(1024)(128)(4,1)} %bitcast.229), calls=%async_computation.4 | async-start | bytes 8388608
  861.7 9.9 copy-start.1
  861.7 9.9 slice-start.2
  861.7 9.9 copy-start.34
  871.6 6.0 copy-start.20
  1011.9 3.9 copy-start.3
  1011.9 3.9 copy-start.29
  1011.9 3.9 copy-start.31
  1015.8 8.2 copy-start.16
  1246.6 4.9 copy-start.27
  1246.6 5.6 copy-start.26
  1246.6 6.4 copy-start.25
  1251.5 2.3 copy-start.24
Sparse Core Ops, SparseCore 0:
  202.1 29.8 all-gather.1
  848.2 37.9 reduce-scatter.3

commit v3 on v2

--- a/solution.py
+++ b/solution.py
@@ -21,22 +21,6 @@
     return (jnp.cos(angles), jnp.sin(angles))
 
 
-def rotate(field, cos_table, sin_table, sign):
-    shaped = field.reshape(field.shape[0], -1, HD)
-    first_half = shaped[..., : HD // 2]
-    second_half = shaped[..., HD // 2 :]
-    cos_heads = cos_table[:, None, :]
-    sin_heads = sin_table[:, None, :] * sign
-    turned = jnp.concatenate(
-        [
-            first_half * cos_heads - second_half * sin_heads,
-            second_half * cos_heads + first_half * sin_heads,
-        ],
-        -1,
-    )
-    return turned.reshape(field.shape)
-
-
 def plain_dot(left, right):
     return jnp.dot(left, right, preferred_element_type=jnp.float32)
 
@@ -58,10 +42,6 @@
         grad_normed
         - inputs_float * inverse * inverse * jnp.mean(grad_normed * inputs_float, -1, keepdims=True)
     )
-
-
-def einsum32(spec, a, b):
-    return jnp.einsum(spec, a, b, preferred_element_type=jnp.float32)
 
 
 class Place:
@@ -246,6 +226,175 @@
         compiler_params=pltpu.CompilerParams(collective_id=cid,has_side_effects=True,vmem_limit_bytes=63*2**20))(*parts)
 
 
+def dot_t(left, right):
+    return lax.dot_general(
+        left, right, (((1,), (1,)), ((), ())), preferred_element_type=jnp.float32
+    )
+
+
+def swap_halves(u):
+    lane = lax.broadcasted_iota(jnp.int32, u.shape, 1)
+    down = pltpu.roll(u, 32, 1)
+    up = pltpu.roll(u, 96, 1)
+    return jnp.where(lax.rem(lane, 64) < 32, up, down)
+
+
+def project_kernel(h_ref, w_ref, cos_ref, sin_ref, out_ref):
+    u = plain_dot(h_ref[...], w_ref[...])
+    for j in range(u.shape[1] // 128):
+        piece = u[:, j * 128 : (j + 1) * 128]
+        turned = piece * cos_ref[0] + swap_halves(piece) * sin_ref[0]
+        out_ref[:, j * 128 : (j + 1) * 128] = turned.astype(jnp.bfloat16)
+
+
+def project(normed, weight, cos_tables, sin_tables, width):
+    tokens, depth = normed.shape
+    steps = weight.shape[1] // width
+    return pl.pallas_call(
+        project_kernel,
+        grid=(steps,),
+        in_specs=[
+            pl.BlockSpec((tokens, depth), lambda j: (0, 0)),
+            pl.BlockSpec((depth, width), lambda j: (0, j)),
+            pl.BlockSpec((1, tokens, 128), lambda j: (j // (steps - 1), 0, 0)),
+            pl.BlockSpec((1, tokens, 128), lambda j: (j // (steps - 1), 0, 0)),
+        ],
+        out_specs=pl.BlockSpec((tokens, width), lambda j: (0, j)),
+        out_shape=jax.ShapeDtypeStruct((tokens, steps * width), jnp.bfloat16),
+        compiler_params=pltpu.CompilerParams(vmem_limit_bytes=48 * 2**20),
+        cost_estimate=pl.CostEstimate(
+            flops=2 * tokens * depth * weight.shape[1],
+            bytes_accessed=2 * depth * weight.shape[1],
+            transcendentals=0,
+        ),
+    )(normed, weight, cos_tables, sin_tables)
+
+
+def lane_masks(rows):
+    lane = lax.broadcasted_iota(jnp.int32, (rows, 128), 1)
+    low_side = (lane < 64).astype(jnp.float32)
+    return low_side.astype(jnp.bfloat16), (1.0 - low_side).astype(jnp.bfloat16)
+
+
+def swapped(kv):
+    return pltpu.roll(kv.astype(jnp.float32), 64, 1).astype(jnp.bfloat16)
+
+
+def attend_kernel(group, q_ref, kv_ref, bias_ref, o_ref, log_ref):
+    kv = kv_ref[0]
+    sides = (kv, swapped(kv))
+    rows = q_ref.shape[0]
+    masks = lane_masks(rows)
+    lane = lax.broadcasted_iota(jnp.int32, (rows, 128), 1)
+    logs = jnp.zeros((rows, 128), jnp.float32)
+    bias = bias_ref[0]
+    for pair in range(group // 2):
+        cols = slice(pair * 128, pair * 128 + 128)
+        q = q_ref[:, cols]
+        found = []
+        for half in range(2):
+            scores = dot_t(q * masks[half], sides[half]) + bias
+            top = jnp.max(scores, -1, keepdims=True)
+            powers = jnp.exp(scores - top)
+            total = jnp.sum(powers, -1, keepdims=True)
+            probs = (powers * (1.0 / total)).astype(jnp.bfloat16)
+            found.append(plain_dot(probs, sides[1 - half]))
+            logs = jnp.where(lane == pair * 2 + half, top + jnp.log(total), logs)
+        o_ref[:, cols] = jnp.where(lane < 64, found[0], found[1]).astype(jnp.bfloat16)
+    log_ref[...] = logs
+
+
+def attend(projected, both_all, bias, kv_heads, group):
+    batches, length, _ = both_all.shape
+    rows = projected.shape[0] // batches
+    wide = group * HD
+    return pl.pallas_call(
+        functools.partial(attend_kernel, group),
+        grid=(batches, kv_heads),
+        in_specs=[
+            pl.BlockSpec((rows, wide), lambda b, h: (b, h)),
+            pl.BlockSpec((1, length, 128), lambda b, h: (b, 0, h)),
+            pl.BlockSpec((1, rows, length), lambda b, h: (b, 0, 0)),
+        ],
+        out_specs=[
+            pl.BlockSpec((rows, wide), lambda b, h: (b, h)),
+            pl.BlockSpec((rows, 128), lambda b, h: (b, h)),
+        ],
+        out_shape=[
+            jax.ShapeDtypeStruct((batches * rows, kv_heads * wide), jnp.bfloat16),
+            jax.ShapeDtypeStruct((batches * rows, kv_heads * 128), jnp.float32),
+        ],
+        compiler_params=pltpu.CompilerParams(vmem_limit_bytes=48 * 2**20),
+    )(projected, both_all, bias)
+
+
+def attend_back_kernel(
+    group, q_ref, do_ref, kv_ref, bias_ref, log_ref, cos_ref, sin_ref, dq_ref, dkv_ref
+):
+    kv = kv_ref[0]
+    sides = (kv, swapped(kv))
+    rows = q_ref.shape[0]
+    length = kv.shape[0]
+    masks = lane_masks(rows)
+    lane = lax.broadcasted_iota(jnp.int32, (rows, 128), 1)
+    bias = bias_ref[0]
+    key_sum = jnp.zeros((128, length), jnp.float32)
+    value_sum = jnp.zeros((128, length), jnp.float32)
+    for pair in range(group // 2):
+        cols = slice(pair * 128, pair * 128 + 128)
+        q = q_ref[:, cols]
+        do = do_ref[:, cols]
+        found = []
+        for half in range(2):
+            q_half = q * masks[half]
+            do_half = do * masks[half]
+            at = pair * 2 + half
+            log_total = log_ref[:, at : at + 1]
+            probs = jnp.exp(dot_t(q_half, sides[half]) + bias - log_total)
+            grad_probs = dot_t(do_half, sides[1 - half])
+            row_dot = jnp.sum(probs * grad_probs, -1, keepdims=True)
+            grad_scores = (probs * (grad_probs - row_dot)).astype(jnp.bfloat16)
+            found.append(plain_dot(grad_scores, sides[half]))
+            key_sum = key_sum + left_dot(q_half, grad_scores)
+            value_sum = value_sum + left_dot(do_half, probs.astype(jnp.bfloat16))
+        dq = jnp.where(lane < 64, found[0], found[1])
+        dq = dq * cos_ref[0] - swap_halves(dq) * sin_ref[0]
+        dq_ref[:, cols] = dq.astype(jnp.bfloat16)
+    both = jnp.concatenate(
+        [key_sum[:64] + key_sum[64:], value_sum[:64] + value_sum[64:]], 0
+    )
+    dkv_ref[0] = both.T.astype(jnp.bfloat16)
+
+
+def attend_back(projected, grad_attended, both_all, bias, logs, cos_tables, sin_tables, group):
+    batches, length, _ = both_all.shape
+    rows = projected.shape[0] // batches
+    wide = group * HD
+    kv_heads = both_all.shape[2] // 128
+    return pl.pallas_call(
+        functools.partial(attend_back_kernel, group),
+        grid=(batches, kv_heads),
+        in_specs=[
+            pl.BlockSpec((rows, wide), lambda b, h: (b, h)),
+            pl.BlockSpec((rows, wide), lambda b, h: (b, h)),
+            pl.BlockSpec((1, length, 128), lambda b, h: (b, 0, h)),
+            pl.BlockSpec((1, rows, length), lambda b, h: (b, 0, 0)),
+            pl.BlockSpec((rows, 128), lambda b, h: (b, h)),
+            pl.BlockSpec((1, rows, 128), lambda b, h: (0, b, 0)),
+            pl.BlockSpec((1, rows, 128), lambda b, h: (0, b, 0)),
+        ],
+        out_specs=[
+            pl.BlockSpec((rows, wide), lambda b, h: (b, h)),
+            pl.BlockSpec((1, length, 128), lambda b, h: (b, 0, h)),
+        ],
+        out_shape=[
+            jax.ShapeDtypeStruct((batches * rows, kv_heads * wide), jnp.bfloat16),
+            jax.ShapeDtypeStruct((batches, length, kv_heads * 128), jnp.bfloat16),
+        ],
+        compiler_params=pltpu.CompilerParams(vmem_limit_bytes=48 * 2**20),
+    )(projected, grad_attended, both_all, bias, logs, cos_tables, sin_tables)
+
+
 def half_of(full):
     return full.astype(jnp.bfloat16)
 
@@ -279,49 +428,51 @@
 
     extras = jnp.zeros((shard, 128), jnp.bfloat16)
     extras = extras.at[:, 0].set(attn_gain).at[:, 1].set(mlp_gain)
-    first_shard = jnp.concatenate([w_query, key_matrix, value_matrix, extras], axis=1)
+    pairs = jnp.concatenate(
+        [key_matrix.reshape(shard, kv_heads, HD), value_matrix.reshape(shard, kv_heads, HD)], -1
+    )
+    first_shard = jnp.concatenate([w_query, pairs.reshape(shard, -1), extras], axis=1)
     fulls = gather(
         (first_shard, w_out, w_gate, w_up, w_down), ("yxc", "xyc", "yxc", "xyc", "yxc"), 1, 5
     )
     first_pack, out_full, gate_full, up_full, down_full = (
         f.reshape(-1, f.shape[-1]) for f in fulls
     )
-    projection = first_pack[:, : query_features + 2 * key_features]
-    gains = first_pack[:, query_features + 2 * key_features :][:, :2].astype(jnp.float32).T
+    used = query_features + 2 * key_features
+    projection = first_pack[:, :used]
+    gains = first_pack[:, used : used + 2].astype(jnp.float32).T
 
     x_float = inputs.reshape(tokens, width).astype(jnp.float32)
     places = positions.reshape(batches, rows)
     cos_table, sin_table = rope_tables(places.reshape(tokens))
+    ones, zeros = jnp.ones((tokens, HD), jnp.float32), jnp.zeros((tokens, HD), jnp.float32)
+    cos_pair = jnp.concatenate([cos_table, cos_table], -1)
+    sin_pair = jnp.concatenate([-sin_table, sin_table], -1)
+    cos_tables = jnp.stack(
+        [
+            jnp.concatenate([cos_pair, cos_pair], -1) * score_scale,
+            jnp.concatenate([cos_pair, ones], -1),
+        ]
+    )
+    sin_tables = jnp.stack(
+        [
+            jnp.concatenate([sin_pair, sin_pair], -1) * score_scale,
+            jnp.concatenate([sin_pair, zeros], -1),
+        ]
+    )
     doc_start = query_index[None, :] - places
     allowed = (key_index[None, None, :] <= query_index[None, :, None]) & (
         key_index[None, None, :] >= doc_start[:, :, None]
     )
+    bias = jnp.where(allowed, 0.0, NEGATIVE)
     attn_inverse = lax.rsqrt(jnp.mean(x_float * x_float, -1, keepdims=True) + EPSILON)
     attn_gain_f = gains[0]
     mlp_gain_f = gains[1]
     normed = (x_float * attn_inverse * attn_gain_f).astype(jnp.bfloat16)
-    projected = plain_dot(normed, projection)
-    queries = (
-        rotate(projected[:, :query_features], cos_table, sin_table, 1.0) * score_scale
-    ).astype(jnp.bfloat16)
-    key_rows = rotate(
-        projected[:, query_features : query_features + key_features], cos_table, sin_table, 1.0
-    ).astype(jnp.bfloat16)
-    value_rows = projected[:, query_features + key_features :].astype(jnp.bfloat16)
-    both_rows = jnp.concatenate([key_rows, value_rows], -1).reshape(batches, rows, -1)
+    projected = project(normed, projection, cos_tables, sin_tables, 2 * key_features)
+    both_rows = projected[:, query_features:].reshape(batches, rows, -1)
     both_all = lax.all_gather(both_rows, "fsdp", axis=1, tiled=True)
-    key_heads = both_all[..., :key_features].reshape(batches, length, kv_heads, HD)
-    value_heads = both_all[..., key_features:].reshape(batches, length, kv_heads, HD)
-    grouped = queries.reshape(batches, rows, kv_heads, group, HD)
-    mask = allowed[:, None, None]
-    scores = einsum32("bqkgd,bskd->bkgqs", grouped, key_heads)
-    scores = jnp.where(mask, scores, NEGATIVE)
-    row_max = jnp.max(scores, -1, keepdims=True)
-    row_total = jnp.sum(jnp.exp(scores - row_max), -1, keepdims=True)
-    log_total = row_max + jnp.log(row_total)
-    probs_low = jnp.exp(scores - log_total).astype(jnp.bfloat16)
-    attended = einsum32("bkgqs,bskd->bqkgd", probs_low, value_heads)
-    attended = attended.reshape(tokens, query_features).astype(jnp.bfloat16)
+    attended, logs = attend(projected, both_all, bias, kv_heads, group)
 
     mixed = x_float + plain_dot(attended, out_full)
     mlp_inverse = lax.rsqrt(jnp.mean(mixed * mixed, -1, keepdims=True) + EPSILON)
@@ -347,34 +498,18 @@
     grad_mixed_low = grad_mixed.astype(jnp.bfloat16)
     grad_out = half_of(left_dot(attended, grad_mixed_low))
     grad_attended = right_dot(grad_mixed_low, out_full).astype(jnp.bfloat16)
-    grad_attended = grad_attended.reshape(batches, rows, kv_heads, group, HD)
-
-    scores_again = einsum32("bqkgd,bskd->bkgqs", grouped, key_heads)
-    scores_again = jnp.where(mask, scores_again, NEGATIVE)
-    probabilities = jnp.exp(scores_again - log_total)
-    grad_probs = einsum32("bqkgd,bskd->bkgqs", grad_attended, value_heads)
-    row_dot = jnp.sum(probabilities * grad_probs, -1, keepdims=True)
-    grad_scores = (probabilities * (grad_probs - row_dot)).astype(jnp.bfloat16)
-    grad_query_rot = einsum32("bkgqs,bskd->bqkgd", grad_scores, key_heads)
-    key_portion = einsum32("bkgqs,bqkgd->bskd", grad_scores, grouped)
-    value_portion = einsum32(
-        "bkgqs,bqkgd->bskd", probabilities.astype(jnp.bfloat16), grad_attended
-    )
-    portions = jnp.concatenate(
-        [
-            key_portion.reshape(batches, length, key_features),
-            value_portion.reshape(batches, length, key_features),
-        ],
-        -1,
-    ).astype(jnp.bfloat16)
+    grad_query_pre, portions = attend_back(
+        projected, grad_attended, both_all, bias, logs, cos_tables, sin_tables, group
+    )
     sums = lax.psum_scatter(portions, "fsdp", scatter_dimension=1, tiled=True)
-    sums = sums.astype(jnp.float32).reshape(tokens, 2 * key_features)
-    grad_query_pre = rotate(
-        grad_query_rot.reshape(tokens, query_features) * score_scale, cos_table, sin_table, -1.0
-    ).astype(jnp.bfloat16)
-    grad_key_pre = rotate(sums[:, :key_features], cos_table, sin_table, -1.0).astype(jnp.bfloat16)
-    grad_value_pre = sums[:, key_features:].astype(jnp.bfloat16)
-    grad_pre = jnp.concatenate([grad_query_pre, grad_key_pre, grad_value_pre], -1)
+    sums = sums.astype(jnp.float32).reshape(tokens, kv_heads, 128)
+    turned = jnp.concatenate([sums[..., 32:64], sums[..., :32], sums[..., 64:]], -1)
+    grad_pair_pre = (sums * cos_tables[1][:, None] - turned * sin_tables[1][:, None]).astype(
+        jnp.bfloat16
+    )
+    grad_pre = jnp.concatenate(
+        [grad_query_pre, grad_pair_pre.reshape(tokens, 2 * key_features)], -1
+    )
     grad_projection = left_dot(normed, grad_pre)
     grad_normed = right_dot(grad_pre, projection)
     grad_attn_gain = jnp.sum(grad_normed * x_float * attn_inverse, 0)
@@ -385,16 +520,16 @@
     grad_down, grad_gate, grad_up, grad_out, last = scatter(
         (grad_down, grad_gate, grad_up, grad_out, grad_first), ("xy", "yx", "xy", "yx", "xy"), 2
     )
-    split = query_features + key_features
+    last_pairs = last[:, query_features:used].reshape(shard, kv_heads, 2, HD)
     return (
         output.reshape(inputs.shape),
         grad_input.astype(jnp.bfloat16).reshape(inputs.shape),
-        last[:, split + key_features],
+        last[:, used],
         last[:, :query_features],
-        last[:, query_features:split],
-        last[:, split : split + key_features],
+        last_pairs[:, :, 0].reshape(shard, key_features),
+        last_pairs[:, :, 1].reshape(shard, key_features),
         grad_out,
-        last[:, split + key_features + 1],
+        last[:, used + 1],
         grad_gate,
         grad_up,
         grad_down,

time: 1270 us -> 654 us (0.51)
  local copies, waits for them, and re-layouts: 562 us -> 36.6 us
  matrix products: 220 us -> 111 us
  Pallas kernels: 382 us -> 451 us
  other arithmetic: 79.8 us -> 24.3 us
    unnamed x97 -> x81, local copies, waits for them, and re-layouts: 504 us -> 5.31 us
    dot_general x6 -> x0, matrix products: 103 us -> none  [einsum32(): return jnp.einsum(spec, a, b, preferred_element_type=jnp.float32)]
    pallas_call x0 -> x3, Pallas kernels: none -> 72 us  [the longest x1 37.3 us: attend_back(): pl.pallas_call(functools.partial(attend_back_kernel, group), grid=(batche...]
    convert_element_type x2 -> x1, other arithmetic: 35.7 us -> 2.01 us  [on_device(): (sums * cos_tables[1][:, None] - turned * sin_tables[1][:, None]).astype(...]
    reduce_sum x1 -> x0, other arithmetic: 17.1 us -> none  [on_device(): row_total = jnp.sum(jnp.exp(scores - row_max), -1, keepdims=True)]
    slice x12 -> x7, local copies, waits for them, and re-layouts: 22.3 us -> 9.27 us  [the longest x1 5.11 us: on_device(): projection = first_pack[:, :used]]
    dot_general x5 -> x4, matrix products: 35.1 us -> 34.7 us  [plain_dot(): return jnp.dot(left, right, preferred_element_type=jnp.float32)]
  transfers between devices with their start and end apart: 2 -> 2, of which waited for: 2 -> 1; matrix products, arithmetic and copies ran while one was open for 5% -> 9% of each run, Pallas kernels for 0% -> 0%
where the time goes in v3:
time: 654 us; the launch traced here: 646 us
  Pallas kernels  451 us (69%)
  matrix products  111 us (17%)
  local copies, waits for them, and re-layouts  36.6 us (6%)
  other arithmetic  24.3 us (4%)
  between operations  15.1 us (2%)
  waiting for transfers between devices  7.36 us (1%)
    pallas_call x1, Pallas kernels, scatter(): pl.pallas_call(functools.partial(scatter_kernel, Z, orders, ahead, dims_)...  207 us
    pallas_call x1, Pallas kernels, gather(): pl.pallas_call(functools.partial(gather_kernel, Z, orders, ahead), out_sh...  172 us
    dot_general x5, matrix products, right_dot(): lax.dot_general(left, right, (((1,), (1,)), ((), ())), preferred_element_...  41.1 us
    pallas_call x1, Pallas kernels, attend_back(): pl.pallas_call(functools.partial(attend_back_kernel, group), grid=(batche...  37.3 us
    dot_general x5, matrix products, left_dot(): lax.dot_general(left, right, (((0,), (0,)), ((), ())), preferred_element_...  34.8 us
    dot_general x4, matrix products, plain_dot(): return jnp.dot(left, right, preferred_element_type=jnp.float32)  34.7 us
    pallas_call x1, Pallas kernels, attend(): pl.pallas_call(functools.partial(attend_kernel, group), grid=(batches, kv...  28.5 us
  transfers between devices with their start and end apart: 2, of which 1 were waited for; matrix products, arithmetic and copies ran while one was open for 9% of the time, Pallas kernels for 0%

profile of v3, /device:TPU:0, one launch (start us, length us, event | category | flops | bytes accessed | tf_op | source)
XLA Modules:
  0.0 645.6 jit_solution(3101068742227643121)
XLA Ops:
  7.2 0.6 compare_reduce_fusion.1
  7.9 0.6 compare_reduce_fusion
  8.5 0.9 reshape.515
  9.4 0.9 reshape.516
  10.3 1.3 fusion.29
  11.8 1.3 fusion.30
  13.3 1.6 pad_maximum_fusion.6.refs_0_
  14.9 171.6 %shard_map.203 = (bf16[32,40,2048]{2,1,0:T(8,128)(2,1)}, bf16[32,40,1280]{2,1,0:T(8,128)(2,1)}, bf16[32,40,3584]{2,1,0:T(8,128)(2,1)}, bf16[32,40,3584]{2,1,0:T(8,128)(2,1)}, bf16[32,112,1280]{2,1,0:T(8,128)(2,1)}) custom-call(bf16[40,2048]{1,0:T(8,128)(2,1)} %pad_maximum_fusion.6.refs_0_, bf16[40,1280]{1,0:T(8,128)(2,1)} %refs_1_.1, ...), custom_call_target="tpu_custom_call" | custom-call | tf_op jit(solution)/shard_map/pallas_call | solution.py:125
  186.5 1.0 convert_bitcast_fusion
  187.6 5.1 slice.87.w_ref
  192.8 0.6 slice_reduce_fusion
  193.5 0.3 fusion.16
  193.8 1.0 fusion.27
  194.8 0.5 maximum_multiply_fusion.1
  195.6 0.6 copy-done.13
  196.2 0.4 fusion.10.h_ref
  196.6 6.2 shard_map.204.q_ref
  202.8 1.0 slice.88
  203.8 0.6 reduce-scatter.2.cloned.1.call-start
  204.4 1.8 copy.35
  206.2 0.8 copy.32
  207.0 2.2 mul.275
  209.2 2.8 copy.33
  212.0 1.5 copy.37
  213.5 0.2 iota_compare_fusion.1
  213.8 1.8 fusion.18.bias_ref
  215.6 10.9 %fusion.36 = f32[3584,512]{0,1:T(8,128)} fusion(bf16[3584,1280]{1,0:T(8,128)(2,1)} %bitcast.146, bf16[512,1280]{1,0:T(8,128)(2,1)S(1)} %bitcast.136), kind=kOutput, calls=%fused_computation.95 | convolution fusion | flops 4697620480 | bytes 17825792 | tf_op jit(solution)/shard_map/dot_general | solution.py:35
  226.5 7.3 %all-gather.2.cloned.1.call-done.kv_ref = bf16[2,1024,640]{2,1,0:T(8,128)(2,1)} async-done(((bf16[2,256,640]{2,1,0:T(8,128)(2,1)}), bf16[2,1024,640]{2,1,0:T(8,128)(2,1)}) %all-gather.2.cloned.1.call-update) | async-done | bytes 2621456 | tf_op jit(solution)/shard_map/all_gather | solution.py:474
  233.8 28.5 %shard_map.205 = (bf16[512,1280]{1,0:T(8,128)(2,1)S(1)}, f32[512,640]{1,0:T(8,128)S(1)}) custom-call(bf16[512,1920]{1,0:T(8,128)(2,1)S(1)} %shard_map.204.q_ref, bf16[2,1024,640]{2,1,0:T(8,128)(2,1)} %all-gather.2.cloned.1.call-done.kv_ref, f32[2,256,1024]{2,1,0:T(8,128)} %fusion.18.bias_ref), custom_call_target="tpu_custom_call" | custom-call | tf_op jit(solution)/shard_map/pallas_call | solution.py:311
  262.4 2.0 multiply_reduce_fusion.2
  264.4 0.3 multiply_convert_fusion.1
  264.7 11.6 %fusion.35 = f32[512,3584]{1,0:T(8,128)} fusion(bf16[512,1280]{1,0:T(8,128)(2,1)S(1)} %multiply_convert_fusion.1, bf16[1280,3584]{1,0:T(8,128)(2,1)} %bitcast.150), kind=kOutput, calls=%fused_computation.94 | convolution fusion | flops 4697620480 | bytes 17825792 | tf_op jit(solution)/shard_map/dot_general | solution.py:25
  276.3 15.2 %fusion.3 = (bf16[512,3584]{1,0:T(8,128)(2,1)}, bf16[512,3584]{1,0:T(8,128)(2,1)S(1)}, bf16[512,3584]{1,0:T(8,128)(2,1)}) fusion(f32[3584,512]{0,1:T(8,128)} %fusion.36, f32[512,3584]{1,0:T(8,128)} %fusion.35, bf16[512,1280]{1,0:T(8,128)(2,1)S(1)} %multiply_convert_fusion.1, bf16[1280,3584]{1,0:T(8,128)(2,1)} %bitcast.152), kind=kOutput, calls=%fused_computation.9 | convolution fusion | flops 4726980608 | bytes 36175872 | tf_op jit(solution)/shard_map/dot_general | solution.py:25
  291.5 10.3 %fusion.37 = f32[512,1280]{1,0:T(8,128)} fusion(bf16[512,3584]{1,0:T(8,128)(2,1)S(1)} %get-tuple-element.96, bf16[1280,3584]{1,0:T(8,128)(2,1)} %bitcast.153), kind=kOutput, calls=%fused_computation.96 | convolution fusion | flops 4697620480 | bytes 15466496 | tf_op jit(solution)/shard_map/dot_general | solution.py:35
  301.8 10.9 %multiply_reduce_fusion = (bf16[1280]{0:T(1024)(128)(2,1)S(1)}, f32[512]{0:T(512)S(1)}, f32[512,1280]{1,0:T(8,128)S(1)}) fusion(f32[512,1280]{1,0:T(8,128)S(1)} %get-tuple-element.107, f32[512]{0:T(512)S(1)} %add_rsqrt_fusion, f32[1280]{0:T(1024)S(1)} %get-tuple-element.89, f32[512,1280]{1,0:T(8,128)} %fusion.37, bf16[512,3584]{1,0:T(8,128)(2,1)} %get-tuple-element.95, ...), kind=kOutput, calls=%fused_computation.35 | convolution fusion | flops 4702206464 | bytes 20721152 | tf_op jit(solution)/shard_map/dot_general | solution.py:35
  312.7 0.8 multiply_add_fusion
  313.5 1.1 copy-done.30
  314.6 1.9 convolution_convert_fusion.5.do_ref
  316.6 37.3 %shard_map.206 = (bf16[512,1280]{1,0:T(8,128)(2,1)S(1)}, bf16[2,1024,640]{2,1,0:T(8,128)(2,1)}) custom-call(bf16[512,1920]{1,0:T(8,128)(2,1)} %copy-done, bf16[512,1280]{1,0:T(8,128)(2,1)S(1)} %convolution_convert_fusion.5.do_ref, bf16[2,1024,640]{2,1,0:T(8,128)(2,1)} %all-gather.2.cloned.1.call-done.kv_ref, f32[2,256,1024]{2,1,0:T(8,128)} %fusion.18.bias_ref, ...), custom_call_target="tpu_custom_call" | custom-call | tf_op jit(solution)/shard_map/pallas_call | solution.py:374
  354.0 5.4 convolution_convert_fusion.3
  359.4 7.4 %convolution_convert_fusion = bf16[1280,3584]{1,0:T(8,128)(2,1)} fusion(bf16[512,1280]{1,0:T(8,128)(2,1)S(1)} %copy-done.18, bf16[512,3584]{1,0:T(8,128)(2,1)S(1)} %copy-done.33), kind=kOutput, calls=%fused_computation | convolution fusion | flops 4702208000 | bytes 14155776 | tf_op jit(solution)/shard_map/dot_general | solution.py:29
  366.8 9.7 %convolution_convert_fusion.1 = bf16[1280,3584]{1,0:T(8,128)(2,1)} fusion(bf16[512,1280]{1,0:T(8,128)(2,1)S(1)} %copy-done.18, bf16[512,3584]{1,0:T(8,128)(2,1)} %copy-done.32), kind=kOutput, calls=%fused_computation.1 | convolution fusion | flops 4702208000 | bytes 14155776 | tf_op jit(solution)/shard_map/dot_general | solution.py:29
  376.6 5.9 fusion.4
  382.6 7.3 %convolution_convert_fusion.2 = bf16[3584,1280]{1,0:T(8,128)(2,1)} fusion(bf16[512,3584]{1,0:T(8,128)(2,1)S(1)} %copy-done.31, bf16[512,1280]{1,0:T(8,128)(2,1)S(1)} %bitcast.137), kind=kOutput, calls=%fused_computation.2 | convolution fusion | flops 4702208000 | bytes 14155776 | tf_op jit(solution)/shard_map/dot_general | solution.py:29
  389.9 3.0 copy.34
  392.9 2.4 reshape.530
  395.6 1.5 copy.36
  397.1 2.0 fusion.21
  399.2 7.1 %fusion.7 = (bf16[1280]{0:T(1024)(128)(2,1)S(1)}, f32[512]{0:T(512)S(1)}, f32[512,1280]{1,0:T(8,128)}) fusion(bf16[2,1,256,1280]{3,2,1,0:T(8,128)(2,1)S(1)} %copy-done.7, f32[512]{0:T(512)S(1)} %bitcast.143, f32[1280]{0:T(1024)S(1)} %get-tuple-element.90, bf16[1280,2048]{1,0:T(8,128)(2,1)} %bitcast.130, bf16[512,640]{1,0:T(8,128)(2,1)S(1)} %fusion.21, ...), kind=kOutput, calls=%fused_computation.24 | convolution fusion | flops 2525100288 | bytes 10825216 | tf_op jit(solution)/shard_map/dot_general | solution.py:35
  406.3 4.9 convolution_convert_fusion.4
  411.3 0.2 copy.44
  411.6 5.4 pad_maximum_fusion.refs_4_
  417.0 207.3 %shard_map.207 = (f32[112,1280]{1,0:T(8,128)}, f32[40,3584]{1,0:T(8,128)}, f32[40,3584]{1,0:T(8,128)}, f32[40,1280]{1,0:T(8,128)}, f32[40,2048]{1,0:T(8,128)}) custom-call(bf16[4,2,2,2,112,1280]{5,4,3,2,1,0:T(8,128)(2,1)} %bitcast.125, bf16[4,2,2,2,40,3584]{5,4,3,2,1,0:T(8,128)(2,1)} %bitcast.124, bf16[4,2,2,2,40,3584]{5,4,3,2,1,0:T(8,128)(2,1)} %bitcast.123, ...), custom_call_target="tpu_custom_call" | custom-call | tf_op jit(solution)/shard_map/pallas_call | solution.py:221
  624.4 1.0 slice.81
  625.4 1.6 slice.80
  627.0 1.5 slice_reduce_fusion.4
  628.7 0.6 slice_reduce_fusion.2
  629.3 0.7 reshape_squeeze.6
  630.0 0.7 reshape_squeeze.7
  630.7 4.5 fusion.15
  635.2 0.7 copy.55
  635.9 0.8 copy.56
  636.7 0.8 copy.57
  637.5 0.8 copy.58
  (107 shorter events, 1.8 us)
Async XLA Ops:
  7.2 226.7 %all-gather.2.cloned.1.call-start = ((), (), s32[]{:S(2)}) async-start(), calls=%async_computation.1 | async-start | bytes 3276800 | tf_op jit(solution)/shard_map/all_gather | solution.py:474
  187.5 5.1 copy-start.27
  187.6 5.9 copy-start.5
  193.8 1.8 copy-start.25
  195.5 0.7 copy-start.13
  195.6 7.2 %copy-start.1 = (f32[2,512,128]{2,1,0:T(8,128)}, f32[2,512,128]{2,1,0:T(8,128)S(1)}, u32[]{:S(2)}) copy-start(f32[2,512,128]{2,1,0:T(8,128)S(1)} %pad_maximum_fusion.4.cos_ref) | copy-start | bytes 1572868
  195.6 7.2 %copy-start.3 = (f32[2,512,128]{2,1,0:T(8,128)}, f32[2,512,128]{2,1,0:T(8,128)S(1)}, u32[]{:S(2)}) copy-start(f32[2,512,128]{2,1,0:T(8,128)S(1)} %pad_maximum_fusion.5.sin_ref) | copy-start | bytes 1572868
  202.8 31.1 %copy-start = (bf16[512,1920]{1,0:T(8,128)(2,1)}, bf16[512,1920]{1,0:T(8,128)(2,1)S(1)}, u32[]{:S(2)}) copy-start(bf16[512,1920]{1,0:T(8,128)(2,1)S(1)} %shard_map.204.q_ref) | copy-start | bytes 5898244
  203.8 186.1 %reduce-scatter.2.cloned.1.call-start = ((), (), s32[]{:S(2)}) async-start(), calls=%async_computation.2 | async-start | bytes 3276800 | tf_op jit(solution)/shard_map/reduce_scatter | solution.py:504
  209.2 4.4 copy-start.28
  213.5 2.1 copy-start.14
  233.8 28.5 %copy-start.6 = (bf16[2,1,256,1280]{3,2,1,0:T(8,128)(2,1)S(1)}, bf16[2,1,256,1280]{3,2,1,0:T(8,128)(2,1)}, u32[]{:S(2)}) copy-start(bf16[2,1,256,1280]{3,2,1,0:T(8,128)(2,1)} %param.16) | copy-start | bytes 3932164
  233.8 28.5 %copy-start.29 = (bf16[32,40,1280]{2,1,0:T(8,128)(2,1)S(1)}, bf16[32,40,1280]{2,1,0:T(8,128)(2,1)}, u32[]{:S(2)}) copy-start(bf16[32,40,1280]{2,1,0:T(8,128)(2,1)} %get-tuple-element.51) | copy-start | bytes 9830404
  264.4 48.3 %copy-start.10 = (f32[512,1280]{1,0:T(8,128)}, f32[512,1280]{1,0:T(8,128)S(1)}, u32[]{:S(2)}) copy-start(f32[512,1280]{1,0:T(8,128)S(1)} %get-tuple-element.107) | copy-start | bytes 7864324
  264.7 11.6 %copy-start.17 = (bf16[512,1280]{1,0:T(8,128)(2,1)}, bf16[512,1280]{1,0:T(8,128)(2,1)S(1)}, u32[]{:S(2)}) copy-start(bf16[512,1280]{1,0:T(8,128)(2,1)S(1)} %multiply_convert_fusion.1) | copy-start | bytes 3932164
  291.5 10.3 %copy-start.32 = (bf16[512,3584]{1,0:T(8,128)(2,1)}, bf16[512,3584]{1,0:T(8,128)(2,1)S(1)}, u32[]{:S(2)}) copy-start(bf16[512,3584]{1,0:T(8,128)(2,1)S(1)} %get-tuple-element.96) | copy-start | bytes 11010052
  301.8 10.9 %copy-start.15 = (bf16[2,1,256,1280]{3,2,1,0:T(8,128)(2,1)S(1)}, bf16[2,1,256,1280]{3,2,1,0:T(8,128)(2,1)}, u32[]{:S(2)}) copy-start(bf16[2,1,256,1280]{3,2,1,0:T(8,128)(2,1)} %param.18) | copy-start | bytes 3932164
  312.7 1.9 copy-start.30
  314.6 1.9 copy-start.9
  314.6 1.9 copy-start.2
  314.6 2.0 copy-start.4
  353.9 5.5 copy-start.18
  354.0 5.5 copy-start.33
  359.4 17.1 %slice-start = ((s8[9175040]{0:T(1024)(128)(4,1)}), s8[4194304]{0:T(1024)(128)(4,1)S(1)}, s32[]{:S(2)}) async-start(s8[9175040]{0:T(1024)(128)(4,1)} %bitcast.147), calls=%async_computation.3 | async-start | bytes 8388608
  359.4 17.1 %slice-start.1 = ((s8[9175040]{0:T(1024)(128)(4,1)}), s8[4194304]{0:T(1024)(128)(4,1)S(1)}, s32[]{:S(2)}) async-start(s8[9175040]{0:T(1024)(128)(4,1)} %bitcast.147), calls=%async_computation.4 | async-start | bytes 8388608
  366.8 9.8 %copy-start.11 = (f32[512,1280]{1,0:T(8,128)S(1)}, f32[512,1280]{1,0:T(8,128)}, u32[]{:S(2)}) copy-start(f32[512,1280]{1,0:T(8,128)} %copy-done.10) | copy-start | bytes 7864324
  366.8 9.8 %slice-start.2 = ((s8[9175040]{0:T(1024)(128)(4,1)}), s8[786432]{0:T(1024)(128)(4,1)S(1)}, s32[]{:S(2)}) async-start(s8[9175040]{0:T(1024)(128)(4,1)} %bitcast.147), calls=%async_computation.5 | async-start | bytes 1572864
  366.8 9.8 %copy-start.31 = (bf16[512,3584]{1,0:T(8,128)(2,1)S(1)}, bf16[512,3584]{1,0:T(8,128)(2,1)}, u32[]{:S(2)}) copy-start(bf16[512,3584]{1,0:T(8,128)(2,1)} %get-tuple-element.97) | copy-start | bytes 11010052
  376.6 6.0 copy-start.16
  392.9 2.5 copy-start.20
  395.4 1.7 copy-start.12
  397.1 2.1 copy-start.7
  397.1 2.1 copy-start.26
  399.2 7.2 %copy-start.19 = (bf16[1280,512]{1,0:T(8,128)(2,1)S(1)}, bf16[1280,512]{1,0:T(8,128)(2,1)}, u32[]{:S(2)}) copy-start(bf16[1280,512]{1,0:T(8,128)(2,1)} %copy.37) | copy-start | bytes 3932164
  624.4 6.3 copy-start.8
  630.7 4.5 copy-start.24
  630.7 5.2 copy-start.23
  630.7 6.0 copy-start.22
  635.2 2.3 copy-start.21
Sparse Core Ops, SparseCore 0:
  203.9 29.8 all-gather.1
  354.1 34.6 reduce-scatter.1

commit v4 on v3

--- a/solution.py
+++ b/solution.py
@@ -128,6 +128,442 @@
         out_specs=[pl.BlockSpec(memory_space=pl.ANY)]*K,
         scratch_shapes=[pltpu.SemaphoreType.DMA((K,)),pltpu.SemaphoreType.DMA((K,8*Z)),pltpu.SemaphoreType.DMA((K,8*Z))],
         compiler_params=pltpu.CompilerParams(collective_id=cid,has_side_effects=True))(*shards)
+
+
+class Gathering:
+    def __init__(self, me, chunks, local, send, recv):
+        self.me, self.chunks = me, chunks
+        self.local, self.send, self.recv = local, send, recv
+        self.table, self.own = {}, []
+
+    def start(self, k, rel, to):
+        shard, full, cols, _ = self.chunks[k]
+        me = self.me
+        if isinstance(to, int):
+            target, landed = me.device(s=to), (to, 0, 0, 0)
+        else:
+            landed = list(rel)
+            landed["zyxc".index(to)] = 1
+            landed = tuple(landed)
+            target = me.device(**{"d" + to: 1})
+        slot = me.slot(*rel)
+        here = full.at[slot, :, cols]
+        at = ((landed[0] * 2 + landed[1]) * 2 + landed[2]) * 2 + landed[3]
+        copy = pltpu.make_async_remote_copy(
+            src_ref=shard.at[:, cols] if rel == (0, 0, 0, 0) else here,
+            dst_ref=here,
+            send_sem=self.send.at[k, at],
+            recv_sem=self.recv.at[k, at],
+            device_id=target,
+            device_id_type=MESH,
+        )
+        copy.start()
+        self.table[(k, landed)] = copy
+
+    def begin(self, k):
+        shard, full, cols, order = self.chunks[k]
+        copy = pltpu.make_async_copy(
+            shard.at[:, cols], full.at[self.me.slot(0, 0, 0, 0), :, cols], self.local.at[k]
+        )
+        copy.start()
+        self.own.append((k, copy))
+        for s in range(1, self.me.Z):
+            self.start(k, (0, 0, 0, 0), s)
+        for d in order:
+            self.start(k, (0, 0, 0, 0), d)
+
+    def step(self, k, stage):
+        order = self.chunks[k][3]
+        where = ["zyxc".index(d) for d in order]
+        for s in range(1 if stage == 0 else 0, self.me.Z):
+            for bits in range(1 << max(stage - 1, 0)):
+                rel = [s, 0, 0, 0]
+                for i in range(stage - 1):
+                    rel[where[i]] = bits >> i & 1
+                if stage:
+                    rel[where[stage - 1]] = 1
+                rel = tuple(rel)
+                self.table[(k, rel)].wait_recv()
+                for d in order[stage:]:
+                    self.start(k, rel, d)
+        if stage == 3:
+            for at, copy in self.own:
+                if at == k:
+                    copy.wait()
+
+    def finish(self):
+        for copy in self.table.values():
+            copy.wait_send()
+
+
+def forward_kernel(sizes, *refs):
+    batches, rows, kv_heads, group, used = sizes
+    (first_s, out_s, gate_s, up_s, down_s, x_ref, place_ref, freq_ref) = refs[:8]
+    (first_w, out_w, gate_w, up_w, down_w, q_out, kv_out, o_out, log_out) = refs[8:17]
+    (mixed_out, h2_out, hidden_out, slope_out, silu_out, bias_out, cos_out, sin_out) = refs[17:25]
+    (raw_a, raw_b, w_a, w_b, normed, queries, kv_all, attended, logs, mixed, h2) = refs[25:36]
+    (hidden, slope, silu, bias, cos_t, sin_t, gains) = refs[36:43]
+    (local, send, recv, kv_send, kv_recv, load_sem, store_sem) = refs[43:]
+    me = Place()
+    greet(me)
+    whole = slice(None)
+    half = down_w.shape[2] // 2
+    comm = Gathering(
+        me,
+        (
+            (first_s, first_w, whole, "yxc"),
+            (out_s, out_w, whole, "xyc"),
+            (gate_s, gate_w, whole, "yxc"),
+            (up_s, up_w, whole, "xyc"),
+            (down_s, down_w, pl.ds(0, half), "yxc"),
+            (down_s, down_w, pl.ds(half, half), "xyc"),
+        ),
+        local,
+        send,
+        recv,
+    )
+    tokens, width = x_ref.shape
+    length = kv_all.shape[1]
+    stores = []
+
+    def store(i, src, dst):
+        copy = pltpu.make_async_copy(src, dst, store_sem.at[i])
+        copy.start()
+        stores.append(copy)
+
+    def over_rows(body, step=64):
+        def one(i, carry):
+            body(pl.ds(pl.multiple_of(i * step, step), step))
+            return carry
+
+        lax.fori_loop(0, tokens // step, one, 0)
+
+    def load(full, raw, col, size, i):
+        return pltpu.make_async_copy(
+            full.at[:, :, pl.ds(col, size)], raw.at[:, :, pl.ds(0, size)], load_sem.at[i]
+        )
+
+    def assemble(raw, flat, size):
+        n, r, _ = raw.shape
+        pair = 2 * r
+
+        def one(i, carry):
+            piece = raw[pl.ds(2 * i, 2), :, pl.ds(0, size)].astype(jnp.float32)
+            flat[pl.ds(pl.multiple_of(pair * i, 16), pair), pl.ds(0, size)] = piece.reshape(
+                pair, size
+            ).astype(jnp.bfloat16)
+            return carry
+
+        lax.fori_loop(0, n // 2, one, 0)
+
+    comm.begin(0)
+    comm.begin(1)
+
+    scale = HD**-0.5
+    lane = lax.broadcasted_iota(jnp.int32, (64, 128), 1)
+    second = lax.rem(lane, HD) >= HD // 2
+    is_value = lane >= HD
+
+    def tables(at):
+        angle = place_ref[at, :].astype(jnp.float32) * freq_ref[...]
+        c, s = jnp.cos(angle), jnp.sin(angle)
+        s = jnp.where(second, s, -s)
+        cos_t[0, at, :] = c * scale
+        sin_t[0, at, :] = s * scale
+        cos_t[1, at, :] = jnp.where(is_value, 1.0, c)
+        sin_t[1, at, :] = jnp.where(is_value, 0.0, s)
+
+    over_rows(tables)
+    first_row = lax.axis_index("fsdp") * rows
+
+    def masks(at):
+        token = at.start
+        inside = lax.rem(token, rows)
+        query = first_row + inside + lax.broadcasted_iota(jnp.int32, (64, length), 0)
+        key = lax.broadcasted_iota(jnp.int32, (64, length), 1)
+        start = query - place_ref[at, :]
+        allowed = (key <= query) & (key >= start)
+        bias[at, :] = jnp.where(allowed, 0.0, NEGATIVE)
+
+    over_rows(masks)
+    store(0, bias, bias_out)
+    store(1, cos_t, cos_out)
+    store(2, sin_t, sin_out)
+
+    comm.step(0, 0)
+    comm.begin(2)
+    comm.step(1, 0)
+    comm.step(0, 1)
+    comm.step(1, 1)
+    comm.step(0, 2)
+    comm.begin(3)
+    comm.step(1, 2)
+    comm.step(0, 3)
+
+    tile = raw_a.shape[2]
+    load(first_w, raw_a, used, 128, 0).start()
+    load(first_w, raw_b, 0, tile, 1).start()
+    load(first_w, raw_a, used, 128, 0).wait()
+    assemble(raw_a, w_a, 128)
+    gains[...] = w_a[:, :128].astype(jnp.float32).T[:8]
+    load(first_w, raw_a, used - tile, tile, 0).start()
+
+    def norm_one(at):
+        x = x_ref[at, :].astype(jnp.float32)
+        inverse = lax.rsqrt(jnp.mean(x * x, -1, keepdims=True) + EPSILON)
+        normed[at, :] = (x * inverse * gains[0:1, :]).astype(jnp.bfloat16)
+
+    over_rows(norm_one)
+
+    def turn(flat, kind, put, step=128):
+        def body(at):
+            u = plain_dot(normed[at, :], flat[...])
+            for j in range(tile // 128):
+                piece = u[:, j * 128 : (j + 1) * 128]
+                piece = piece * cos_t[kind, at, :] + swap_halves(piece) * sin_t[kind, at, :]
+                put(at, j, piece.astype(jnp.bfloat16))
+
+        over_rows(body, step)
+
+    slot = (me.x * 2 + me.c) * rows
+
+    def put_pair(at, j, piece):
+        token = at.start
+        b = token // rows
+        row = pl.multiple_of(slot + lax.rem(token, rows), 128)
+        kv_all[b, pl.ds(row, 128), j * 128 : (j + 1) * 128] = piece
+
+    load(first_w, raw_a, used - tile, tile, 0).wait()
+    assemble(raw_a, w_a, tile)
+    turn(w_a, 1, put_pair)
+
+    def share(i, dx, to):
+        row = (lax.rem(me.x + dx, 2) * 2 + me.c) * rows
+        block = kv_all.at[:, pl.ds(pl.multiple_of(row, 256), rows), :]
+        copy = pltpu.make_async_remote_copy(
+            src_ref=block,
+            dst_ref=block,
+            send_sem=kv_send.at[i],
+            recv_sem=kv_recv.at[i],
+            device_id=me.device(**{"d" + to: 1}),
+            device_id_type=MESH,
+        )
+        copy.start()
+        return copy
+
+    to_x = share(0, 0, "x")
+    to_c = share(1, 0, "c")
+    for j in range(queries.shape[1] // tile):
+        raw, flat = ((raw_b, w_b), (raw_a, w_a))[j % 2]
+        if (j + 1) * tile < queries.shape[1]:
+            load(first_w, (raw_a, raw_b)[j % 2], (j + 1) * tile, tile, j % 2).start()
+        load(first_w, raw, j * tile, tile, 1 - j % 2).wait()
+        assemble(raw, flat, tile)
+
+        def put_query(at, i, piece, j=j):
+            queries[at, j * tile + i * 128 : j * tile + (i + 1) * 128] = piece
+
+        turn(flat, 0, put_query)
+    store(3, queries, q_out)
+    comm.step(2, 0)
+    comm.step(1, 3)
+    comm.begin(4)
+    comm.step(3, 0)
+    comm.step(2, 1)
+    to_x.wait_recv()
+    to_far = share(2, 1, "c")
+    to_c.wait_recv()
+    to_far.wait_recv()
+    store(4, kv_all, kv_out)
+
+    lanes = lax.broadcasted_iota(jnp.int32, (rows, 128), 1)
+    sides_mask = lane_masks(rows)
+
+    def head(i, carry):
+        b = i // kv_heads
+        h = lax.rem(i, kv_heads)
+        at = pl.ds(pl.multiple_of(b * rows, 256), rows)
+        kv = kv_all[b, :, pl.ds(pl.multiple_of(h * 128, 128), 128)]
+        sides = (kv, swapped(kv))
+        shift = bias[at, :]
+        log_piece = jnp.zeros((rows, 128), jnp.float32)
+        for pair in range(group // 2):
+            cols = pl.ds(pl.multiple_of(h * group * HD + pair * 128, 128), 128)
+            q = queries[at, cols]
+            found = []
+            for side in range(2):
+                scores = dot_t(q * sides_mask[side], sides[side]) + shift
+                top = jnp.max(scores, -1, keepdims=True)
+                powers = jnp.exp(scores - top)
+                total = jnp.sum(powers, -1, keepdims=True)
+                probs = (powers * (1.0 / total)).astype(jnp.bfloat16)
+                found.append(plain_dot(probs, sides[1 - side]))
+                log_piece = jnp.where(
+                    lanes == pair * 2 + side, top + jnp.log(total), log_piece
+                )
+            attended[at, cols] = jnp.where(lanes < HD, found[0], found[1]).astype(jnp.bfloat16)
+        logs[at, pl.ds(pl.multiple_of(h * 128, 128), 128)] = log_piece
+        return carry
+
+    count = batches * kv_heads
+    pumps = [(3, 1), (2, 2), (4, 0), (3, 2)]
+    done = 0
+    for i in range(5):
+        upto = count * (i + 1) // 5
+        lax.fori_loop(done, upto, head, 0)
+        done = upto
+        if i == 0:
+            comm.begin(5)
+        if i < len(pumps):
+            comm.step(*pumps[i])
+    store(5, attended, o_out)
+    store(6, logs, log_out)
+
+    steps = width // tile
+    load(out_w, raw_a, 0, tile, 0).start()
+    for j in range(steps):
+        raw, flat = ((raw_a, w_a), (raw_b, w_b))[j % 2]
+        if j + 1 < steps:
+            load(out_w, (raw_b, raw_a)[j % 2], (j + 1) * tile, tile, 1 - j % 2).start()
+        load(out_w, raw, j * tile, tile, j % 2).wait()
+        assemble(raw, flat, tile)
+
+        def add_in(at, flat=flat, j=j):
+            cols = slice(j * tile, (j + 1) * tile)
+            mixed[at, cols] = x_ref[at, cols].astype(jnp.float32) + plain_dot(
+                attended[at, :], flat[...]
+            )
+
+        over_rows(add_in, 128)
+
+    def norm_two(at):
+        y = mixed[at, :]
+        inverse = lax.rsqrt(jnp.mean(y * y, -1, keepdims=True) + EPSILON)
+        h2[at, :] = (y * inverse * gains[1:2, :]).astype(jnp.bfloat16)
+
+    over_rows(norm_two)
+    store(7, mixed, mixed_out)
+    store(8, h2, h2_out)
+
+    comm.step(5, 0)
+    comm.step(4, 1)
+    comm.step(2, 3)
+    comm.step(3, 3)
+
+    wide = 512
+    features = hidden.shape[1]
+    pumps = {1: (5, 1), 3: (4, 2), 5: (5, 2)}
+    load(gate_w, raw_a, 0, wide, 0).start()
+    load(up_w, raw_b, 0, wide, 1).start()
+    for j in range(features // wide):
+        load(gate_w, raw_a, j * wide, wide, 0).wait()
+        assemble(raw_a, w_a, wide)
+        load(up_w, raw_b, j * wide, wide, 1).wait()
+        assemble(raw_b, w_b, wide)
+        if (j + 1) * wide < features:
+            load(gate_w, raw_a, (j + 1) * wide, wide, 0).start()
+            load(up_w, raw_b, (j + 1) * wide, wide, 1).start()
+
+        def units(at, j=j):
+            cols = slice(j * wide, (j + 1) * wide)
+            g = plain_dot(h2[at, :], w_a[:, :wide])
+            u = plain_dot(h2[at, :], w_b[:, :wide])
+            sig = jax.nn.sigmoid(g)
+            soft = g * sig
+            hidden[at, cols] = (soft * u).astype(jnp.bfloat16)
+            silu[at, cols] = soft.astype(jnp.bfloat16)
+            slope[at, cols] = (u * (sig * (1.0 + g * (1.0 - sig)))).astype(jnp.bfloat16)
+
+        over_rows(units, 128)
+        if j in pumps:
+            comm.step(*pumps[j])
+    store(9, hidden, hidden_out)
+    store(10, silu, silu_out)
+    store(11, slope, slope_out)
+    comm.step(4, 3)
+    comm.step(5, 3)
+    for copy in (to_x, to_c, to_far):
+        copy.wait_send()
+    comm.finish()
+    for copy in stores:
+        copy.wait()
+
+
+def forward(shards, x, places, kv_heads, group, batches):
+    first_s, out_s, gate_s, up_s, down_s = shards
+    n = lax.axis_size("dp") * lax.axis_size("fsdp")
+    Z = lax.axis_size("dp") // 2
+    tokens, width = x.shape
+    rows = tokens // batches
+    length = rows * lax.axis_size("fsdp")
+    key_wide = kv_heads * 128
+    query_wide = kv_heads * group * HD
+    used = query_wide + key_wide
+    features = gate_s.shape[1]
+    r = first_s.shape[0]
+    freqs = ROPE_BASE ** (-jnp.arange(HD // 2).astype(jnp.float32) / (HD // 2))
+    freqs = jnp.tile(freqs, 4)[None]
+    bf, f32 = jnp.bfloat16, jnp.float32
+    shape = jax.ShapeDtypeStruct
+    outs = [shape((n,) + s.shape, s.dtype) for s in shards] + [
+        shape((tokens, query_wide), bf),
+        shape((batches, length, key_wide), bf),
+        shape((tokens, query_wide), bf),
+        shape((tokens, key_wide), f32),
+        shape((tokens, width), f32),
+        shape((tokens, width), bf),
+        shape((tokens, features), bf),
+        shape((tokens, features), bf),
+        shape((tokens, features), bf),
+        shape((tokens, length), f32),
+        shape((2, tokens, 128), f32),
+        shape((2, tokens, 128), f32),
+    ]
+    vmem = pltpu.VMEM
+    scratch = [
+        vmem((n, r, key_wide), bf),
+        vmem((n, r, key_wide), bf),
+        vmem((width, key_wide), bf),
+        vmem((width, key_wide), bf),
+        vmem((tokens, width), bf),
+        vmem((tokens, query_wide), bf),
+        vmem((batches, length, key_wide), bf),
+        vmem((tokens, query_wide), bf),
+        vmem((tokens, key_wide), f32),
+        vmem((tokens, width), f32),
+        vmem((tokens, width), bf),
+        vmem((tokens, features), bf),
+        vmem((tokens, features), bf),
+        vmem((tokens, features), bf),
+        vmem((tokens, length), f32),
+        vmem((2, tokens, 128), f32),
+        vmem((2, tokens, 128), f32),
+        vmem((8, width), f32),
+        pltpu.SemaphoreType.DMA((6,)),
+        pltpu.SemaphoreType.DMA((6, 8 * Z)),
+        pltpu.SemaphoreType.DMA((6, 8 * Z)),
+        pltpu.SemaphoreType.DMA((3,)),
+        pltpu.SemaphoreType.DMA((3,)),
+        pltpu.SemaphoreType.DMA((2,)),
+        pltpu.SemaphoreType.DMA((12,)),
+    ]
+    any_space = pl.BlockSpec(memory_space=pl.ANY)
+    in_vmem = pl.BlockSpec(memory_space=pltpu.VMEM)
+    return pl.pallas_call(
+        functools.partial(forward_kernel, (batches, rows, kv_heads, group, used)),
+        out_shape=outs,
+        in_specs=[any_space] * 5 + [in_vmem] * 3,
+        out_specs=[any_space] * len(outs),
+        scratch_shapes=scratch,
+        compiler_params=pltpu.CompilerParams(
+            collective_id=1, has_side_effects=True, vmem_limit_bytes=63 * 2**20
+        ),
+        cost_estimate=pl.CostEstimate(
+            flops=2 * tokens * width * (used + width + 2 * features),
+            bytes_accessed=4 * n * r * (used + width + 3 * features),
+            transcendentals=tokens * features,
+        ),
+    )(*shards, x, places, freqs)
 
 
 def tile_of(N):
@@ -399,6 +835,75 @@
     return full.astype(jnp.bfloat16)
 
 
+def rotary_pairs(places, tokens, score_scale):
+    cos_table, sin_table = rope_tables(places.reshape(tokens))
+    ones, zeros = jnp.ones((tokens, HD), jnp.float32), jnp.zeros((tokens, HD), jnp.float32)
+    cos_pair = jnp.concatenate([cos_table, cos_table], -1)
+    sin_pair = jnp.concatenate([-sin_table, sin_table], -1)
+    cos_tables = jnp.stack(
+        [
+            jnp.concatenate([cos_pair, cos_pair], -1) * score_scale,
+            jnp.concatenate([cos_pair, ones], -1),
+        ]
+    )
+    sin_tables = jnp.stack(
+        [
+            jnp.concatenate([sin_pair, sin_pair], -1) * score_scale,
+            jnp.concatenate([sin_pair, zeros], -1),
+        ]
+    )
+    return cos_tables, sin_tables
+
+
+def forward_plain(shards, x, places, kv_heads, group, batches):
+    tokens = x.shape[0]
+    rows = tokens // batches
+    length = rows * lax.axis_size("fsdp")
+    query_features = kv_heads * group * HD
+    used = query_features + kv_heads * 128
+    fulls = gather(shards, ("yxc", "xyc", "yxc", "xyc", "yxc"), 1, 5)
+    first_pack, out_full, gate_full, up_full, _ = (f.reshape(-1, f.shape[-1]) for f in fulls)
+    gains = first_pack[:, used : used + 2].astype(jnp.float32).T
+    query_index = lax.axis_index("fsdp") * rows + jnp.arange(rows, dtype=jnp.int32)
+    key_index = jnp.arange(length, dtype=jnp.int32)
+    x_float = x.astype(jnp.float32)
+    cos_tables, sin_tables = rotary_pairs(places, tokens, HD**-0.5)
+    doc_start = query_index[None, :] - places.reshape(batches, rows)
+    allowed = (key_index[None, None, :] <= query_index[None, :, None]) & (
+        key_index[None, None, :] >= doc_start[:, :, None]
+    )
+    bias = jnp.where(allowed, 0.0, NEGATIVE)
+    attn_inverse = lax.rsqrt(jnp.mean(x_float * x_float, -1, keepdims=True) + EPSILON)
+    normed = (x_float * attn_inverse * gains[0]).astype(jnp.bfloat16)
+    projected = project(normed, first_pack[:, :used], cos_tables, sin_tables, kv_heads * 128)
+    both_rows = projected[:, query_features:].reshape(batches, rows, -1)
+    both_all = lax.all_gather(both_rows, "fsdp", axis=1, tiled=True)
+    attended, logs = attend(projected, both_all, bias, kv_heads, group)
+    mixed = x_float + plain_dot(attended, out_full)
+    mlp_inverse = lax.rsqrt(jnp.mean(mixed * mixed, -1, keepdims=True) + EPSILON)
+    normed_mlp = (mixed * mlp_inverse * gains[1]).astype(jnp.bfloat16)
+    gate_pre = plain_dot(normed_mlp, gate_full)
+    up_proj = plain_dot(normed_mlp, up_full)
+    gate_sig = jax.nn.sigmoid(gate_pre)
+    silu = gate_pre * gate_sig
+    slope = up_proj * gate_sig * (1.0 + gate_pre * (1.0 - gate_sig))
+    low = jnp.bfloat16
+    return list(fulls) + [
+        projected[:, :query_features],
+        both_all,
+        attended,
+        logs,
+        mixed,
+        normed_mlp,
+        (silu * up_proj).astype(low),
+        slope.astype(low),
+        silu.astype(low),
+        bias.reshape(tokens, length),
+        cos_tables,
+        sin_tables,
+    ]
+
+
 def on_device(
     inputs,
     positions,
@@ -420,11 +925,7 @@
     kv_heads = key_features // HD
     group = query_features // key_features
     tokens = batches * rows
-    length = rows * lax.axis_size("fsdp")
-    first_row = lax.axis_index("fsdp") * rows
-    query_index = first_row + jnp.arange(rows, dtype=jnp.int32)
-    key_index = jnp.arange(length, dtype=jnp.int32)
-    score_scale = HD ** (-0.5)
+    used = query_features + 2 * key_features
 
     extras = jnp.zeros((shard, 128), jnp.bfloat16)
     extras = extras.at[:, 0].set(attn_gain).at[:, 1].set(mlp_gain)
@@ -432,64 +933,33 @@
         [key_matrix.reshape(shard, kv_heads, HD), value_matrix.reshape(shard, kv_heads, HD)], -1
     )
     first_shard = jnp.concatenate([w_query, pairs.reshape(shard, -1), extras], axis=1)
-    fulls = gather(
-        (first_shard, w_out, w_gate, w_up, w_down), ("yxc", "xyc", "yxc", "xyc", "yxc"), 1, 5
+    shards = (first_shard, w_out, w_gate, w_up, w_down)
+    x_low = inputs.reshape(tokens, width)
+    x_float = x_low.astype(jnp.float32)
+    fits = shard % 8 == 0 and lax.axis_size("fsdp") == 4 and rows % 256 == 0
+    saved = (forward if fits else forward_plain)(
+        shards, x_low, positions.reshape(tokens, 1), kv_heads, group, batches
     )
     first_pack, out_full, gate_full, up_full, down_full = (
-        f.reshape(-1, f.shape[-1]) for f in fulls
-    )
-    used = query_features + 2 * key_features
+        f.reshape(-1, f.shape[-1]) for f in saved[:5]
+    )
+    queries, both_all, attended, logs, mixed, normed_mlp = saved[5:11]
+    hidden, slope, silu, bias, cos_tables, sin_tables = saved[11:]
     projection = first_pack[:, :used]
     gains = first_pack[:, used : used + 2].astype(jnp.float32).T
-
-    x_float = inputs.reshape(tokens, width).astype(jnp.float32)
-    places = positions.reshape(batches, rows)
-    cos_table, sin_table = rope_tables(places.reshape(tokens))
-    ones, zeros = jnp.ones((tokens, HD), jnp.float32), jnp.zeros((tokens, HD), jnp.float32)
-    cos_pair = jnp.concatenate([cos_table, cos_table], -1)
-    sin_pair = jnp.concatenate([-sin_table, sin_table], -1)
-    cos_tables = jnp.stack(
-        [
-            jnp.concatenate([cos_pair, cos_pair], -1) * score_scale,
-            jnp.concatenate([cos_pair, ones], -1),
-        ]
-    )
-    sin_tables = jnp.stack(
-        [
-            jnp.concatenate([sin_pair, sin_pair], -1) * score_scale,
-            jnp.concatenate([sin_pair, zeros], -1),
-        ]
-    )
-    doc_start = query_index[None, :] - places
-    allowed = (key_index[None, None, :] <= query_index[None, :, None]) & (
-        key_index[None, None, :] >= doc_start[:, :, None]
-    )
-    bias = jnp.where(allowed, 0.0, NEGATIVE)
-    attn_inverse = lax.rsqrt(jnp.mean(x_float * x_float, -1, keepdims=True) + EPSILON)
     attn_gain_f = gains[0]
     mlp_gain_f = gains[1]
+    attn_inverse = lax.rsqrt(jnp.mean(x_float * x_float, -1, keepdims=True) + EPSILON)
     normed = (x_float * attn_inverse * attn_gain_f).astype(jnp.bfloat16)
-    projected = project(normed, projection, cos_tables, sin_tables, 2 * key_features)
-    both_rows = projected[:, query_features:].reshape(batches, rows, -1)
-    both_all = lax.all_gather(both_rows, "fsdp", axis=1, tiled=True)
-    attended, logs = attend(projected, both_all, bias, kv_heads, group)
-
-    mixed = x_float + plain_dot(attended, out_full)
     mlp_inverse = lax.rsqrt(jnp.mean(mixed * mixed, -1, keepdims=True) + EPSILON)
-    normed_mlp = (mixed * mlp_inverse * mlp_gain_f).astype(jnp.bfloat16)
-    gate_pre = plain_dot(normed_mlp, gate_full)
-    up_proj = plain_dot(normed_mlp, up_full)
-    gate_sig = jax.nn.sigmoid(gate_pre)
-    hidden = (gate_pre * gate_sig * up_proj).astype(jnp.bfloat16)
     output = (mixed + plain_dot(hidden, down_full)).astype(jnp.bfloat16)
 
     cot_low = cotangent.reshape(tokens, width)
     cot_float = cot_low.astype(jnp.float32)
     grad_down = half_of(left_dot(hidden, cot_low))
     grad_hidden = right_dot(cot_low, down_full)
-    sig_slope = gate_sig * (1.0 + gate_pre * (1.0 - gate_sig))
-    grad_gate_pre = (grad_hidden * up_proj * sig_slope).astype(jnp.bfloat16)
-    grad_up_pre = (grad_hidden * gate_pre * gate_sig).astype(jnp.bfloat16)
+    grad_gate_pre = (grad_hidden * slope.astype(jnp.float32)).astype(jnp.bfloat16)
+    grad_up_pre = (grad_hidden * silu.astype(jnp.float32)).astype(jnp.bfloat16)
     grad_gate = half_of(left_dot(normed_mlp, grad_gate_pre))
     grad_up = half_of(left_dot(normed_mlp, grad_up_pre))
     grad_normed_mlp = right_dot(grad_gate_pre, gate_full) + right_dot(grad_up_pre, up_full)
@@ -499,7 +969,14 @@
     grad_out = half_of(left_dot(attended, grad_mixed_low))
     grad_attended = right_dot(grad_mixed_low, out_full).astype(jnp.bfloat16)
     grad_query_pre, portions = attend_back(
-        projected, grad_attended, both_all, bias, logs, cos_tables, sin_tables, group
+        queries,
+        grad_attended,
+        both_all,
+        bias.reshape(batches, rows, -1),
+        logs,
+        cos_tables,
+        sin_tables,
+        group,
     )
     sums = lax.psum_scatter(portions, "fsdp", scatter_dimension=1, tiled=True)
     sums = sums.astype(jnp.float32).reshape(tokens, kv_heads, 128)

time: 654 us -> 632 us (0.966)
  the two profiles are of different devices: /device:TPU:0 before, /device:TPU:20 now
where the time goes in v4:
time: 632 us; the launch traced here: 622 us
  Pallas kernels  459 us (73%)
  matrix products  98.7 us (16%)
  local copies, waits for them, and re-layouts  27.6 us (4%)
  other arithmetic  21.5 us (3%)
  between operations  14.9 us (2%)
    pallas_call x1, Pallas kernels, scatter(): pl.pallas_call(functools.partial(scatter_kernel, Z, orders, ahead, dims_)...  223 us
    pallas_call x1, Pallas kernels, forward(): pl.pallas_call(functools.partial(forward_kernel, (batches, rows, kv_heads...  199 us
    dot_general x5, matrix products, right_dot(): lax.dot_general(left, right, (((1,), (1,)), ((), ())), preferred_element_...  46.1 us
    dot_general x5, matrix products, left_dot(): lax.dot_general(left, right, (((0,), (0,)), ((), ())), preferred_element_...  41.7 us
    pallas_call x1, Pallas kernels, attend_back(): pl.pallas_call(functools.partial(attend_back_kernel, group), grid=(batche...  37.1 us
  transfers between devices with their start and end apart: 1, of which 0 were waited for; matrix products, arithmetic and copies ran while one was open for 8% of the time, Pallas kernels for 0%

profile of v4, /device:TPU:20, one launch (start us, length us, event | category | flops | bytes accessed | tf_op | source)
XLA Modules:
  0.0 622.0 jit_solution(6182591470870706357)
XLA Ops:
  7.2 0.0 reduce-scatter.2.cloned.1.call-start
  7.2 0.6 compare_reduce_fusion.1
  7.9 0.6 compare_reduce_fusion
  8.5 1.3 fusion.22
  9.8 0.1 copy.29
  9.9 1.3 fusion.23
  11.2 0.1 copy.30
  11.3 0.9 reshape.193
  12.2 0.9 reshape.192
  13.1 0.1 pad_maximum_fusion.5
  13.2 1.5 copy.31.refs_6_
  14.7 0.6 broadcast_in_dim_tile.3.refs_7_
  15.3 0.1 scatter.9
  15.5 1.6 pad_maximum_fusion.4.refs_0_
  17.0 199.0 %shard_map.203 = (bf16[32,40,2048]{2,1,0:T(8,128)(2,1)}, bf16[32,40,1280]{2,1,0:T(8,128)(2,1)}, bf16[32,40,3584]{2,1,0:T(8,128)(2,1)}, bf16[32,40,3584]{2,1,0:T(...) custom-call(bf16[40,2048]{1,0:T(8,128)(2,1)} %pad_maximum_fusion.4.r, ...), custom_call_target="tpu_custom_call" | custom-call | flops 13589544960 | bytes 71434240 | tf_op jit(solution)/shard_map/pallas_call | solution.py:552
  216.0 0.0 copy-start.8
  216.0 1.1 slice_convert_fusion
  217.2 0.2 copy.49
  217.4 2.0 multiply_reduce_fusion.3
  219.5 11.1 %fusion.32 = f32[3584,512]{0,1:T(8,128)} fusion(bf16[3584,1280]{1,0:T(8,128)(2,1)} %bitcast.106, bf16[512,1280]{1,0:T(8,128)(2,1)S(1)} %bitcast.94), kind=kOutput, calls=%fused_computation.73 | convolution fusion | flops 4697620480 | bytes 17825792 | tf_op jit(solution)/shard_map/dot_general | solution.py:35
  230.6 12.4 %fusion.29 = f32[512,1280]{1,0:T(8,128)} fusion(bf16[1280,3584]{1,0:T(8,128)(2,1)} %bitcast.109, f32[3584,512]{0,1:T(8,128)} %fusion.32, bf16[512,3584]{1,0:T(8,128)(2,1)S(1)} %copy-done.18), kind=kOutput, calls=%fused_computation.71 | convolution fusion | flops 4703125504 | bytes 22806528 | tf_op jit(solution)/shard_map/dot_general | solution.py:35
  243.0 13.5 %multiply_reduce_fusion = (bf16[1280]{0:T(1024)(128)(2,1)}, f32[512]{0:T(512)S(1)}, f32[512,1280]{1,0:T(8,128)S(1)}) fusion(f32[512,1280]{1,0:T(8,128)S(1)} %copy-done.4, f32[512]{0:T(512)S(1)} %add_rsqrt_fusion, f32[1280]{0:T(1024)S(1)} %get-tuple-element.114, f32[512,1280]{1,0:T(8,128)} %fusion.29, bf16[1280,3584]{1,0:T(8,128)(2,1)} %bitcast.108, ...), kind=kOutput, calls=%fused_computation.30 | convolution fusion | flops 4707711488 | bytes 28061184 | tf_op jit(solution)/shard_map/dot_general | solution.py:35
  256.5 0.8 multiply_add_fusion
  257.3 1.4 copy-done.16
  258.7 1.9 convolution_convert_fusion.5.do_ref
  260.7 37.1 %shard_map.204 = (bf16[512,1280]{1,0:T(8,128)(2,1)S(1)}, bf16[2,1024,640]{2,1,0:T(8,128)(2,1)}) custom-call(bf16[512,1280]{1,0:T(8,128)(2,1)S(1)} %copy-done, bf16[512,1280]{1,0:T(8,128)(2,1)S(1)} %convolution_convert_fusion.5.do_ref, bf16[2,1024,640]{2,1,0:T(8,128)(2,1)} %get-tuple-element.69.kv_ref, f32[2,256,1024]{2,1,0:T(8,128)} %bitcast.92, ...), custom_call_target="tpu_custom_call" | custom-call | tf_op jit(solution)/shard_map/pallas_call | solution.py:810
  297.8 0.0 reduce-scatter.2.cloned.1.call-update
  297.8 1.6 multiply_reduce_fusion.1
  299.5 0.6 copy.48
  300.1 5.8 convolution_convert_fusion.3
  305.9 0.1 copy.37
  306.0 0.1 copy.34
  306.2 0.2 mul.166
  306.3 1.5 copy.35
  307.9 13.3 %convolution_convert_fusion.1 = bf16[1280,3584]{1,0:T(8,128)(2,1)} fusion(bf16[512,1280]{1,0:T(8,128)(2,1)} %get-tuple-element.76, f32[3584,512]{0,1:T(8,128)} %fusion.32, bf16[512,3584]{1,0:T(8,128)(2,1)} %get-tuple-element.62), kind=kOutput, calls=%fused_computation.1 | convolution fusion | flops 4707713024 | bytes 21495808 | tf_op jit(solution)/shard_map/dot_general | solution.py:29
  321.2 10.8 %convolution_convert_fusion = bf16[1280,3584]{1,0:T(8,128)(2,1)} fusion(bf16[512,1280]{1,0:T(8,128)(2,1)S(1)} %copy-done.19, f32[3584,512]{0,1:T(8,128)} %fusion.32, bf16[512,3584]{1,0:T(8,128)(2,1)S(1)} %copy-done.17), kind=kOutput, calls=%fused_computation | convolution fusion | flops 4707713024 | bytes 21495808 | tf_op jit(solution)/shard_map/dot_general | solution.py:29
  332.1 10.9 %fusion.6 = bf16[512,1280]{1,0:T(8,128)(2,1)} fusion(f32[512,1280]{1,0:T(8,128)S(1)} %copy-done.5, bf16[512,3584]{1,0:T(8,128)(2,1)} %get-tuple-element.60, bf16[3584,1280]{1,0:T(8,128)(2,1)} %bitcast.107), kind=kOutput, calls=%fused_computation.19 | convolution fusion | flops 4698931200 | bytes 16777216 | tf_op jit(solution)/shard_map/dot_general | solution.py:25
  342.9 7.3 %convolution_convert_fusion.2 = bf16[3584,1280]{1,0:T(8,128)(2,1)} fusion(bf16[512,3584]{1,0:T(8,128)(2,1)S(1)} %copy-done.20, bf16[512,1280]{1,0:T(8,128)(2,1)S(1)} %bitcast.95), kind=kOutput, calls=%fused_computation.2 | convolution fusion | flops 4702208000 | bytes 14155776 | tf_op jit(solution)/shard_map/dot_general | solution.py:29
  350.3 3.0 copy.36
  353.3 2.3 reshape.208
  355.6 0.1 slice.93
  355.7 0.2 maximum_multiply_fusion
  355.9 1.5 copy.38
  357.4 2.0 fusion.19
  359.4 0.1 copy-done.6
  359.5 7.2 %fusion.15 = (bf16[1280]{0:T(1024)(128)(2,1)S(1)}, f32[512]{0:T(512)S(1)}, f32[512,1280]{1,0:T(8,128)}) fusion(f32[512]{0:T(512)S(1)} %bitcast.103, bf16[2,1,256,1280]{3,2,1,0:T(8,128)(2,1)S(1)} %copy-done.6, f32[1280]{0:T(1024)S(1)} %get-tuple-element.113, bf16[1280,2048]{1,0:T(8,128)(2,1)} %bitcast.102, bf16[512,640]{1,0:T(8,128)(2,1)S(1)} %fusion.19, ...), kind=kOutput, calls=%fused_computation.29 | convolution fusion | flops 2525100288 | bytes 10825216 | tf_op jit(solution)/shard_map/dot_general | solution.py:35
  366.7 0.2 copy.46
  367.0 0.1 pad.10.clone
  367.0 5.0 fusion.17
  372.1 1.6 copy.39
  373.7 4.5 convolution_convert_fusion.4
  378.1 3.1 pad_maximum_fusion.refs_4_
  381.2 223.2 %shard_map.205 = (f32[112,1280]{1,0:T(8,128)}, f32[40,3584]{1,0:T(8,128)}, f32[40,3584]{1,0:T(8,128)}, f32[40,1280]{1,0:T(8,128)}, f32[40,2048]{1,0:T(8,128)}) custom-call(bf16[4,2,2,2,112,1280]{5,4,3,2,1,0:T(8,128)(2,1)} %bitcast.87, bf16[4,2,2,2,40,3584]{5,4,3,2,1,0:T(8,128)(2,1)} %bitcast.85, bf16[4,2,2,2,40,3584]{5,4,3,2,1,0:T(8,128)(2,1)} %bitcast.86, ...), custom_call_target="tpu_custom_call" | custom-call | tf_op jit(solution)/shard_map/pallas_call | solution.py:657
  604.4 1.6 slice_reduce_fusion.2
  606.0 1.6 slice.84
  607.6 0.9 slice.85
  608.5 0.2 reshape.214
  608.7 0.6 slice_reduce_fusion
  609.3 0.7 reshape_squeeze.6
  610.0 0.7 reshape_squeeze.7
  610.7 1.6 copy.57
  612.3 0.8 copy.58
  613.1 0.8 copy.59
  614.0 0.8 copy.60
  (54 shorter events, 0.3 us)
Async XLA Ops:
  7.2 343.1 %reduce-scatter.2.cloned.1.call-start = ((), (), s32[]{:S(2)}) async-start(), calls=%async_computation.1 | async-start | bytes 3276800 | tf_op jit(solution)/shard_map/reduce_scatter | solution.py:981
  216.0 3.4 copy-start.8
  219.4 11.1 %copy-start.18 = (bf16[512,3584]{1,0:T(8,128)(2,1)S(1)}, bf16[512,3584]{1,0:T(8,128)(2,1)}, u32[]{:S(2)}) copy-start(bf16[512,3584]{1,0:T(8,128)(2,1)} %get-tuple-element.62) | copy-start | bytes 11010052
  230.5 12.4 %copy-start.4 = (f32[512,1280]{1,0:T(8,128)S(1)}, f32[512,1280]{1,0:T(8,128)}, u32[]{:S(2)}) copy-start(f32[512,1280]{1,0:T(8,128)} %get-tuple-element.59) | copy-start | bytes 7864324
  256.5 2.3 copy-start.16
  257.3 3.3 copy-start.3
  258.7 1.9 copy-start
  258.7 1.9 copy-start.1
  258.7 1.9 copy-start.2
  305.9 1.9 copy-start.15
  307.9 13.3 %copy-start.17 = (bf16[512,3584]{1,0:T(8,128)(2,1)S(1)}, bf16[512,3584]{1,0:T(8,128)(2,1)}, u32[]{:S(2)}) copy-start(bf16[512,3584]{1,0:T(8,128)(2,1)} %get-tuple-element.64) | copy-start | bytes 11010052
  307.9 13.3 %copy-start.19 = (bf16[512,1280]{1,0:T(8,128)(2,1)S(1)}, bf16[512,1280]{1,0:T(8,128)(2,1)}, u32[]{:S(2)}) copy-start(bf16[512,1280]{1,0:T(8,128)(2,1)} %get-tuple-element.76) | copy-start | bytes 3932164
  321.2 10.9 %copy-start.5 = (f32[512,1280]{1,0:T(8,128)S(1)}, f32[512,1280]{1,0:T(8,128)}, u32[]{:S(2)}) copy-start(f32[512,1280]{1,0:T(8,128)} %get-tuple-element.59) | copy-start | bytes 7864324
  332.0 10.9 %copy-start.9 = (bf16[2,1,256,1280]{3,2,1,0:T(8,128)(2,1)S(1)}, bf16[2,1,256,1280]{3,2,1,0:T(8,128)(2,1)}, u32[]{:S(2)}) copy-start(bf16[2,1,256,1280]{3,2,1,0:T(8,128)(2,1)} %param.18) | copy-start | bytes 3932164
  332.0 10.9 %copy-start.20 = (bf16[512,3584]{1,0:T(8,128)(2,1)S(1)}, bf16[512,3584]{1,0:T(8,128)(2,1)}, u32[]{:S(2)}) copy-start(bf16[512,3584]{1,0:T(8,128)(2,1)} %get-tuple-element.60) | copy-start | bytes 11010052
  355.7 1.7 copy-start.7
  357.4 2.1 copy-start.6
  357.4 2.1 copy-start.14
  359.4 7.3 %copy-start.10 = (bf16[512,640]{1,0:T(8,128)(2,1)}, bf16[512,640]{1,0:T(8,128)(2,1)S(1)}, u32[]{:S(2)}) copy-start(bf16[512,640]{1,0:T(8,128)(2,1)S(1)} %fusion.19) | copy-start | bytes 1966084
  604.4 7.9 %copy-start.13 = (f32[40,3584]{1,0:T(8,128)S(1)}, f32[40,3584]{1,0:T(8,128)}, u32[]{:S(2)}) copy-start(f32[40,3584]{1,0:T(8,128)} %get-tuple-element.142) | copy-start | bytes 1720324
  604.4 8.7 %copy-start.12 = (f32[40,3584]{1,0:T(8,128)S(1)}, f32[40,3584]{1,0:T(8,128)}, u32[]{:S(2)}) copy-start(f32[40,3584]{1,0:T(8,128)} %get-tuple-element.143) | copy-start | bytes 1720324
  604.4 9.5 %copy-start.11 = (f32[112,1280]{1,0:T(8,128)S(1)}, f32[112,1280]{1,0:T(8,128)}, u32[]{:S(2)}) copy-start(f32[112,1280]{1,0:T(8,128)} %get-tuple-element.144) | copy-start | bytes 1720324
Sparse Core Ops, SparseCore 0:
  297.9 46.7 reduce-scatter.1

commit v5 on v4

--- a/solution.py
+++ b/solution.py
@@ -283,7 +283,7 @@
         key = lax.broadcasted_iota(jnp.int32, (64, length), 1)
         start = query - place_ref[at, :]
         allowed = (key <= query) & (key >= start)
-        bias[at, :] = jnp.where(allowed, 0.0, NEGATIVE)
+        bias[at, :] = jnp.where(allowed, 0.0, NEGATIVE).astype(jnp.bfloat16)
 
     over_rows(masks)
     store(0, bias, bias_out)
@@ -376,6 +376,7 @@
     to_far.wait_recv()
     store(4, kv_all, kv_out)
 
+    logs[...] = jnp.zeros_like(logs)
     lanes = lax.broadcasted_iota(jnp.int32, (rows, 128), 1)
     sides_mask = lane_masks(rows)
 
@@ -385,8 +386,8 @@
         at = pl.ds(pl.multiple_of(b * rows, 256), rows)
         kv = kv_all[b, :, pl.ds(pl.multiple_of(h * 128, 128), 128)]
         sides = (kv, swapped(kv))
-        shift = bias[at, :]
-        log_piece = jnp.zeros((rows, 128), jnp.float32)
+        shift = bias[at, :].astype(jnp.float32)
+        log_piece = logs[at, :]
         for pair in range(group // 2):
             cols = pl.ds(pl.multiple_of(h * group * HD + pair * 128, 128), 128)
             q = queries[at, cols]
@@ -399,10 +400,10 @@
                 probs = (powers * (1.0 / total)).astype(jnp.bfloat16)
                 found.append(plain_dot(probs, sides[1 - side]))
                 log_piece = jnp.where(
-                    lanes == pair * 2 + side, top + jnp.log(total), log_piece
+                    lanes == h * group + pair * 2 + side, top + jnp.log(total), log_piece
                 )
             attended[at, cols] = jnp.where(lanes < HD, found[0], found[1]).astype(jnp.bfloat16)
-        logs[at, pl.ds(pl.multiple_of(h * 128, 128), 128)] = log_piece
+        logs[at, :] = log_piece
         return carry
 
     count = batches * kv_heads
@@ -509,13 +510,13 @@
         shape((tokens, query_wide), bf),
         shape((batches, length, key_wide), bf),
         shape((tokens, query_wide), bf),
-        shape((tokens, key_wide), f32),
+        shape((tokens, 128), f32),
         shape((tokens, width), f32),
         shape((tokens, width), bf),
         shape((tokens, features), bf),
         shape((tokens, features), bf),
         shape((tokens, features), bf),
-        shape((tokens, length), f32),
+        shape((tokens, length), bf),
         shape((2, tokens, 128), f32),
         shape((2, tokens, 128), f32),
     ]
@@ -529,13 +530,13 @@
         vmem((tokens, query_wide), bf),
         vmem((batches, length, key_wide), bf),
         vmem((tokens, query_wide), bf),
-        vmem((tokens, key_wide), f32),
+        vmem((tokens, 128), f32),
         vmem((tokens, width), f32),
         vmem((tokens, width), bf),
         vmem((tokens, features), bf),
         vmem((tokens, features), bf),
         vmem((tokens, features), bf),
-        vmem((tokens, length), f32),
+        vmem((tokens, length), bf),
         vmem((2, tokens, 128), f32),
         vmem((2, tokens, 128), f32),
         vmem((8, width), f32),
@@ -831,6 +832,857 @@
     )(projected, grad_attended, both_all, bias, logs, cos_tables, sin_tables)
 
 
+class Scattering:
+    def __init__(self, me, chunks, send, recv, free):
+        self.me, self.chunks = me, chunks
+        self.send, self.recv, self.free = send, recv, free
+        self.copies = {}
+        self.friends = [me.device(s=s) for s in range(1, me.Z)]
+        self.friends += [me.device(dy=1), me.device(dx=1), me.device(dc=1)]
+
+    def ship(self, k, name, index, src, dst, target):
+        copy = pltpu.make_async_remote_copy(
+            src_ref=src,
+            dst_ref=dst,
+            send_sem=self.send.at[k, index],
+            recv_sem=self.recv.at[k, index],
+            device_id=target,
+            device_id_type=MESH,
+        )
+        copy.start()
+        self.copies[(k, name)] = copy
+
+    def add(self, dst, src, wide):
+        depth = dst.shape[0]
+        t = tile_of(wide)
+        count = wide // t
+
+        def body(i, carry):
+            at = i // count
+            cols = pl.ds(pl.multiple_of(lax.rem(i, count) * t, 128), t)
+            dst[at, :, cols] = dst[at, :, cols] + src[at, :, cols]
+            return carry
+
+        lax.fori_loop(0, depth * count, body, 0)
+
+    def buffers(self, k):
+        own, one, two, last, wide = self.chunks[k][:5]
+        cols = pl.ds(0, wide)
+        return own, one, two, last, wide, cols
+
+    def begin(self, k):
+        own, one, two, last, wide, cols = self.buffers(k)
+        order = self.chunks[k][5]
+        for b in (1, 0):
+            self.ship(
+                k,
+                ("1", b),
+                b,
+                own.at[1, b, :, :, cols],
+                one.at[b, :, :, cols],
+                self.me.device(**{"d" + order[0]: 1}),
+            )
+
+    def first(self, k):
+        own, one, two, last, wide, cols = self.buffers(k)
+        order = self.chunks[k][5]
+        for b in (1, 0):
+            self.copies[(k, ("1", b))].wait_recv()
+            self.add(own.at[0, b], one.at[b], wide)
+            if b == 1:
+                self.ship(
+                    k,
+                    "2",
+                    2,
+                    own.at[0, 1, :, :, cols],
+                    two.at[:, :, cols],
+                    self.me.device(**{"d" + order[1]: 1}),
+                )
+
+    def second(self, k):
+        own, one, two, last, wide, cols = self.buffers(k)
+        me = self.me
+        self.copies[(k, "2")].wait_recv()
+        self.add(own.at[0, 0], two, wide)
+        for s in range(1, me.Z):
+            self.ship(
+                k,
+                ("z", s),
+                2 + s,
+                own.at[0, 0, lax.rem(me.z + s, me.Z), :, cols],
+                last.at[s - 1, :, cols],
+                me.device(s=s),
+            )
+
+    def third(self, k):
+        own, one, two, last, wide, cols = self.buffers(k)
+        me = self.me
+        _, out, base, group = self.chunks[k][5:]
+        for s in range(1, me.Z):
+            self.copies[(k, ("z", s))].wait_recv()
+        t = tile_of(wide)
+
+        def body(j, carry):
+            here = pl.ds(pl.multiple_of(j * t, 128), t)
+            there = pl.ds(pl.multiple_of(base + j * t, 128), t)
+            total = own[0, 0, me.z, :, here].astype(jnp.float32)
+            for s in range(1, me.Z):
+                total = total + last[s - 1, :, here].astype(jnp.float32)
+            out[:, there] = total
+            return carry
+
+        lax.fori_loop(0, wide // t, body, 0)
+        for (at, _), copy in self.copies.items():
+            if at == k:
+                copy.wait_send()
+        if group is not None:
+            for friend in self.friends:
+                pl.semaphore_signal(
+                    self.free.at[group], inc=1, device_id=friend, device_id_type=MESH
+                )
+
+    def reuse(self, group):
+        pl.semaphore_wait(self.free.at[group], len(self.friends))
+
+
+def backward_kernel(sizes, *refs):
+    batches, rows, kv_heads, group, used = sizes
+    (dy_ref, first_w, out_w, gate_w, up_w, down_w) = refs[:6]
+    (q_in, kv_in, log_in, mixed_in, hidden_in, slope_in, silu_in, bias_in, cos_in, sin_in) = refs[6:16]
+    (hid_t, h2_t, att_t, nor_t, x_in) = refs[16:21]
+    outs = refs[21:36]
+    (result_out, grad_out, g_first, g_out, g_gate, g_up, g_down) = outs[:7]
+    (hid_s, h2_s, att_s, nor_s, dy_p, gate_p, up_p, dm_p) = outs[7:]
+    pre_p, dy1_h = refs[36:38]
+    sc = list(refs[38:])
+    take = lambda n: [sc.pop(0) for _ in range(n)]
+    sets = [take(4) for _ in range(3)]
+    down_sets = [take(4) for _ in range(2)]
+    gain_set = take(4)
+    (lhs_d, lhs, lraw, rhs, acc, part, cot, low_t, queries, grads, pre) = take(11)
+    (kv_all, dkv, bias, logs, cos_t, sin_t, dkv_r, dkv_x) = take(8)
+    (raw_a, raw_b, w_a, w_b, wd, fac_a, fac_b, dgt, dut, gains, gsum, gcol) = take(12)
+    (send, recv, free, x_send, x_recv, t_send, t_recv, load_sem, lhs_sem, store_sem, own_sem, part_sem) = take(12)
+    me = Place()
+    greet(me)
+    tokens, width = cot.shape
+    length = kv_all.shape[1]
+    features = hidden_in.shape[1]
+    wide = dgt.shape[2]
+    tiles = features // wide
+    scale = HD**-0.5
+    sibling = me.device(dc=1)
+    f32, bf = jnp.float32, jnp.bfloat16
+    r = lhs.shape[0] // (4 * me.Z)
+    rd = lhs_d.shape[0] // me.Z
+    big = sets[0][0].shape[-1]
+    half = features // 2
+    d_wide = down_sets[0][0].shape[-1]
+    d_rest = width - 2 * d_wide
+    chunks = (
+        (*down_sets[0], d_wide, "xy", g_down, 0, 4),
+        (*down_sets[1], d_wide, "yx", g_down, d_wide, None),
+        (*sets[0], half, "xy", g_gate, 0, 0),
+        (*sets[1], half, "yx", g_gate, half, 1),
+        (*sets[2], half, "xy", g_up, 0, 2),
+        (*sets[0], half, "yx", g_up, half, 3),
+        (*sets[1], width, "xy", g_out, 0, None),
+        (*sets[2], pre.shape[1] - kv_heads * 128, "yx", g_first, 0, None),
+        (*sets[0], kv_heads * 128, "xy", g_first, pre.shape[1] - kv_heads * 128, None),
+        (*gain_set, 128, "yx", g_first, pre.shape[1], None),
+        (*down_sets[0], d_rest, "yx", g_down, 2 * d_wide, None),
+    )
+    D0, D1, G0, G1, U0, U1, O, Q, KV, GAIN, D2 = range(11)
+    comm = Scattering(me, chunks, send, recv, free)
+
+    def over_rows(body, step=64):
+        def one(i, carry):
+            body(pl.ds(pl.multiple_of(i * step, step), step))
+            return carry
+
+        lax.fori_loop(0, tokens // step, one, 0)
+
+    passes = []
+
+    def hand(i, src, dst):
+        copy = pltpu.make_async_remote_copy(
+            src_ref=src,
+            dst_ref=dst,
+            send_sem=x_send.at[i],
+            recv_sem=x_recv.at[i],
+            device_id=sibling,
+            device_id_type=MESH,
+        )
+        copy.start()
+        passes.append(copy)
+        return copy
+
+    other = lax.rem(me.c + 1, 2)
+    got_hid = hand(0, hid_t.at[:, :, :, other], hid_s)
+    got_dy = hand(1, dy_ref, dy_p.at[1])
+    got_h2 = hand(2, h2_t.at[:, :, :, other], h2_s)
+    got_att = hand(3, att_t.at[:, :, :, other], att_s)
+    got_nor = hand(4, nor_t.at[:, :, :, other], nor_s)
+
+    def fetch(i, src, dst):
+        copy = pltpu.make_async_copy(src, dst, load_sem.at[i])
+        copy.start()
+        return copy
+
+    stores = []
+
+    def store(i, src, dst):
+        copy = pltpu.make_async_copy(src, dst, store_sem.at[i])
+        copy.start()
+        stores.append(copy)
+        return copy
+
+    need_cot = fetch(0, dy_ref, cot)
+    own_dy = store(0, dy_ref, dy_p.at[0])
+    def block(ref, a, b, order, c=None):
+        rel = {order[0]: a, order[1]: b}
+        y = lax.rem(me.y + rel["y"], 2)
+        x = lax.rem(me.x + rel["x"], 2)
+        return ref.at[:, y, x] if c is None else ref.at[:, y, x, c]
+
+    def left_rows(own_t, sib_t, order):
+        for side, ref in ((0, own_t), (1, sib_t)):
+            loads = []
+            for i in range(4):
+                src = block(ref, i // 2, i % 2, order, me.c if side == 0 else None)
+                copy = pltpu.make_async_copy(src, lraw.at[i], lhs_sem.at[i])
+                copy.start()
+                loads.append(copy)
+            for copy in loads:
+                copy.wait()
+
+            def one(i, carry, side=side):
+                for j in range(me.Z // 2):
+                    piece = lraw[i, 2 * j : 2 * j + 2].astype(f32).reshape(2 * r, tokens)
+                    at = pl.multiple_of((i * me.Z + 2 * j) * r, 16)
+                    lhs[pl.ds(at, 2 * r), side * tokens : (side + 1) * tokens] = piece.astype(bf)
+                return carry
+
+            lax.fori_loop(0, 4, one, 0)
+
+    def product_down(k, base):
+        order = chunks[k][5]
+        for i in (3, 2, 1, 0):
+            loads = []
+            for side, ref in ((0, hid_t), (1, hid_s)):
+                src = block(ref, i // 2, i % 2, order, me.c if side == 0 else None)
+                for z in range(me.Z):
+                    copy = pltpu.make_async_copy(
+                        src.at[z],
+                        lhs_d.at[pl.ds(z * rd, rd), pl.ds(side * tokens, tokens)],
+                        lhs_sem.at[side * me.Z + z],
+                    )
+                    copy.start()
+                    loads.append(copy)
+            for copy in loads:
+                copy.wait()
+            product(k, dy_p, base, lhs_d, rd, (i,))
+        comm.begin(k)
+
+    def product(k, pair, base, left, depth, blocks=(0, 1, 2, 3)):
+        own, wide_k = chunks[k][0], chunks[k][4]
+        t = rhs.shape[3] if wide_k % rhs.shape[3] == 0 else 128
+        count = wide_k // t
+        span = len(blocks)
+
+        def tile(j, slot):
+            cols = pl.ds(pl.multiple_of(base + j * t, 128), t)
+            return [
+                pltpu.make_async_copy(
+                    pair.at[side, :, cols],
+                    rhs.at[slot, side, :, pl.ds(0, t)],
+                    own_sem.at[slot, side],
+                )
+                for side in range(2)
+            ]
+
+        for copy in tile(0, 0):
+            copy.start()
+
+        def body(j, carry):
+            slot = lax.rem(j, 2)
+
+            @pl.when(j + 1 < count)
+            def _():
+                for copy in tile(j + 1, lax.rem(j + 1, 2)):
+                    copy.start()
+
+            for copy in tile(j, slot):
+                copy.wait()
+            cols = pl.ds(pl.multiple_of(j * t, 128), t)
+            total = plain_dot(left[:, :tokens], rhs[slot, 0, :, :t]) + plain_dot(
+                left[:, tokens:], rhs[slot, 1, :, :t]
+            )
+            total = total.reshape(span, me.Z, depth, t).astype(bf)
+            for q, at in enumerate(blocks):
+                own[at // 2, at % 2, :, :, cols] = total[q]
+            return carry
+
+        lax.fori_loop(0, count, body, 0)
+
+    def load3(i, full, raw, col, size):
+        return pltpu.make_async_copy(
+            full.at[:, :, pl.ds(col, size)], raw.at[:, :, pl.ds(0, size)], load_sem.at[i]
+        )
+
+    def assemble(raw, flat, size):
+        n, depth, _ = raw.shape
+        pair = 2 * depth
+
+        def one(i, carry):
+            piece = raw[pl.ds(2 * i, 2), :, pl.ds(0, size)].astype(f32)
+            flat[pl.ds(pl.multiple_of(pair * i, 16), pair), pl.ds(0, size)] = piece.reshape(
+                pair, size
+            ).astype(bf)
+            return carry
+
+        lax.fori_loop(0, n // 2, one, 0)
+
+    def tile_loads(j):
+        at = pl.ds(j * wide, wide)
+        return [
+            pltpu.make_async_copy(down_w.at[at, :], wd, load_sem.at[2]),
+            pltpu.make_async_copy(slope_in.at[:, at], fac_a, load_sem.at[3]),
+            pltpu.make_async_copy(silu_in.at[:, at], fac_b, load_sem.at[4]),
+        ]
+
+    gather_tiles = lambda j: [
+        load3(5, gate_w, raw_a, j * wide, wide),
+        load3(6, up_w, raw_b, j * wide, wide),
+    ]
+    head_pack = load3(7, first_w, raw_a, used, 128)
+    head_pack.start()
+    head_pack.wait()
+    assemble(raw_a, w_a, 128)
+    gains[...] = w_a[:, :128].astype(f32).T[:8]
+    for copy in tile_loads(0) + gather_tiles(0):
+        copy.start()
+    need_cot.wait()
+    own_dy.wait()
+    tile_sends = [None] * tiles
+    for j in range(tiles):
+        slot = j % 2
+        for copy in tile_loads(j):
+            copy.wait()
+        if j >= 2:
+            for copy in tile_sends[j - 2]:
+                copy.wait()
+        for copy in gather_tiles(j):
+            copy.wait()
+        assemble(raw_a, w_a, wide)
+        assemble(raw_b, w_b, wide)
+        if j + 1 < tiles:
+            for copy in gather_tiles(j + 1):
+                copy.start()
+
+        def units(at, slot=slot, j=j):
+            grad_hidden = dot_t(cot[at, :], wd[...])
+            dg = (grad_hidden * fac_a[at, :].astype(f32)).astype(bf)
+            du = (grad_hidden * fac_b[at, :].astype(f32)).astype(bf)
+            dgt[slot, at, :] = dg
+            dut[slot, at, :] = du
+            piece = dot_t(dg, w_a[:, :wide]) + dot_t(du, w_b[:, :wide])
+            acc[at, :] = piece if j == 0 else acc[at, :] + piece
+
+        over_rows(units, 256)
+        if j + 1 < tiles:
+            for copy in tile_loads(j + 1):
+                copy.start()
+        cols = pl.ds(j * wide, wide)
+        sends = []
+        for i, (src, dst) in enumerate(((dgt, gate_p), (dut, up_p))):
+            here = pltpu.make_async_copy(
+                src.at[slot], dst.at[0, :, cols], store_sem.at[1 + 2 * slot + i]
+            )
+            there = pltpu.make_async_remote_copy(
+                src_ref=src.at[slot],
+                dst_ref=dst.at[1, :, cols],
+                send_sem=t_send.at[2 * j + i],
+                recv_sem=t_recv.at[2 * j + i],
+                device_id=sibling,
+                device_id_type=MESH,
+            )
+            here.start()
+            there.start()
+            passes.append(there)
+            sends.append(here)
+        tile_sends[j] = [_Both(here, there) for here, there in zip(sends, passes[-2:])]
+        if j == 1:
+            got_hid.wait_recv()
+            got_dy.wait_recv()
+            product_down(D0, 0)
+        if j == 3:
+            product_down(D1, d_wide)
+    for j in (tiles - 2, tiles - 1):
+        for copy in tile_sends[j]:
+            copy.wait()
+    arrived = [p for p in passes[5:]]
+    for copy in arrived:
+        copy.wait_recv()
+    got_h2.wait_recv()
+    left_rows(h2_t, h2_s, "xy")
+    product(G0, gate_p, 0, lhs, r)
+    comm.begin(G0)
+    product(U0, up_p, 0, lhs, r)
+    comm.begin(U0)
+    comm.first(D0)
+    left_rows(h2_t, h2_s, "yx")
+    product(G1, gate_p, half, lhs, r)
+    comm.begin(G1)
+    comm.first(D1)
+
+    gsum[...] = jnp.zeros_like(gsum)
+
+    def stream(src, body):
+        def piece(i, slot):
+            at = pl.ds(pl.multiple_of(i * 64, 64), 64)
+            return pltpu.make_async_copy(src.at[at, :], part.at[slot], part_sem.at[slot])
+
+        piece(0, 0).start()
+
+        def one(i, carry):
+            slot = lax.rem(i, 2)
+
+            @pl.when(i + 1 < tokens // 64)
+            def _():
+                piece(i + 1, lax.rem(i + 1, 2)).start()
+
+            piece(i, slot).wait()
+            body(pl.ds(pl.multiple_of(i * 64, 64), 64), part[slot])
+            return carry
+
+        lax.fori_loop(0, tokens // 64, one, 0)
+
+    def norm_two(at, y):
+        inverse = lax.rsqrt(jnp.mean(y * y, -1, keepdims=True) + EPSILON)
+        grad = acc[at, :]
+        gsum[1:2, :] += jnp.sum(grad * (y * inverse), 0, keepdims=True)
+        e = grad * gains[1:2, :]
+        dy1 = cot[at, :].astype(f32) + inverse * (
+            e - y * (inverse * inverse) * jnp.mean(e * y, -1, keepdims=True)
+        )
+        acc[at, :] = dy1
+        low_t[at, :] = dy1.astype(bf)
+
+    stream(mixed_in, norm_two)
+    keep_dy1 = pltpu.make_async_copy(acc, dy1_h, part_sem.at[2])
+    keep_dy1.start()
+    own_low = store(5, low_t, dm_p.at[0])
+    got_low = hand(5, low_t, dm_p.at[1])
+
+    need_q = fetch(0, q_in, queries)
+    need_kv = fetch(1, kv_in, kv_all)
+    need = [
+        fetch(8, bias_in, bias),
+        fetch(9, log_in, logs),
+        fetch(10, cos_in, cos_t),
+        fetch(11, sin_in, sin_t),
+    ]
+    tile_w = raw_a.shape[2]
+    steps = width // tile_w
+    load3(5, out_w, raw_a, 0, tile_w).start()
+    for j in range(steps):
+        raw, flat = ((raw_a, w_a), (raw_b, w_b))[j % 2]
+        if j + 1 < steps:
+            load3(5 + (j + 1) % 2, out_w, (raw_b, raw_a)[j % 2], (j + 1) * tile_w, tile_w).start()
+        load3(5 + j % 2, out_w, raw, j * tile_w, tile_w).wait()
+        assemble(raw, flat, tile_w)
+
+    def back_out(at):
+        grads[at, :] = (
+            dot_t(low_t[at, :tile_w], w_a[...]) + dot_t(low_t[at, tile_w:], w_b[...])
+        ).astype(bf)
+
+    over_rows(back_out, 256)
+    comm.second(D0)
+    comm.first(G0)
+    comm.second(D1)
+
+    need_q.wait()
+    need_kv.wait()
+    for copy in need:
+        copy.wait()
+    lanes = lax.broadcasted_iota(jnp.int32, (rows, 128), 1)
+    sides_mask = lane_masks(rows)
+
+    def head(i, carry):
+        b = i // kv_heads
+        h = lax.rem(i, kv_heads)
+        at = pl.ds(pl.multiple_of(b * rows, 256), rows)
+        here = pl.ds(pl.multiple_of(h * 128, 128), 128)
+        kv = kv_all[b, :, here]
+        sides = (kv, swapped(kv))
+        shift = bias[at, :].astype(f32)
+        key_sum = jnp.zeros((128, length), f32)
+        value_sum = jnp.zeros((128, length), f32)
+        log_piece = logs[at, :]
+        for pair in range(group // 2):
+            cols = pl.ds(pl.multiple_of(h * group * HD + pair * 128, 128), 128)
+            q = queries[at, cols]
+            do = grads[at, cols]
+            found = []
+            for side in range(2):
+                q_half = q * sides_mask[side]
+                do_half = do * sides_mask[side]
+                head_at = pair * 2 + side
+                log_total = jnp.sum(
+                    jnp.where(lanes == h * group + head_at, log_piece, 0.0), -1, keepdims=True
+                )
+                probs = jnp.exp(dot_t(q_half, sides[side]) + shift - log_total)
+                grad_probs = dot_t(do_half, sides[1 - side])
+                row_dot = jnp.sum(probs * grad_probs, -1, keepdims=True)
+                grad_scores = (probs * (grad_probs - row_dot)).astype(bf)
+                found.append(plain_dot(grad_scores, sides[side]))
+                key_sum = key_sum + left_dot(q_half, grad_scores)
+                value_sum = value_sum + left_dot(do_half, probs.astype(bf))
+            dq = jnp.where(lanes < HD, found[0], found[1])
+            dq = dq * cos_t[0, at, :] - swap_halves(dq) * sin_t[0, at, :]
+            pre[at, cols] = dq.astype(bf)
+        both = jnp.concatenate(
+            [key_sum[:HD] + key_sum[HD:], value_sum[:HD] + value_sum[HD:]], 0
+        )
+        dkv[b, :, here] = both.T.astype(bf)
+        return carry
+
+    count = batches * kv_heads
+    lax.fori_loop(0, 2, head, 0)
+    own_low.wait()
+    got_low.wait_recv()
+    comm.first(U0)
+    comm.second(G0)
+    comm.third(D0)
+    lax.fori_loop(2, 4, head, 0)
+    comm.first(G1)
+    comm.third(D1)
+    comm.third(G0)
+    lax.fori_loop(4, 6, head, 0)
+    comm.reuse(4)
+    product_down(D2, 2 * d_wide)
+    comm.reuse(0)
+    left_rows(h2_t, h2_s, "yx")
+    product(U1, up_p, half, lhs, r)
+    comm.begin(U1)
+    comm.second(U0)
+    comm.second(G1)
+    lax.fori_loop(6, 8, head, 0)
+    comm.third(U0)
+    comm.third(G1)
+    lax.fori_loop(8, count, head, 0)
+    comm.first(D2)
+
+    def portion(dx, c):
+        row = (lax.rem(me.x + dx, 2) * 2 + c) * rows
+        return pl.ds(pl.multiple_of(row, 256), rows)
+
+    to_c = [hand(6 + dx, dkv.at[:, portion(dx, other), :], dkv_r.at[dx]) for dx in (1, 0)]
+    comm.reuse(1)
+    got_att.wait_recv()
+    left_rows(att_t, att_s, "xy")
+    product(O, dm_p, 0, lhs, r)
+    comm.begin(O)
+
+    def gather_portion(dx):
+        place = portion(dx, me.c)
+        for b in range(batches):
+
+            def body(j, carry, b=b):
+                at = pl.ds(pl.multiple_of(j * 64, 64), 64)
+                there = pl.ds(pl.multiple_of(place.start + j * 64, 64), 64)
+                total = dkv_r[dx, b, at, :].astype(f32) + dkv[b, there, :].astype(f32)
+                dkv_r[dx, b, at, :] = total.astype(bf)
+                return carry
+
+            lax.fori_loop(0, rows // 64, body, 0)
+
+    to_c[0].wait_recv()
+    gather_portion(1)
+    to_x = pltpu.make_async_remote_copy(
+        src_ref=dkv_r.at[1],
+        dst_ref=dkv_x,
+        send_sem=x_send.at[8],
+        recv_sem=x_recv.at[8],
+        device_id=me.device(dx=1),
+        device_id_type=MESH,
+    )
+    to_x.start()
+    passes.append(to_x)
+    query_wide = pre.shape[1] - kv_heads * 128
+    own_q = store(6, pre.at[:, pl.ds(0, query_wide)], pre_p.at[0, :, pl.ds(0, query_wide)])
+    got_q = hand(9, pre.at[:, pl.ds(0, query_wide)], pre_p.at[1, :, pl.ds(0, query_wide)])
+    to_c[1].wait_recv()
+    gather_portion(0)
+    comm.first(U1)
+    comm.second(D2)
+    comm.reuse(2)
+    got_nor.wait_recv()
+    left_rows(nor_t, nor_s, "yx")
+    own_q.wait()
+    got_q.wait_recv()
+    product(Q, pre_p, 0, lhs, r)
+    comm.begin(Q)
+    comm.first(O)
+    comm.second(U1)
+    to_x.wait_recv()
+    for b in range(batches):
+
+        def merge(j, carry, b=b):
+            at = pl.ds(pl.multiple_of(j * 64, 64), 64)
+            token = pl.ds(pl.multiple_of(b * rows + j * 64, 64), 64)
+            for h in range(kv_heads):
+                cols = slice(h * 128, (h + 1) * 128)
+                total = dkv_r[0, b, at, cols].astype(f32) + dkv_x[b, at, cols].astype(f32)
+                total = total * cos_t[1, token, :] - swap_halves(total) * sin_t[1, token, :]
+                pre[token, query_wide + h * 128 : query_wide + (h + 1) * 128] = total.astype(bf)
+            return carry
+
+        lax.fori_loop(0, rows // 64, merge, 0)
+    rest = pl.ds(query_wide, kv_heads * 128)
+    own_kv = store(7, pre.at[:, rest], pre_p.at[0, :, rest])
+    got_kv = hand(10, pre.at[:, rest], pre_p.at[1, :, rest])
+
+    need_x = fetch(0, x_in, cot)
+    keep_dy1.wait()
+    steps = pre.shape[1] // tile_w
+    load3(5, first_w, raw_a, 0, tile_w).start()
+    for j in range(steps):
+        raw, flat = ((raw_a, w_a), (raw_b, w_b))[j % 2]
+        if j + 1 < steps:
+            load3(5 + (j + 1) % 2, first_w, (raw_b, raw_a)[j % 2], (j + 1) * tile_w, tile_w).start()
+        load3(5 + j % 2, first_w, raw, j * tile_w, tile_w).wait()
+        assemble(raw, flat, tile_w)
+
+        def back_in(at, j=j, flat=flat):
+            piece = dot_t(pre[at, j * tile_w : (j + 1) * tile_w], flat[...])
+            acc[at, :] = piece if j == 0 else acc[at, :] + piece
+
+        over_rows(back_in, 256)
+    comm.third(U1)
+    comm.third(D2)
+    comm.reuse(3)
+    own_kv.wait()
+    got_kv.wait_recv()
+    left_rows(nor_t, nor_s, "xy")
+    product(KV, pre_p, query_wide, lhs, r)
+    comm.begin(KV)
+    need_x.wait()
+
+    def norm_one(at, dy1):
+        x = cot[at, :].astype(f32)
+        inverse = lax.rsqrt(jnp.mean(x * x, -1, keepdims=True) + EPSILON)
+        grad = acc[at, :]
+        gsum[0:1, :] += jnp.sum(grad * (x * inverse), 0, keepdims=True)
+        e = grad * gains[0:1, :]
+        total = dy1 + inverse * (
+            e - x * (inverse * inverse) * jnp.mean(e * x, -1, keepdims=True)
+        )
+        queries[at, :] = total.astype(bf)
+
+    stream(dy1_h, norm_one)
+    store(8, queries, grad_out)
+    comm.first(Q)
+    comm.second(O)
+
+    gsib = gain_set[0]
+    columns = jnp.concatenate([gsum[...], jnp.zeros((120, width), f32)], 0).T
+    gcol[0] = columns.reshape(gcol.shape[1:]).astype(bf)
+    got_gain = hand(11, gcol.at[0], gcol.at[1])
+    comm.first(KV)
+    got_gain.wait_recv()
+    for a in range(2):
+        for b in range(2):
+            y = lax.rem(me.y + b, 2)
+            x = lax.rem(me.x + a, 2)
+            if chunks[GAIN][5] == "yx":
+                y, x = lax.rem(me.y + a, 2), lax.rem(me.x + b, 2)
+            for z in range(me.Z):
+                at = ((z * 2 + y) * 2 + x) * 2 + me.c
+                gsib[a, b, z] = gcol[0, at] + gcol[1, at]
+    comm.begin(GAIN)
+    comm.second(Q)
+
+    need_mixed = fetch(1, mixed_in, acc)
+    need_mixed.wait()
+    for j in range(tiles):
+        at = pl.ds(j * wide, wide)
+        wd_load = pltpu.make_async_copy(down_w.at[at, :], wd, load_sem.at[2])
+        hidden_load = pltpu.make_async_copy(hidden_in.at[:, at], fac_a, load_sem.at[3])
+        wd_load.start()
+        hidden_load.start()
+        wd_load.wait()
+        hidden_load.wait()
+
+        def add_down(at):
+            acc[at, :] = acc[at, :] + plain_dot(fac_a[at, :], wd[...])
+
+        over_rows(add_down, 256)
+        if j == 1:
+            comm.first(GAIN)
+            comm.third(O)
+        if j == 2:
+            comm.second(KV)
+        if j == 4:
+            comm.third(Q)
+            comm.second(GAIN)
+
+    def round_result(at):
+        low_t[at, :] = acc[at, :].astype(bf)
+
+    got_low.wait_send()
+    over_rows(round_result)
+    store(9, low_t, result_out)
+    comm.third(KV)
+    comm.third(GAIN)
+    for copy in passes:
+        if copy is not got_low and not any(copy is p for p in arrived):
+            copy.wait_send()
+    for copy in stores:
+        if not any(copy is p for p in (own_dy, own_low, own_q, own_kv)):
+            copy.wait()
+
+
+class _Both:
+    def __init__(self, here, there):
+        self.here, self.there = here, there
+
+    def wait(self):
+        self.here.wait()
+        self.there.wait_send()
+
+
+def backward(saved, transposed, dy, x, kv_heads, group, batches):
+    first_w, out_w, gate_w, up_w, down_w = saved[:5]
+    queries, both_all, _, logs, mixed, _ = saved[5:11]
+    hidden, slope, silu, bias, cos_tables, sin_tables = saved[11:]
+    tokens, width = x.shape
+    rows = tokens // batches
+    Z = lax.axis_size("dp") // 2
+    X = lax.axis_size("fsdp") // 2
+    n, r, first_wide = first_w.shape
+    rd = down_w.shape[1]
+    key_wide = kv_heads * 128
+    query_wide = kv_heads * group * HD
+    used = query_wide + key_wide
+    length = both_all.shape[1]
+    features = hidden.shape[1]
+    half = features // 2
+    d_wide = width * 2 // 5 // 256 * 256
+    wide, t = 512, 256
+    bf, f32 = jnp.bfloat16, jnp.float32
+    shape = jax.ShapeDtypeStruct
+    vmem, dma = pltpu.VMEM, pltpu.SemaphoreType.DMA
+
+    def four(depth, size):
+        return [
+            vmem((2, 2, Z, depth, size), bf),
+            vmem((2, Z, depth, size), bf),
+            vmem((Z, depth, size), bf),
+            vmem((Z - 1, depth, size), bf),
+        ]
+
+    outs = [
+        shape((tokens, width), bf),
+        shape((tokens, width), bf),
+        shape((r, first_wide), f32),
+        shape((r, width), f32),
+        shape((r, features), f32),
+        shape((r, features), f32),
+        shape((rd, width), f32),
+        shape((Z, 2, X, rd, tokens), bf),
+        shape((Z, 2, X, r, tokens), bf),
+        shape((Z, 2, X, r, tokens), bf),
+        shape((Z, 2, X, r, tokens), bf),
+        shape((2, tokens, width), bf),
+        shape((2, tokens, features), bf),
+        shape((2, tokens, features), bf),
+        shape((2, tokens, width), bf),
+        shape((2, tokens, used), bf),
+        shape((tokens, width), f32),
+    ]
+    any_space = pl.BlockSpec(memory_space=pl.ANY)
+    in_vmem = pl.BlockSpec(memory_space=pltpu.VMEM)
+    scratch = sum([four(r, half) for _ in range(3)], [])
+    scratch += four(rd, d_wide) + four(rd, d_wide) + four(r, 128)
+    scratch += [
+        vmem((Z * rd, 2 * tokens), bf),
+        vmem((4 * Z * r, 2 * tokens), bf),
+        vmem((4, Z, r, tokens), bf),
+        vmem((2, 2, tokens, t), bf),
+        vmem((tokens, width), f32),
+        vmem((2, 64, width), f32),
+        vmem((tokens, width), bf),
+        vmem((tokens, width), bf),
+        vmem((tokens, query_wide), bf),
+        vmem((tokens, query_wide), bf),
+        vmem((tokens, used), bf),
+        vmem((batches, length, key_wide), bf),
+        vmem((batches, length, key_wide), bf),
+        vmem((tokens, length), bias.dtype),
+        vmem((tokens, 128), f32),
+        vmem((2, tokens, 128), f32),
+        vmem((2, tokens, 128), f32),
+        vmem((2, batches, rows, key_wide), bf),
+        vmem((batches, rows, key_wide), bf),
+        vmem((n, r, key_wide), bf),
+        vmem((n, r, key_wide), bf),
+        vmem((width, key_wide), bf),
+        vmem((width, key_wide), bf),
+        vmem((wide, width), bf),
+        vmem((tokens, wide), bf),
+        vmem((tokens, wide), bf),
+        vmem((2, tokens, wide), bf),
+        vmem((2, tokens, wide), bf),
+        vmem((8, width), f32),
+        vmem((8, width), f32),
+        vmem((2, n, r, 128), bf),
+        dma((11, 2 + Z)),
+        dma((11, 2 + Z)),
+        pltpu.SemaphoreType.REGULAR((5,)),
+        dma((12,)),
+        dma((12,)),
+        dma((2 * (features // wide),)),
+        dma((2 * (features // wide),)),
+        dma((12,)),
+        dma((8 * Z,)),
+        dma((10,)),
+        dma((2, 2)),
+        dma((3,)),
+    ]
+    return pl.pallas_call(
+        functools.partial(backward_kernel, (batches, rows, kv_heads, group, used)),
+        out_shape=outs,
+        in_specs=[any_space] * 21,
+        out_specs=[any_space] * 2 + [in_vmem] * 5 + [any_space] * 10,
+        scratch_shapes=scratch,
+        compiler_params=pltpu.CompilerParams(
+            collective_id=2, has_side_effects=True, vmem_limit_bytes=63 * 2**20
+        ),
+    )(
+        dy,
+        first_w,
+        out_w,
+        gate_w,
+        up_w,
+        down_w.reshape(-1, width),
+        queries,
+        both_all,
+        logs,
+        mixed,
+        hidden,
+        slope,
+        silu,
+        bias,
+        cos_tables,
+        sin_tables,
+        *transposed,
+        x,
+    )
+
+
 def half_of(full):
     return full.astype(jnp.bfloat16)
 
@@ -904,6 +1756,81 @@
     ]
 
 
+def backward_plain(saved, cotangent, x_low, kv_heads, group, batches):
+    tokens, width = x_low.shape
+    rows = tokens // batches
+    key_features = kv_heads * HD
+    query_features = kv_heads * group * HD
+    used = query_features + 2 * key_features
+    x_float = x_low.astype(jnp.float32)
+    first_pack, out_full, gate_full, up_full, down_full = (
+        f.reshape(-1, f.shape[-1]) for f in saved[:5]
+    )
+    queries, both_all, attended, logs, mixed, normed_mlp = saved[5:11]
+    hidden, slope, silu, bias, cos_tables, sin_tables = saved[11:]
+    projection = first_pack[:, :used]
+    gains = first_pack[:, used : used + 2].astype(jnp.float32).T
+    attn_gain_f = gains[0]
+    mlp_gain_f = gains[1]
+    attn_inverse = lax.rsqrt(jnp.mean(x_float * x_float, -1, keepdims=True) + EPSILON)
+    normed = (x_float * attn_inverse * attn_gain_f).astype(jnp.bfloat16)
+    mlp_inverse = lax.rsqrt(jnp.mean(mixed * mixed, -1, keepdims=True) + EPSILON)
+    output = (mixed + plain_dot(hidden, down_full)).astype(jnp.bfloat16)
+
+    cot_low = cotangent
+    cot_float = cot_low.astype(jnp.float32)
+    grad_down = half_of(left_dot(hidden, cot_low))
+    grad_hidden = right_dot(cot_low, down_full)
+    grad_gate_pre = (grad_hidden * slope.astype(jnp.float32)).astype(jnp.bfloat16)
+    grad_up_pre = (grad_hidden * silu.astype(jnp.float32)).astype(jnp.bfloat16)
+    grad_gate = half_of(left_dot(normed_mlp, grad_gate_pre))
+    grad_up = half_of(left_dot(normed_mlp, grad_up_pre))
+    grad_normed_mlp = right_dot(grad_gate_pre, gate_full) + right_dot(grad_up_pre, up_full)
+    grad_mlp_gain = jnp.sum(grad_normed_mlp * mixed * mlp_inverse, 0)
+    grad_mixed = cot_float + norm_back(grad_normed_mlp * mlp_gain_f, mixed, mlp_inverse)
+    grad_mixed_low = grad_mixed.astype(jnp.bfloat16)
+    grad_out = half_of(left_dot(attended, grad_mixed_low))
+    grad_attended = right_dot(grad_mixed_low, out_full).astype(jnp.bfloat16)
+    grad_query_pre, portions = attend_back(
+        queries,
+        grad_attended,
+        both_all,
+        bias.reshape(batches, rows, -1),
+        logs,
+        cos_tables,
+        sin_tables,
+        group,
+    )
+    sums = lax.psum_scatter(portions, "fsdp", scatter_dimension=1, tiled=True)
+    sums = sums.astype(jnp.float32).reshape(tokens, kv_heads, 128)
+    turned = jnp.concatenate([sums[..., 32:64], sums[..., :32], sums[..., 64:]], -1)
+    grad_pair_pre = (sums * cos_tables[1][:, None] - turned * sin_tables[1][:, None]).astype(
+        jnp.bfloat16
+    )
+    grad_pre = jnp.concatenate(
+        [grad_query_pre, grad_pair_pre.reshape(tokens, 2 * key_features)], -1
+    )
+    grad_projection = left_dot(normed, grad_pre)
+    grad_normed = right_dot(grad_pre, projection)
+    grad_attn_gain = jnp.sum(grad_normed * x_float * attn_inverse, 0)
+    grad_input = grad_mixed + norm_back(grad_normed * attn_gain_f, x_float, attn_inverse)
+    gain_columns = jnp.stack([grad_attn_gain, grad_mlp_gain], -1)
+    gain_columns = jnp.pad(gain_columns, ((0, 0), (0, 126)))
+    grad_first = half_of(jnp.concatenate([grad_projection, gain_columns], 1))
+    grad_down, grad_gate, grad_up, grad_out, last = scatter(
+        (grad_down, grad_gate, grad_up, grad_out, grad_first), ("xy", "yx", "xy", "yx", "xy"), 2
+    )
+    return (
+        output,
+        grad_input.astype(jnp.bfloat16),
+        last,
+        grad_out,
+        grad_gate,
+        grad_up,
+        grad_down,
+    )
+
+
 def on_device(
     inputs,
     positions,
@@ -935,72 +1862,28 @@
     first_shard = jnp.concatenate([w_query, pairs.reshape(shard, -1), extras], axis=1)
     shards = (first_shard, w_out, w_gate, w_up, w_down)
     x_low = inputs.reshape(tokens, width)
-    x_float = x_low.astype(jnp.float32)
+    cot_low = cotangent.reshape(tokens, width)
     fits = shard % 8 == 0 and lax.axis_size("fsdp") == 4 and rows % 256 == 0
     saved = (forward if fits else forward_plain)(
         shards, x_low, positions.reshape(tokens, 1), kv_heads, group, batches
     )
-    first_pack, out_full, gate_full, up_full, down_full = (
-        f.reshape(-1, f.shape[-1]) for f in saved[:5]
-    )
-    queries, both_all, attended, logs, mixed, normed_mlp = saved[5:11]
-    hidden, slope, silu, bias, cos_tables, sin_tables = saved[11:]
-    projection = first_pack[:, :used]
-    gains = first_pack[:, used : used + 2].astype(jnp.float32).T
-    attn_gain_f = gains[0]
-    mlp_gain_f = gains[1]
-    attn_inverse = lax.rsqrt(jnp.mean(x_float * x_float, -1, keepdims=True) + EPSILON)
-    normed = (x_float * attn_inverse * attn_gain_f).astype(jnp.bfloat16)
-    mlp_inverse = lax.rsqrt(jnp.mean(mixed * mixed, -1, keepdims=True) + EPSILON)
-    output = (mixed + plain_dot(hidden, down_full)).astype(jnp.bfloat16)
-
-    cot_low = cotangent.reshape(tokens, width)
-    cot_float = cot_low.astype(jnp.float32)
-    grad_down = half_of(left_dot(hidden, cot_low))
-    grad_hidden = right_dot(cot_low, down_full)
-    grad_gate_pre = (grad_hidden * slope.astype(jnp.float32)).astype(jnp.bfloat16)
-    grad_up_pre = (grad_hidden * silu.astype(jnp.float32)).astype(jnp.bfloat16)
-    grad_gate = half_of(left_dot(normed_mlp, grad_gate_pre))
-    grad_up = half_of(left_dot(normed_mlp, grad_up_pre))
-    grad_normed_mlp = right_dot(grad_gate_pre, gate_full) + right_dot(grad_up_pre, up_full)
-    grad_mlp_gain = jnp.sum(grad_normed_mlp * mixed * mlp_inverse, 0)
-    grad_mixed = cot_float + norm_back(grad_normed_mlp * mlp_gain_f, mixed, mlp_inverse)
-    grad_mixed_low = grad_mixed.astype(jnp.bfloat16)
-    grad_out = half_of(left_dot(attended, grad_mixed_low))
-    grad_attended = right_dot(grad_mixed_low, out_full).astype(jnp.bfloat16)
-    grad_query_pre, portions = attend_back(
-        queries,
-        grad_attended,
-        both_all,
-        bias.reshape(batches, rows, -1),
-        logs,
-        cos_tables,
-        sin_tables,
-        group,
-    )
-    sums = lax.psum_scatter(portions, "fsdp", scatter_dimension=1, tiled=True)
-    sums = sums.astype(jnp.float32).reshape(tokens, kv_heads, 128)
-    turned = jnp.concatenate([sums[..., 32:64], sums[..., :32], sums[..., 64:]], -1)
-    grad_pair_pre = (sums * cos_tables[1][:, None] - turned * sin_tables[1][:, None]).astype(
-        jnp.bfloat16
-    )
-    grad_pre = jnp.concatenate(
-        [grad_query_pre, grad_pair_pre.reshape(tokens, 2 * key_features)], -1
-    )
-    grad_projection = left_dot(normed, grad_pre)
-    grad_normed = right_dot(grad_pre, projection)
-    grad_attn_gain = jnp.sum(grad_normed * x_float * attn_inverse, 0)
-    grad_input = grad_mixed + norm_back(grad_normed * attn_gain_f, x_float, attn_inverse)
-    gain_columns = jnp.stack([grad_attn_gain, grad_mlp_gain], -1)
-    gain_columns = jnp.pad(gain_columns, ((0, 0), (0, 126)))
-    grad_first = half_of(jnp.concatenate([grad_projection, gain_columns], 1))
-    grad_down, grad_gate, grad_up, grad_out, last = scatter(
-        (grad_down, grad_gate, grad_up, grad_out, grad_first), ("xy", "yx", "xy", "yx", "xy"), 2
-    )
+    if fits:
+        x_float = x_low.astype(jnp.float32)
+        attn_inverse = lax.rsqrt(jnp.mean(x_float * x_float, -1, keepdims=True) + EPSILON)
+        gain = saved[0].reshape(width, -1)[:, used].astype(jnp.float32)
+        normed = (x_float * attn_inverse * gain).astype(jnp.bfloat16)
+        by_place = (lax.axis_size("dp") // 2, 2, lax.axis_size("fsdp") // 2, 2, -1, tokens)
+        transposed = [
+            t.T.reshape(by_place) for t in (saved[11], saved[10], saved[7], normed)
+        ]
+        found = backward(saved, transposed, cot_low, x_low, kv_heads, group, batches)
+    else:
+        found = backward_plain(saved, cot_low, x_low, kv_heads, group, batches)
+    output, grad_input, last, grad_out, grad_gate, grad_up, grad_down = found[:7]
     last_pairs = last[:, query_features:used].reshape(shard, kv_heads, 2, HD)
     return (
         output.reshape(inputs.shape),
-        grad_input.astype(jnp.bfloat16).reshape(inputs.shape),
+        grad_input.reshape(inputs.shape),
         last[:, used],
         last[:, :query_features],
         last_pairs[:, :, 0].reshape(shard, key_features),

time: 632 us -> 629 us (level)
  the two profiles are of different devices: /device:TPU:20 before, /device:TPU:4 now
where the time goes in v5:
time: 629 us; the launch traced here: 617 us
  Pallas kernels  577 us (92%)
  local copies, waits for them, and re-layouts  29.6 us (5%)
  other arithmetic  8.95 us (1%)
    pallas_call x1, Pallas kernels, backward(): pl.pallas_call(functools.partial(backward_kernel, (batches, rows, kv_head...  371 us
    pallas_call x1, Pallas kernels, forward(): pl.pallas_call(functools.partial(forward_kernel, (batches, rows, kv_heads...  206 us

profile of v5, /device:TPU:4, one launch (start us, length us, event | category | flops | bytes accessed | tf_op | source)
XLA Modules:
  0.0 616.7 jit_solution(10931149247569807960)
XLA Ops:
  0.6 0.6 compare_reduce_fusion.1
  1.3 0.6 compare_reduce_fusion
  1.9 1.3 fusion.2
  3.2 1.3 fusion.1
  4.6 0.6 broadcast_in_dim_tile.3.refs_7_
  5.2 1.6 multiply_reduce_fusion
  6.8 0.1 copy.31
  6.9 0.1 copy.32
  7.0 0.1 scatter.9
  7.2 0.9 reshape.154
  8.0 0.9 reshape.155
  8.9 0.1 pad_maximum_fusion.1
  9.0 1.6 pad_maximum_fusion.refs_0_
  10.6 1.5 copy.33.refs_6_
  12.1 206.0 %shard_map.203 = (bf16[32,40,2048]{2,1,0:T(8,128)(2,1)}, bf16[32,40,1280]{2,1,0:T(8,128)(2,1)}, bf16[32,40,3584]{2,1,0:T(8,128)(2,1)}, bf16[32,40,3584]{2,1,0:T(...) custom-call(bf16[40,2048]{1,0:T(8,128)(2,1)} %pad_maximum_fusion.ref, ...), custom_call_target="tpu_custom_call" | custom-call | flops 13589544960 | bytes 71434240 | tf_op jit(solution)/shard_map/pallas_call | solution.py:553
  218.2 1.0 slice.57
  219.2 0.2 copy.41
  219.4 1.7 fusion
  221.1 0.0 copy-start.1
  221.1 1.5 copy.38
  222.6 2.4 copy.35
  225.0 0.0 copy-done.1
  225.0 1.5 copy.36
  226.5 5.9 copy.34
  232.4 370.8 %shard_map.204 = (bf16[512,1280]{1,0:T(8,128)(2,1)}, bf16[512,1280]{1,0:T(8,128)(2,1)}, f32[40,2048]{1,0:T(8,128)}, f32[40,1280]{1,0:T(8,128)}, f32[40,3584]{1,0...) custom-call(bf16[512,1280]{1,0:T(8,128)(2,1)} %bitcast.45, ...), custom_call_target="tpu_custom_call" | custom-call | tf_op jit(solution)/shard_map/pallas_call | solution.py:1655
  603.3 0.0 copy-start
  603.3 1.5 slice_reduce_fusion.2
  604.8 0.9 slice.53
  605.7 1.6 slice.52
  607.3 0.2 reshape.169
  607.5 0.6 slice_reduce_fusion
  608.1 0.7 reshape_squeeze.7
  608.8 0.7 reshape_squeeze.6
  609.5 0.0 copy-start.5
  609.5 0.0 copy-start.4
  609.5 2.5 copy.53
  612.0 0.0 copy-done
  612.0 0.0 copy-start.3
  612.0 0.0 copy-start.2
  612.0 1.1 copy.54
  613.1 0.0 copy-done.5
  613.1 0.7 copy.55
  613.8 0.0 copy-done.4
  613.8 0.8 copy.56
  614.6 0.0 copy-done.3
  614.6 0.8 copy.57
  615.4 0.0 copy-done.2
  615.4 0.8 copy.58
  (7 shorter events, 0.1 us)
Async XLA Ops:
  221.1 3.9 copy-start.1
  603.3 8.8 %copy-start = (bf16[512,1280]{1,0:T(8,128)(2,1)S(1)}, bf16[512,1280]{1,0:T(8,128)(2,1)}, u32[]{:S(2)}) copy-start(bf16[512,1280]{1,0:T(8,128)(2,1)} %get-tuple-element.77) | copy-start | bytes 3932164
  609.5 3.6 copy-start.5
  609.5 4.3 copy-start.4
  612.0 2.6 copy-start.3
  612.0 3.4 copy-start.2

commit v6 on v5

--- a/solution.py
+++ b/solution.py
@@ -201,9 +201,11 @@
     (first_s, out_s, gate_s, up_s, down_s, x_ref, place_ref, freq_ref) = refs[:8]
     (first_w, out_w, gate_w, up_w, down_w, q_out, kv_out, o_out, log_out) = refs[8:17]
     (mixed_out, h2_out, hidden_out, slope_out, silu_out, bias_out, cos_out, sin_out) = refs[17:25]
-    (raw_a, raw_b, w_a, w_b, normed, queries, kv_all, attended, logs, mixed, h2) = refs[25:36]
-    (hidden, slope, silu, bias, cos_t, sin_t, gains) = refs[36:43]
-    (local, send, recv, kv_send, kv_recv, load_sem, store_sem) = refs[43:]
+    (hid_turned, h2_turned, att_turned, nor_turned) = refs[25:29]
+    (raw_a, raw_b, w_a, w_b, normed, queries, kv_all, attended, logs, mixed, h2) = refs[29:40]
+    (hidden, slope, silu, bias, cos_t, sin_t, gains) = refs[40:47]
+    (hid_t, h2_t, att_t, nor_t) = refs[47:51]
+    (local, send, recv, kv_send, kv_recv, load_sem, store_sem) = refs[51:]
     me = Place()
     greet(me)
     whole = slice(None)
@@ -256,8 +258,14 @@
 
         lax.fori_loop(0, n // 2, one, 0)
 
+    def turn_rows(src, dst, base, size):
+        for i in range(size // 256):
+            at = slice(base + i * 256, base + (i + 1) * 256)
+            dst[at, :] = src[:, at].astype(jnp.float32).T.astype(jnp.bfloat16)
+
     comm.begin(0)
     comm.begin(1)
+    comm.begin(2)
 
     scale = HD**-0.5
     lane = lax.broadcasted_iota(jnp.int32, (64, 128), 1)
@@ -291,12 +299,16 @@
     store(2, sin_t, sin_out)
 
     comm.step(0, 0)
-    comm.begin(2)
+    comm.begin(3)
     comm.step(1, 0)
     comm.step(0, 1)
+    comm.begin(4)
+    comm.step(2, 0)
     comm.step(1, 1)
     comm.step(0, 2)
-    comm.begin(3)
+    comm.begin(5)
+    comm.step(3, 0)
+    comm.step(2, 1)
     comm.step(1, 2)
     comm.step(0, 3)
 
@@ -314,8 +326,9 @@
         normed[at, :] = (x * inverse * gains[0:1, :]).astype(jnp.bfloat16)
 
     over_rows(norm_one)
-
-    def turn(flat, kind, put, step=128):
+    comm.step(4, 0)
+
+    def turn(flat, kind, put, step=256):
         def body(at):
             u = plain_dot(normed[at, :], flat[...])
             for j in range(tile // 128):
@@ -330,8 +343,8 @@
     def put_pair(at, j, piece):
         token = at.start
         b = token // rows
-        row = pl.multiple_of(slot + lax.rem(token, rows), 128)
-        kv_all[b, pl.ds(row, 128), j * 128 : (j + 1) * 128] = piece
+        row = pl.multiple_of(slot + lax.rem(token, rows), 256)
+        kv_all[b, pl.ds(row, 256), j * 128 : (j + 1) * 128] = piece
 
     load(first_w, raw_a, used - tile, tile, 0).wait()
     assemble(raw_a, w_a, tile)
@@ -353,6 +366,7 @@
 
     to_x = share(0, 0, "x")
     to_c = share(1, 0, "c")
+    comm.step(3, 1)
     for j in range(queries.shape[1] // tile):
         raw, flat = ((raw_b, w_b), (raw_a, w_a))[j % 2]
         if (j + 1) * tile < queries.shape[1]:
@@ -364,12 +378,12 @@
             queries[at, j * tile + i * 128 : j * tile + (i + 1) * 128] = piece
 
         turn(flat, 0, put_query)
+        if j == 0:
+            comm.step(2, 2)
     store(3, queries, q_out)
-    comm.step(2, 0)
+    turn_rows(normed, nor_t, 0, width)
+    store(12, nor_t, nor_turned)
     comm.step(1, 3)
-    comm.begin(4)
-    comm.step(3, 0)
-    comm.step(2, 1)
     to_x.wait_recv()
     to_far = share(2, 1, "c")
     to_c.wait_recv()
@@ -407,16 +421,13 @@
         return carry
 
     count = batches * kv_heads
-    pumps = [(3, 1), (2, 2), (4, 0), (3, 2)]
+    pumps = [(5, 0), (4, 1), (3, 2), (2, 3), (5, 1), (4, 2)]
     done = 0
-    for i in range(5):
-        upto = count * (i + 1) // 5
+    for i in range(6):
+        upto = (2, 4, 6, 8, 9, 10)[i] * count // 10
         lax.fori_loop(done, upto, head, 0)
         done = upto
-        if i == 0:
-            comm.begin(5)
-        if i < len(pumps):
-            comm.step(*pumps[i])
+        comm.step(*pumps[i])
     store(5, attended, o_out)
     store(6, logs, log_out)
 
@@ -435,7 +446,7 @@
                 attended[at, :], flat[...]
             )
 
-        over_rows(add_in, 128)
+        over_rows(add_in, 256)
 
     def norm_two(at):
         y = mixed[at, :]
@@ -445,15 +456,15 @@
     over_rows(norm_two)
     store(7, mixed, mixed_out)
     store(8, h2, h2_out)
-
-    comm.step(5, 0)
-    comm.step(4, 1)
-    comm.step(2, 3)
+    turn_rows(attended, att_t, 0, attended.shape[1])
+    store(13, att_t, att_turned)
+    turn_rows(h2, h2_t, 0, width)
+    store(14, h2_t, h2_turned)
     comm.step(3, 3)
 
     wide = 512
     features = hidden.shape[1]
-    pumps = {1: (5, 1), 3: (4, 2), 5: (5, 2)}
+    pumps = {2: (5, 2), 5: (4, 3)}
     load(gate_w, raw_a, 0, wide, 0).start()
     load(up_w, raw_b, 0, wide, 1).start()
     for j in range(features // wide):
@@ -475,13 +486,14 @@
             silu[at, cols] = soft.astype(jnp.bfloat16)
             slope[at, cols] = (u * (sig * (1.0 + g * (1.0 - sig)))).astype(jnp.bfloat16)
 
-        over_rows(units, 128)
+        over_rows(units, 256)
+        turn_rows(hidden, hid_t, j * wide, wide)
         if j in pumps:
             comm.step(*pumps[j])
     store(9, hidden, hidden_out)
     store(10, silu, silu_out)
     store(11, slope, slope_out)
-    comm.step(4, 3)
+    store(15, hid_t, hid_turned)
     comm.step(5, 3)
     for copy in (to_x, to_c, to_far):
         copy.wait_send()
@@ -519,6 +531,10 @@
         shape((tokens, length), bf),
         shape((2, tokens, 128), f32),
         shape((2, tokens, 128), f32),
+        shape((features, tokens), bf),
+        shape((width, tokens), bf),
+        shape((query_wide, tokens), bf),
+        shape((width, tokens), bf),
     ]
     vmem = pltpu.VMEM
     scratch = [
@@ -540,13 +556,17 @@
         vmem((2, tokens, 128), f32),
         vmem((2, tokens, 128), f32),
         vmem((8, width), f32),
+        vmem((features, tokens), bf),
+        vmem((width, tokens), bf),
+        vmem((query_wide, tokens), bf),
+        vmem((width, tokens), bf),
         pltpu.SemaphoreType.DMA((6,)),
         pltpu.SemaphoreType.DMA((6, 8 * Z)),
         pltpu.SemaphoreType.DMA((6, 8 * Z)),
         pltpu.SemaphoreType.DMA((3,)),
         pltpu.SemaphoreType.DMA((3,)),
         pltpu.SemaphoreType.DMA((2,)),
-        pltpu.SemaphoreType.DMA((12,)),
+        pltpu.SemaphoreType.DMA((16,)),
     ]
     any_space = pl.BlockSpec(memory_space=pl.ANY)
     in_vmem = pl.BlockSpec(memory_space=pltpu.VMEM)
@@ -961,38 +981,40 @@
     gain_set = take(4)
     (lhs_d, lhs, lraw, rhs, acc, part, cot, low_t, queries, grads, pre) = take(11)
     (kv_all, dkv, bias, logs, cos_t, sin_t, dkv_r, dkv_x) = take(8)
-    (raw_a, raw_b, w_a, w_b, wd, fac_a, fac_b, dgt, dut, gains, gsum, gcol) = take(12)
+    (raw_a, w_a, wd, fac_a, fac_b, dgt, dut, gains, gsum, gcol) = take(10)
     (send, recv, free, x_send, x_recv, t_send, t_recv, load_sem, lhs_sem, store_sem, own_sem, part_sem) = take(12)
     me = Place()
     greet(me)
     tokens, width = cot.shape
     length = kv_all.shape[1]
     features = hidden_in.shape[1]
-    wide = dgt.shape[2]
+    wide = dgt.shape[1]
     tiles = features // wide
     scale = HD**-0.5
     sibling = me.device(dc=1)
     f32, bf = jnp.float32, jnp.bfloat16
     r = lhs.shape[0] // (4 * me.Z)
-    rd = lhs_d.shape[0] // me.Z
+    rd = lhs_d.shape[1] // me.Z
     big = sets[0][0].shape[-1]
     half = features // 2
+    key_wide = kv_heads * 128
+    query_wide = pre.shape[1] - key_wide
     d_wide = down_sets[0][0].shape[-1]
     d_rest = width - 2 * d_wide
     chunks = (
         (*down_sets[0], d_wide, "xy", g_down, 0, 4),
         (*down_sets[1], d_wide, "yx", g_down, d_wide, None),
         (*sets[0], half, "xy", g_gate, 0, 0),
-        (*sets[1], half, "yx", g_gate, half, 1),
-        (*sets[2], half, "xy", g_up, 0, 2),
+        (*sets[1], half, "yx", g_up, 0, 1),
+        (*sets[2], half, "xy", g_gate, half, 2),
         (*sets[0], half, "yx", g_up, half, 3),
         (*sets[1], width, "xy", g_out, 0, None),
-        (*sets[2], pre.shape[1] - kv_heads * 128, "yx", g_first, 0, None),
-        (*sets[0], kv_heads * 128, "xy", g_first, pre.shape[1] - kv_heads * 128, None),
-        (*gain_set, 128, "yx", g_first, pre.shape[1], None),
-        (*down_sets[0], d_rest, "yx", g_down, 2 * d_wide, None),
-    )
-    D0, D1, G0, G1, U0, U1, O, Q, KV, GAIN, D2 = range(11)
+        (*sets[2], query_wide, "yx", g_first, 0, None),
+        (*sets[0], key_wide, "xy", g_first, query_wide, None),
+        (*gain_set, 128, "yx", g_first, query_wide + key_wide, None),
+        (*down_sets[0], d_rest, "xy", g_down, 2 * d_wide, None),
+    )
+    D0, D1, G0, U0, G1, U1, O, Q, KV, GAIN, D2 = range(11)
     comm = Scattering(me, chunks, send, recv, free)
 
     def over_rows(body, step=64):
@@ -1045,11 +1067,11 @@
         x = lax.rem(me.x + rel["x"], 2)
         return ref.at[:, y, x] if c is None else ref.at[:, y, x, c]
 
-    def left_rows(own_t, sib_t, order):
+    def left_rows(own_t, sib_t):
         for side, ref in ((0, own_t), (1, sib_t)):
             loads = []
             for i in range(4):
-                src = block(ref, i // 2, i % 2, order, me.c if side == 0 else None)
+                src = block(ref, i // 2, i % 2, "xy", me.c if side == 0 else None)
                 copy = pltpu.make_async_copy(src, lraw.at[i], lhs_sem.at[i])
                 copy.start()
                 loads.append(copy)
@@ -1065,23 +1087,46 @@
 
             lax.fori_loop(0, 4, one, 0)
 
-    def product_down(k, base):
-        order = chunks[k][5]
-        for i in (3, 2, 1, 0):
-            loads = []
-            for side, ref in ((0, hid_t), (1, hid_s)):
-                src = block(ref, i // 2, i % 2, order, me.c if side == 0 else None)
-                for z in range(me.Z):
-                    copy = pltpu.make_async_copy(
+    def down_rows(k, i, slot):
+        copies = []
+        for side, ref in ((0, hid_t), (1, hid_s)):
+            src = block(ref, i // 2, i % 2, chunks[k][5], me.c if side == 0 else None)
+            for z in range(me.Z):
+                copies.append(
+                    pltpu.make_async_copy(
                         src.at[z],
-                        lhs_d.at[pl.ds(z * rd, rd), pl.ds(side * tokens, tokens)],
-                        lhs_sem.at[side * me.Z + z],
+                        lhs_d.at[slot, pl.ds(z * rd, rd), pl.ds(side * tokens, tokens)],
+                        lhs_sem.at[(slot * 2 + side) * me.Z + z],
                     )
+                )
+        return copies
+
+    def product_down(k, base, right=None):
+        own, wide_k = chunks[k][0], chunks[k][4]
+        for copy in down_rows(k, 3, 0):
+            copy.start()
+        for n, i in enumerate((3, 2, 1, 0)):
+            slot = n % 2
+            if i > 0:
+                for copy in down_rows(k, i - 1, 1 - slot):
                     copy.start()
-                    loads.append(copy)
-            for copy in loads:
+            for copy in down_rows(k, i, slot):
                 copy.wait()
-            product(k, dy_p, base, lhs_d, rd, (i,))
+            left = lhs_d.at[slot]
+            if right is None:
+                product(k, dy_p, base, left, rd, (i,))
+            else:
+
+                def body(j, carry, i=i, left=left):
+                    cols = pl.ds(pl.multiple_of(base + j * 256, 256), 256)
+                    here = pl.ds(pl.multiple_of(j * 256, 256), 256)
+                    total = plain_dot(left[:, :tokens], right[0][:, cols]) + plain_dot(
+                        left[:, tokens:], right[1][:, cols]
+                    )
+                    own[i // 2, i % 2, :, :, here] = total.reshape(me.Z, rd, 256).astype(bf)
+                    return carry
+
+                lax.fori_loop(0, wide_k // 256, body, 0)
         comm.begin(k)
 
     def product(k, pair, base, left, depth, blocks=(0, 1, 2, 3)):
@@ -1101,15 +1146,18 @@
                 for side in range(2)
             ]
 
-        for copy in tile(0, 0):
-            copy.start()
+        depth_of = rhs.shape[0]
+        for j in range(min(depth_of - 1, count)):
+            for copy in tile(j, j):
+                copy.start()
 
         def body(j, carry):
-            slot = lax.rem(j, 2)
-
-            @pl.when(j + 1 < count)
+            slot = lax.rem(j, depth_of)
+            ahead = j + depth_of - 1
+
+            @pl.when(ahead < count)
             def _():
-                for copy in tile(j + 1, lax.rem(j + 1, 2)):
+                for copy in tile(ahead, lax.rem(ahead, depth_of)):
                     copy.start()
 
             for copy in tile(j, slot):
@@ -1120,7 +1168,10 @@
             )
             total = total.reshape(span, me.Z, depth, t).astype(bf)
             for q, at in enumerate(blocks):
-                own[at // 2, at % 2, :, :, cols] = total[q]
+                if chunks[k][5] == "xy" or span == 1:
+                    own[at // 2, at % 2, :, :, cols] = total[q]
+                else:
+                    own[at % 2, at // 2, :, :, cols] = total[q]
             return carry
 
         lax.fori_loop(0, count, body, 0)
@@ -1146,61 +1197,61 @@
     def tile_loads(j):
         at = pl.ds(j * wide, wide)
         return [
-            pltpu.make_async_copy(down_w.at[at, :], wd, load_sem.at[2]),
-            pltpu.make_async_copy(slope_in.at[:, at], fac_a, load_sem.at[3]),
-            pltpu.make_async_copy(silu_in.at[:, at], fac_b, load_sem.at[4]),
+            pltpu.make_async_copy(down_w.at[at, :], wd.at[j % 2], load_sem.at[2]),
+            pltpu.make_async_copy(slope_in.at[:, at], fac_a.at[j % 2], load_sem.at[3]),
+            pltpu.make_async_copy(silu_in.at[:, at], fac_b.at[j % 2], load_sem.at[4]),
         ]
 
-    gather_tiles = lambda j: [
-        load3(5, gate_w, raw_a, j * wide, wide),
-        load3(6, up_w, raw_b, j * wide, wide),
-    ]
+    gate_tile = lambda j: load3(5, gate_w, raw_a, j * wide, wide)
+    up_tile = lambda j: load3(6, up_w, raw_a, j * wide, wide)
     head_pack = load3(7, first_w, raw_a, used, 128)
     head_pack.start()
     head_pack.wait()
     assemble(raw_a, w_a, 128)
     gains[...] = w_a[:, :128].astype(f32).T[:8]
-    for copy in tile_loads(0) + gather_tiles(0):
+    for copy in tile_loads(0) + [gate_tile(0)]:
         copy.start()
     need_cot.wait()
     own_dy.wait()
     tile_sends = [None] * tiles
+
+    def arrive(low, high):
+        for j in range(low, high):
+            for copy in tile_sends[j]:
+                copy.settle()
+
     for j in range(tiles):
         slot = j % 2
         for copy in tile_loads(j):
             copy.wait()
-        if j >= 2:
-            for copy in tile_sends[j - 2]:
-                copy.wait()
-        for copy in gather_tiles(j):
-            copy.wait()
-        assemble(raw_a, w_a, wide)
-        assemble(raw_b, w_b, wide)
-        if j + 1 < tiles:
-            for copy in gather_tiles(j + 1):
-                copy.start()
-
-        def units(at, slot=slot, j=j):
-            grad_hidden = dot_t(cot[at, :], wd[...])
-            dg = (grad_hidden * fac_a[at, :].astype(f32)).astype(bf)
-            du = (grad_hidden * fac_b[at, :].astype(f32)).astype(bf)
-            dgt[slot, at, :] = dg
-            dut[slot, at, :] = du
-            piece = dot_t(dg, w_a[:, :wide]) + dot_t(du, w_b[:, :wide])
-            acc[at, :] = piece if j == 0 else acc[at, :] + piece
-
-        over_rows(units, 256)
         if j + 1 < tiles:
             for copy in tile_loads(j + 1):
                 copy.start()
+        gate_tile(j).wait()
+        assemble(raw_a, w_a, wide)
+        up_tile(j).start()
+        if j >= 1:
+            for copy in tile_sends[j - 1]:
+                copy.wait()
+
+        def units(at, slot=slot, j=j):
+            grad_hidden = dot_t(cot[at, :], wd[slot])
+            dg = (grad_hidden * fac_a[slot, at, :].astype(f32)).astype(bf)
+            du = (grad_hidden * fac_b[slot, at, :].astype(f32)).astype(bf)
+            dgt[at, :] = dg
+            dut[at, :] = du
+            piece = dot_t(dg, w_a[:, :wide])
+            acc[at, :] = piece if j == 0 else acc[at, :] + piece
+
+        over_rows(units, 256)
         cols = pl.ds(j * wide, wide)
         sends = []
         for i, (src, dst) in enumerate(((dgt, gate_p), (dut, up_p))):
             here = pltpu.make_async_copy(
-                src.at[slot], dst.at[0, :, cols], store_sem.at[1 + 2 * slot + i]
+                src, dst.at[0, :, cols], store_sem.at[1 + i]
             )
             there = pltpu.make_async_remote_copy(
-                src_ref=src.at[slot],
+                src_ref=src,
                 dst_ref=dst.at[1, :, cols],
                 send_sem=t_send.at[2 * j + i],
                 recv_sem=t_recv.at[2 * j + i],
@@ -1209,32 +1260,42 @@
             )
             here.start()
             there.start()
-            passes.append(there)
-            sends.append(here)
-        tile_sends[j] = [_Both(here, there) for here, there in zip(sends, passes[-2:])]
+            sends.append(_Both(here, there))
+        tile_sends[j] = sends
+        up_tile(j).wait()
+        assemble(raw_a, w_a, wide)
+        if j + 1 < tiles:
+            gate_tile(j + 1).start()
+
+        def units_up(at):
+            acc[at, :] = acc[at, :] + dot_t(dut[at, :], w_a[:, :wide])
+
+        over_rows(units_up, 256)
+        if j == 0:
+            got_dy.wait_recv()
+            need_sib = fetch(1, dy_p.at[1], low_t)
+            got_hid.wait_recv()
+            need_sib.wait()
+            product_down(D0, 0, (cot, low_t))
         if j == 1:
-            got_hid.wait_recv()
-            got_dy.wait_recv()
-            product_down(D0, 0)
+            product_down(D1, d_wide, (cot, low_t))
         if j == 3:
-            product_down(D1, d_wide)
-    for j in (tiles - 2, tiles - 1):
-        for copy in tile_sends[j]:
-            copy.wait()
-    arrived = [p for p in passes[5:]]
-    for copy in arrived:
-        copy.wait_recv()
-    got_h2.wait_recv()
-    left_rows(h2_t, h2_s, "xy")
-    product(G0, gate_p, 0, lhs, r)
-    comm.begin(G0)
-    product(U0, up_p, 0, lhs, r)
-    comm.begin(U0)
-    comm.first(D0)
-    left_rows(h2_t, h2_s, "yx")
+            got_h2.wait_recv()
+            left_rows(h2_t, h2_s)
+            arrive(0, 4)
+            product(G0, gate_p, 0, lhs, r)
+            comm.begin(G0)
+            product(U0, up_p, 0, lhs, r)
+            comm.begin(U0)
+        if j == 4:
+            comm.first(D0)
+        if j == 5:
+            comm.first(D1)
+    arrive(4, tiles)
     product(G1, gate_p, half, lhs, r)
     comm.begin(G1)
-    comm.first(D1)
+    comm.second(D0)
+    comm.second(D1)
 
     gsum[...] = jnp.zeros_like(gsum)
 
@@ -1286,22 +1347,26 @@
     tile_w = raw_a.shape[2]
     steps = width // tile_w
     load3(5, out_w, raw_a, 0, tile_w).start()
+    keep_dy1.wait()
     for j in range(steps):
-        raw, flat = ((raw_a, w_a), (raw_b, w_b))[j % 2]
+        load3(5, out_w, raw_a, j * tile_w, tile_w).wait()
+        assemble(raw_a, w_a, tile_w)
         if j + 1 < steps:
-            load3(5 + (j + 1) % 2, out_w, (raw_b, raw_a)[j % 2], (j + 1) * tile_w, tile_w).start()
-        load3(5 + j % 2, out_w, raw, j * tile_w, tile_w).wait()
-        assemble(raw, flat, tile_w)
-
-    def back_out(at):
-        grads[at, :] = (
-            dot_t(low_t[at, :tile_w], w_a[...]) + dot_t(low_t[at, tile_w:], w_b[...])
-        ).astype(bf)
-
-    over_rows(back_out, 256)
-    comm.second(D0)
+            load3(5, out_w, raw_a, (j + 1) * tile_w, tile_w).start()
+
+        def back_out(at, j=j):
+            piece = dot_t(low_t[at, j * tile_w : (j + 1) * tile_w], w_a[...])
+            if j > 0:
+                piece = acc[at, :] + piece
+            if j + 1 < steps:
+                acc[at, :] = piece
+            else:
+                grads[at, :] = piece.astype(bf)
+
+        over_rows(back_out, 256)
     comm.first(G0)
-    comm.second(D1)
+    comm.third(D0)
+    comm.third(D1)
 
     need_q.wait()
     need_kv.wait()
@@ -1351,41 +1416,36 @@
 
     count = batches * kv_heads
     lax.fori_loop(0, 2, head, 0)
+    comm.first(U0)
     own_low.wait()
     got_low.wait_recv()
-    comm.first(U0)
     comm.second(G0)
-    comm.third(D0)
     lax.fori_loop(2, 4, head, 0)
+    comm.second(U0)
     comm.first(G1)
-    comm.third(D1)
     comm.third(G0)
+    comm.reuse(0)
+    product(U1, up_p, half, lhs, r)
+    comm.begin(U1)
     lax.fori_loop(4, 6, head, 0)
+    comm.third(U0)
+    comm.second(G1)
+    comm.reuse(1)
+    got_att.wait_recv()
+    left_rows(att_t, att_s)
+    product(O, dm_p, 0, lhs, r)
+    comm.begin(O)
+    lax.fori_loop(6, 8, head, 0)
     comm.reuse(4)
     product_down(D2, 2 * d_wide)
-    comm.reuse(0)
-    left_rows(h2_t, h2_s, "yx")
-    product(U1, up_p, half, lhs, r)
-    comm.begin(U1)
-    comm.second(U0)
-    comm.second(G1)
-    lax.fori_loop(6, 8, head, 0)
-    comm.third(U0)
     comm.third(G1)
     lax.fori_loop(8, count, head, 0)
-    comm.first(D2)
 
     def portion(dx, c):
         row = (lax.rem(me.x + dx, 2) * 2 + c) * rows
         return pl.ds(pl.multiple_of(row, 256), rows)
 
     to_c = [hand(6 + dx, dkv.at[:, portion(dx, other), :], dkv_r.at[dx]) for dx in (1, 0)]
-    comm.reuse(1)
-    got_att.wait_recv()
-    left_rows(att_t, att_s, "xy")
-    product(O, dm_p, 0, lhs, r)
-    comm.begin(O)
-
     def gather_portion(dx):
         place = portion(dx, me.c)
         for b in range(batches):
@@ -1411,21 +1471,20 @@
     )
     to_x.start()
     passes.append(to_x)
-    query_wide = pre.shape[1] - kv_heads * 128
     own_q = store(6, pre.at[:, pl.ds(0, query_wide)], pre_p.at[0, :, pl.ds(0, query_wide)])
     got_q = hand(9, pre.at[:, pl.ds(0, query_wide)], pre_p.at[1, :, pl.ds(0, query_wide)])
     to_c[1].wait_recv()
     gather_portion(0)
     comm.first(U1)
-    comm.second(D2)
     comm.reuse(2)
     got_nor.wait_recv()
-    left_rows(nor_t, nor_s, "yx")
+    left_rows(nor_t, nor_s)
     own_q.wait()
     got_q.wait_recv()
     product(Q, pre_p, 0, lhs, r)
     comm.begin(Q)
     comm.first(O)
+    comm.first(D2)
     comm.second(U1)
     to_x.wait_recv()
     for b in range(batches):
@@ -1446,27 +1505,25 @@
     got_kv = hand(10, pre.at[:, rest], pre_p.at[1, :, rest])
 
     need_x = fetch(0, x_in, cot)
-    keep_dy1.wait()
     steps = pre.shape[1] // tile_w
     load3(5, first_w, raw_a, 0, tile_w).start()
     for j in range(steps):
-        raw, flat = ((raw_a, w_a), (raw_b, w_b))[j % 2]
+        load3(5, first_w, raw_a, j * tile_w, tile_w).wait()
+        assemble(raw_a, w_a, tile_w)
         if j + 1 < steps:
-            load3(5 + (j + 1) % 2, first_w, (raw_b, raw_a)[j % 2], (j + 1) * tile_w, tile_w).start()
-        load3(5 + j % 2, first_w, raw, j * tile_w, tile_w).wait()
-        assemble(raw, flat, tile_w)
-
-        def back_in(at, j=j, flat=flat):
-            piece = dot_t(pre[at, j * tile_w : (j + 1) * tile_w], flat[...])
+            load3(5, first_w, raw_a, (j + 1) * tile_w, tile_w).start()
+
+        def back_in(at, j=j):
+            piece = dot_t(pre[at, j * tile_w : (j + 1) * tile_w], w_a[...])
             acc[at, :] = piece if j == 0 else acc[at, :] + piece
 
         over_rows(back_in, 256)
+    comm.second(O)
+    comm.second(D2)
     comm.third(U1)
-    comm.third(D2)
     comm.reuse(3)
     own_kv.wait()
     got_kv.wait_recv()
-    left_rows(nor_t, nor_s, "xy")
     product(KV, pre_p, query_wide, lhs, r)
     comm.begin(KV)
     need_x.wait()
@@ -1485,7 +1542,6 @@
     stream(dy1_h, norm_one)
     store(8, queries, grad_out)
     comm.first(Q)
-    comm.second(O)
 
     gsib = gain_set[0]
     columns = jnp.concatenate([gsum[...], jnp.zeros((120, width), f32)], 0).T
@@ -1507,22 +1563,31 @@
 
     need_mixed = fetch(1, mixed_in, acc)
     need_mixed.wait()
+    last_loads = lambda j: [
+        pltpu.make_async_copy(
+            down_w.at[pl.ds(j * wide, wide), :], wd.at[j % 2], load_sem.at[2]
+        ),
+        pltpu.make_async_copy(
+            hidden_in.at[:, pl.ds(j * wide, wide)], fac_a.at[j % 2], load_sem.at[3]
+        ),
+    ]
+    for copy in last_loads(0):
+        copy.start()
     for j in range(tiles):
-        at = pl.ds(j * wide, wide)
-        wd_load = pltpu.make_async_copy(down_w.at[at, :], wd, load_sem.at[2])
-        hidden_load = pltpu.make_async_copy(hidden_in.at[:, at], fac_a, load_sem.at[3])
-        wd_load.start()
-        hidden_load.start()
-        wd_load.wait()
-        hidden_load.wait()
-
-        def add_down(at):
-            acc[at, :] = acc[at, :] + plain_dot(fac_a[at, :], wd[...])
+        for copy in last_loads(j):
+            copy.wait()
+        if j + 1 < tiles:
+            for copy in last_loads(j + 1):
+                copy.start()
+
+        def add_down(at, j=j):
+            acc[at, :] = acc[at, :] + plain_dot(fac_a[j % 2, at, :], wd[j % 2])
 
         over_rows(add_down, 256)
         if j == 1:
             comm.first(GAIN)
             comm.third(O)
+            comm.third(D2)
         if j == 2:
             comm.second(KV)
         if j == 4:
@@ -1538,7 +1603,7 @@
     comm.third(KV)
     comm.third(GAIN)
     for copy in passes:
-        if copy is not got_low and not any(copy is p for p in arrived):
+        if copy is not got_low:
             copy.wait_send()
     for copy in stores:
         if not any(copy is p for p in (own_dy, own_low, own_q, own_kv)):
@@ -1547,11 +1612,19 @@
 
 class _Both:
     def __init__(self, here, there):
-        self.here, self.there = here, there
+        self.here, self.there, self.sent, self.settled = here, there, False, False
 
     def wait(self):
-        self.here.wait()
-        self.there.wait_send()
+        if not self.sent:
+            self.here.wait()
+            self.there.wait_send()
+        self.sent = True
+
+    def settle(self):
+        self.wait()
+        if not self.settled:
+            self.there.wait_recv()
+        self.settled = True
 
 
 def backward(saved, transposed, dy, x, kv_heads, group, batches):
@@ -1608,10 +1681,10 @@
     scratch = sum([four(r, half) for _ in range(3)], [])
     scratch += four(rd, d_wide) + four(rd, d_wide) + four(r, 128)
     scratch += [
-        vmem((Z * rd, 2 * tokens), bf),
+        vmem((2, Z * rd, 2 * tokens), bf),
         vmem((4 * Z * r, 2 * tokens), bf),
         vmem((4, Z, r, tokens), bf),
-        vmem((2, 2, tokens, t), bf),
+        vmem((3, 2, tokens, t), bf),
         vmem((tokens, width), f32),
         vmem((2, 64, width), f32),
         vmem((tokens, width), bf),
@@ -1628,14 +1701,12 @@
         vmem((2, batches, rows, key_wide), bf),
         vmem((batches, rows, key_wide), bf),
         vmem((n, r, key_wide), bf),
-        vmem((n, r, key_wide), bf),
         vmem((width, key_wide), bf),
-        vmem((width, key_wide), bf),
-        vmem((wide, width), bf),
+        vmem((2, wide, width), bf),
+        vmem((2, tokens, wide), bf),
+        vmem((2, tokens, wide), bf),
         vmem((tokens, wide), bf),
         vmem((tokens, wide), bf),
-        vmem((2, tokens, wide), bf),
-        vmem((2, tokens, wide), bf),
         vmem((8, width), f32),
         vmem((8, width), f32),
         vmem((2, n, r, 128), bf),
@@ -1649,7 +1720,7 @@
         dma((12,)),
         dma((8 * Z,)),
         dma((10,)),
-        dma((2, 2)),
+        dma((3, 2)),
         dma((3,)),
     ]
     return pl.pallas_call(
@@ -1868,15 +1939,9 @@
         shards, x_low, positions.reshape(tokens, 1), kv_heads, group, batches
     )
     if fits:
-        x_float = x_low.astype(jnp.float32)
-        attn_inverse = lax.rsqrt(jnp.mean(x_float * x_float, -1, keepdims=True) + EPSILON)
-        gain = saved[0].reshape(width, -1)[:, used].astype(jnp.float32)
-        normed = (x_float * attn_inverse * gain).astype(jnp.bfloat16)
         by_place = (lax.axis_size("dp") // 2, 2, lax.axis_size("fsdp") // 2, 2, -1, tokens)
-        transposed = [
-            t.T.reshape(by_place) for t in (saved[11], saved[10], saved[7], normed)
-        ]
-        found = backward(saved, transposed, cot_low, x_low, kv_heads, group, batches)
+        transposed = [t.reshape(by_place) for t in saved[17:]]
+        found = backward(saved[:17], transposed, cot_low, x_low, kv_heads, group, batches)
     else:
         found = backward_plain(saved, cot_low, x_low, kv_heads, group, batches)
     output, grad_input, last, grad_out, grad_gate, grad_up, grad_down = found[:7]

time: 629 us -> 561 us (0.89)
  Pallas kernels: 577 us -> 527 us
  local copies, waits for them, and re-layouts: 29.6 us -> 17.1 us
    pallas_call x1, Pallas kernels: 371 us -> 314 us  [backward(): pl.pallas_call(functools.partial(backward_kernel, (batches, rows, kv_head...]
    transpose x4 -> x0, local copies, waits for them, and re-layouts: 11.3 us -> none  [on_device(): t.T.reshape(by_place)]
    pallas_call x1, Pallas kernels: 206 us -> 213 us  [forward(): pl.pallas_call(functools.partial(forward_kernel, (batches, rows, kv_heads...]
where the time goes in v6:
time: 561 us; the launch traced here: 551 us
  Pallas kernels  527 us (94%)
  local copies, waits for them, and re-layouts  17.1 us (3%)
    pallas_call x1, Pallas kernels, backward(): pl.pallas_call(functools.partial(backward_kernel, (batches, rows, kv_head...  314 us
    pallas_call x1, Pallas kernels, forward(): pl.pallas_call(functools.partial(forward_kernel, (batches, rows, kv_heads...  213 us

profile of v6, /device:TPU:4, one launch (start us, length us, event | category | flops | bytes accessed | tf_op | source)
XLA Modules:
  0.0 551.3 jit_solution(10207718016016049630)
XLA Ops:
  0.6 0.6 compare_reduce_fusion.1
  1.3 0.6 compare_reduce_fusion
  1.9 1.3 fusion.1
  3.2 1.3 fusion
  4.6 0.6 broadcast_in_dim_tile.3.refs_7_
  5.2 0.1 copy.27
  5.3 0.1 copy.28
  5.4 0.1 scatter.9
  5.5 0.9 reshape.125
  6.4 0.9 reshape.126
  7.2 0.1 pad_maximum_fusion.1
  7.3 1.6 pad_maximum_fusion.refs_0_
  8.9 1.5 copy.29.refs_6_
  10.4 213.1 %shard_map.203 = (bf16[32,40,2048]{2,1,0:T(8,128)(2,1)}, bf16[32,40,1280]{2,1,0:T(8,128)(2,1)}, bf16[32,40,3584]{2,1,0:T(8,128)(2,1)}, bf16[32,40,3584]{2,1,0:T(...) custom-call(bf16[40,2048]{1,0:T(8,128)(2,1)} %pad_maximum_fusion.ref, ...), custom_call_target="tpu_custom_call" | custom-call | flops 13589544960 | bytes 71434240 | tf_op jit(solution)/shard_map/pallas_call | solution.py:573
  223.5 314.3 %shard_map.204 = (bf16[512,1280]{1,0:T(8,128)(2,1)}, bf16[512,1280]{1,0:T(8,128)(2,1)}, f32[40,2048]{1,0:T(8,128)}, f32[40,1280]{1,0:T(8,128)}, f32[40,3584]{1,0...) custom-call(bf16[512,1280]{1,0:T(8,128)(2,1)} %bitcast.26, ...), custom_call_target="tpu_custom_call" | custom-call | tf_op jit(solution)/shard_map/pallas_call | solution.py:1726
  537.9 0.0 copy-start
  537.9 1.5 slice_reduce_fusion.2
  539.4 0.9 slice.49
  540.3 1.6 slice.48
  542.0 0.2 reshape.139
  542.1 0.6 slice_reduce_fusion
  542.7 0.7 reshape_squeeze.7
  543.4 0.7 reshape_squeeze.6
  544.1 0.0 copy-start.4
  544.1 0.0 copy-start.3
  544.1 2.5 copy.42
  546.7 0.0 copy-done
  546.7 0.0 copy-start.2
  546.7 0.0 copy-start.1
  546.7 1.1 copy.43
  547.7 0.0 copy-done.4
  547.7 0.7 copy.44
  548.4 0.0 copy-done.3
  548.4 0.8 copy.45
  549.2 0.0 copy-done.2
  549.2 0.8 copy.46
  550.0 0.0 copy-done.1
  550.0 0.8 copy.47
  (4 shorter events, 0.0 us)
Async XLA Ops:
  537.9 8.8 %copy-start = (bf16[512,1280]{1,0:T(8,128)(2,1)S(1)}, bf16[512,1280]{1,0:T(8,128)(2,1)}, u32[]{:S(2)}) copy-start(bf16[512,1280]{1,0:T(8,128)(2,1)} %get-tuple-element.81) | copy-start | bytes 3932164
  544.1 3.6 copy-start.4
  544.1 4.3 copy-start.3
  546.7 2.6 copy-start.2
  546.7 3.4 copy-start.1

commit v7 on v6

--- a/solution.py
+++ b/solution.py
@@ -213,8 +213,8 @@
     comm = Gathering(
         me,
         (
-            (first_s, first_w, whole, "yxc"),
-            (out_s, out_w, whole, "xyc"),
+            (first_s, first_w, whole, "xyc"),
+            (out_s, out_w, whole, "yxc"),
             (gate_s, gate_w, whole, "yxc"),
             (up_s, up_w, whole, "xyc"),
             (down_s, down_w, pl.ds(0, half), "yxc"),
@@ -302,11 +302,10 @@
     comm.begin(3)
     comm.step(1, 0)
     comm.step(0, 1)
-    comm.begin(4)
     comm.step(2, 0)
     comm.step(1, 1)
     comm.step(0, 2)
-    comm.begin(5)
+    comm.begin(4)
     comm.step(3, 0)
     comm.step(2, 1)
     comm.step(1, 2)
@@ -367,6 +366,7 @@
     to_x = share(0, 0, "x")
     to_c = share(1, 0, "c")
     comm.step(3, 1)
+    comm.begin(5)
     for j in range(queries.shape[1] // tile):
         raw, flat = ((raw_b, w_b), (raw_a, w_a))[j % 2]
         if (j + 1) * tile < queries.shape[1]:
@@ -872,14 +872,14 @@
         copy.start()
         self.copies[(k, name)] = copy
 
-    def add(self, dst, src, wide):
+    def add(self, dst, src, wide, base):
         depth = dst.shape[0]
         t = tile_of(wide)
         count = wide // t
 
         def body(i, carry):
             at = i // count
-            cols = pl.ds(pl.multiple_of(lax.rem(i, count) * t, 128), t)
+            cols = pl.ds(pl.multiple_of(base + lax.rem(i, count) * t, 128), t)
             dst[at, :, cols] = dst[at, :, cols] + src[at, :, cols]
             return carry
 
@@ -887,7 +887,7 @@
 
     def buffers(self, k):
         own, one, two, last, wide = self.chunks[k][:5]
-        cols = pl.ds(0, wide)
+        cols = pl.ds(self.chunks[k][9], wide)
         return own, one, two, last, wide, cols
 
     def begin(self, k):
@@ -908,7 +908,7 @@
         order = self.chunks[k][5]
         for b in (1, 0):
             self.copies[(k, ("1", b))].wait_recv()
-            self.add(own.at[0, b], one.at[b], wide)
+            self.add(own.at[0, b], one.at[b], wide, self.chunks[k][9])
             if b == 1:
                 self.ship(
                     k,
@@ -923,7 +923,7 @@
         own, one, two, last, wide, cols = self.buffers(k)
         me = self.me
         self.copies[(k, "2")].wait_recv()
-        self.add(own.at[0, 0], two, wide)
+        self.add(own.at[0, 0], two, wide, self.chunks[k][9])
         for s in range(1, me.Z):
             self.ship(
                 k,
@@ -937,13 +937,13 @@
     def third(self, k):
         own, one, two, last, wide, cols = self.buffers(k)
         me = self.me
-        _, out, base, group = self.chunks[k][5:]
+        _, out, base, group, off = self.chunks[k][5:]
         for s in range(1, me.Z):
             self.copies[(k, ("z", s))].wait_recv()
         t = tile_of(wide)
 
         def body(j, carry):
-            here = pl.ds(pl.multiple_of(j * t, 128), t)
+            here = pl.ds(pl.multiple_of(off + j * t, 128), t)
             there = pl.ds(pl.multiple_of(base + j * t, 128), t)
             total = own[0, 0, me.z, :, here].astype(jnp.float32)
             for s in range(1, me.Z):
@@ -1002,17 +1002,17 @@
     d_wide = down_sets[0][0].shape[-1]
     d_rest = width - 2 * d_wide
     chunks = (
-        (*down_sets[0], d_wide, "xy", g_down, 0, 4),
-        (*down_sets[1], d_wide, "yx", g_down, d_wide, None),
-        (*sets[0], half, "xy", g_gate, 0, 0),
-        (*sets[1], half, "yx", g_up, 0, 1),
-        (*sets[2], half, "xy", g_gate, half, 2),
-        (*sets[0], half, "yx", g_up, half, 3),
-        (*sets[1], width, "xy", g_out, 0, None),
-        (*sets[2], query_wide, "yx", g_first, 0, None),
-        (*sets[0], key_wide, "xy", g_first, query_wide, None),
-        (*gain_set, 128, "yx", g_first, query_wide + key_wide, None),
-        (*down_sets[0], d_rest, "xy", g_down, 2 * d_wide, None),
+        (*down_sets[0], d_wide, "xy", g_down, 0, 4, 0),
+        (*down_sets[1], d_wide, "yx", g_down, d_wide, None, 0),
+        (*sets[0], half, "xy", g_gate, 0, 0, 0),
+        (*sets[1], half, "yx", g_up, 0, 1, 0),
+        (*sets[2], half, "xy", g_gate, half, 2, 0),
+        (*sets[0], half, "yx", g_up, half, None, 0),
+        (*sets[1], width, "xy", g_out, 0, None, 0),
+        (*sets[2], query_wide, "yx", g_first, 0, None, 0),
+        (*sets[2], key_wide - 128, "yx", g_first, query_wide, None, query_wide),
+        (*gain_set, 256, "yx", g_first, query_wide + key_wide - 128, None, 0),
+        (*down_sets[0], d_rest, "yx", g_down, 2 * d_wide, None, 0),
     )
     D0, D1, G0, U0, G1, U1, O, Q, KV, GAIN, D2 = range(11)
     comm = Scattering(me, chunks, send, recv, free)
@@ -1129,8 +1129,8 @@
                 lax.fori_loop(0, wide_k // 256, body, 0)
         comm.begin(k)
 
-    def product(k, pair, base, left, depth, blocks=(0, 1, 2, 3)):
-        own, wide_k = chunks[k][0], chunks[k][4]
+    def product(k, pair, base, left, depth, blocks=(0, 1, 2, 3), size=None):
+        own, wide_k = chunks[k][0], size or chunks[k][4]
         t = rhs.shape[3] if wide_k % rhs.shape[3] == 0 else 128
         count = wide_k // t
         span = len(blocks)
@@ -1162,7 +1162,7 @@
 
             for copy in tile(j, slot):
                 copy.wait()
-            cols = pl.ds(pl.multiple_of(j * t, 128), t)
+            cols = pl.ds(pl.multiple_of(chunks[k][9] + j * t, 128), t)
             total = plain_dot(left[:, :tokens], rhs[slot, 0, :, :t]) + plain_dot(
                 left[:, tokens:], rhs[slot, 1, :, :t]
             )
@@ -1294,8 +1294,6 @@
     arrive(4, tiles)
     product(G1, gate_p, half, lhs, r)
     comm.begin(G1)
-    comm.second(D0)
-    comm.second(D1)
 
     gsum[...] = jnp.zeros_like(gsum)
 
@@ -1364,14 +1362,69 @@
                 grads[at, :] = piece.astype(bf)
 
         over_rows(back_out, 256)
+    comm.second(D0)
     comm.first(G0)
-    comm.third(D0)
-    comm.third(D1)
+    comm.second(D1)
 
     need_q.wait()
     need_kv.wait()
     for copy in need:
         copy.wait()
+    def portion(dx, c):
+        row = (lax.rem(me.x + dx, 2) * 2 + c) * rows
+        return pl.ds(pl.multiple_of(row, 256), rows)
+
+    def to_sibling(b):
+        return [
+            hand(6 + 2 * b + dx, dkv.at[b, portion(dx, other), :], dkv_r.at[dx, b])
+            for dx in (1, 0)
+        ]
+
+    def gather_portion(b, dx):
+        place = portion(dx, me.c)
+
+        def body(j, carry):
+            at = pl.ds(pl.multiple_of(j * 64, 64), 64)
+            there = pl.ds(pl.multiple_of(place.start + j * 64, 64), 64)
+            total = dkv_r[dx, b, at, :].astype(f32) + dkv[b, there, :].astype(f32)
+            dkv_r[dx, b, at, :] = total.astype(bf)
+            return carry
+
+        lax.fori_loop(0, rows // 64, body, 0)
+
+    def to_neighbour(b, handed):
+        handed[0].wait_recv()
+        gather_portion(b, 1)
+        copy = pltpu.make_async_remote_copy(
+            src_ref=dkv_r.at[1, b],
+            dst_ref=dkv_x.at[b],
+            send_sem=x_send.at[10 + b],
+            recv_sem=x_recv.at[10 + b],
+            device_id=me.device(dx=1),
+            device_id_type=MESH,
+        )
+        copy.start()
+        passes.append(copy)
+        handed[1].wait_recv()
+        gather_portion(b, 0)
+        return copy
+
+    def merge_portion(b, copy):
+        copy.wait_recv()
+
+        def merge(j, carry):
+            at = pl.ds(pl.multiple_of(j * 64, 64), 64)
+            token = pl.ds(pl.multiple_of(b * rows + j * 64, 64), 64)
+            for h in range(kv_heads):
+                cols = slice(h * 128, (h + 1) * 128)
+                total = dkv_r[0, b, at, cols].astype(f32) + dkv_x[b, at, cols].astype(f32)
+                total = total * cos_t[1, token, :] - swap_halves(total) * sin_t[1, token, :]
+                pre[token, query_wide + h * 128 : query_wide + (h + 1) * 128] = total.astype(bf)
+            return carry
+
+        lax.fori_loop(0, rows // 64, merge, 0)
+
+    to_x = [None] * batches
     lanes = lax.broadcasted_iota(jnp.int32, (rows, 128), 1)
     sides_mask = lane_masks(rows)
 
@@ -1417,65 +1470,35 @@
     count = batches * kv_heads
     lax.fori_loop(0, 2, head, 0)
     comm.first(U0)
+    comm.third(D0)
     own_low.wait()
     got_low.wait_recv()
+    lax.fori_loop(2, 5, head, 0)
+    comm.third(D1)
     comm.second(G0)
-    lax.fori_loop(2, 4, head, 0)
+    handed = to_sibling(0)
+    comm.first(G1)
+    lax.fori_loop(5, 8, head, 0)
     comm.second(U0)
-    comm.first(G1)
     comm.third(G0)
     comm.reuse(0)
     product(U1, up_p, half, lhs, r)
     comm.begin(U1)
-    lax.fori_loop(4, 6, head, 0)
+    to_x[0] = to_neighbour(0, handed)
+    lax.fori_loop(8, count, head, 0)
     comm.third(U0)
     comm.second(G1)
+    merge_portion(0, to_x[0])
     comm.reuse(1)
     got_att.wait_recv()
     left_rows(att_t, att_s)
     product(O, dm_p, 0, lhs, r)
     comm.begin(O)
-    lax.fori_loop(6, 8, head, 0)
-    comm.reuse(4)
-    product_down(D2, 2 * d_wide)
+    handed = to_sibling(1)
+    own_q = store(6, pre.at[:, pl.ds(0, query_wide)], pre_p.at[0, :, pl.ds(0, query_wide)])
+    got_q = hand(12, pre.at[:, pl.ds(0, query_wide)], pre_p.at[1, :, pl.ds(0, query_wide)])
+    to_x[1] = to_neighbour(1, handed)
     comm.third(G1)
-    lax.fori_loop(8, count, head, 0)
-
-    def portion(dx, c):
-        row = (lax.rem(me.x + dx, 2) * 2 + c) * rows
-        return pl.ds(pl.multiple_of(row, 256), rows)
-
-    to_c = [hand(6 + dx, dkv.at[:, portion(dx, other), :], dkv_r.at[dx]) for dx in (1, 0)]
-    def gather_portion(dx):
-        place = portion(dx, me.c)
-        for b in range(batches):
-
-            def body(j, carry, b=b):
-                at = pl.ds(pl.multiple_of(j * 64, 64), 64)
-                there = pl.ds(pl.multiple_of(place.start + j * 64, 64), 64)
-                total = dkv_r[dx, b, at, :].astype(f32) + dkv[b, there, :].astype(f32)
-                dkv_r[dx, b, at, :] = total.astype(bf)
-                return carry
-
-            lax.fori_loop(0, rows // 64, body, 0)
-
-    to_c[0].wait_recv()
-    gather_portion(1)
-    to_x = pltpu.make_async_remote_copy(
-        src_ref=dkv_r.at[1],
-        dst_ref=dkv_x,
-        send_sem=x_send.at[8],
-        recv_sem=x_recv.at[8],
-        device_id=me.device(dx=1),
-        device_id_type=MESH,
-    )
-    to_x.start()
-    passes.append(to_x)
-    own_q = store(6, pre.at[:, pl.ds(0, query_wide)], pre_p.at[0, :, pl.ds(0, query_wide)])
-    got_q = hand(9, pre.at[:, pl.ds(0, query_wide)], pre_p.at[1, :, pl.ds(0, query_wide)])
-    to_c[1].wait_recv()
-    gather_portion(0)
-    comm.first(U1)
     comm.reuse(2)
     got_nor.wait_recv()
     left_rows(nor_t, nor_s)
@@ -1483,26 +1506,13 @@
     got_q.wait_recv()
     product(Q, pre_p, 0, lhs, r)
     comm.begin(Q)
-    comm.first(O)
-    comm.first(D2)
-    comm.second(U1)
-    to_x.wait_recv()
-    for b in range(batches):
-
-        def merge(j, carry, b=b):
-            at = pl.ds(pl.multiple_of(j * 64, 64), 64)
-            token = pl.ds(pl.multiple_of(b * rows + j * 64, 64), 64)
-            for h in range(kv_heads):
-                cols = slice(h * 128, (h + 1) * 128)
-                total = dkv_r[0, b, at, cols].astype(f32) + dkv_x[b, at, cols].astype(f32)
-                total = total * cos_t[1, token, :] - swap_halves(total) * sin_t[1, token, :]
-                pre[token, query_wide + h * 128 : query_wide + (h + 1) * 128] = total.astype(bf)
-            return carry
-
-        lax.fori_loop(0, rows // 64, merge, 0)
+    comm.reuse(4)
+    product_down(D2, 2 * d_wide)
+    comm.first(U1)
+    merge_portion(1, to_x[1])
     rest = pl.ds(query_wide, kv_heads * 128)
     own_kv = store(7, pre.at[:, rest], pre_p.at[0, :, rest])
-    got_kv = hand(10, pre.at[:, rest], pre_p.at[1, :, rest])
+    got_kv = hand(13, pre.at[:, rest], pre_p.at[1, :, rest])
 
     need_x = fetch(0, x_in, cot)
     steps = pre.shape[1] // tile_w
@@ -1518,14 +1528,13 @@
             acc[at, :] = piece if j == 0 else acc[at, :] + piece
 
         over_rows(back_in, 256)
-    comm.second(O)
-    comm.second(D2)
-    comm.third(U1)
-    comm.reuse(3)
+    comm.first(O)
     own_kv.wait()
     got_kv.wait_recv()
     product(KV, pre_p, query_wide, lhs, r)
     comm.begin(KV)
+    product(GAIN, pre_p, query_wide + key_wide - 128, lhs, r, size=128)
+    comm.second(U1)
     need_x.wait()
 
     def norm_one(at, dy1):
@@ -1541,13 +1550,14 @@
 
     stream(dy1_h, norm_one)
     store(8, queries, grad_out)
+    comm.first(D2)
     comm.first(Q)
 
     gsib = gain_set[0]
     columns = jnp.concatenate([gsum[...], jnp.zeros((120, width), f32)], 0).T
     gcol[0] = columns.reshape(gcol.shape[1:]).astype(bf)
-    got_gain = hand(11, gcol.at[0], gcol.at[1])
-    comm.first(KV)
+    got_gain = hand(14, gcol.at[0], gcol.at[1])
+    comm.second(O)
     got_gain.wait_recv()
     for a in range(2):
         for b in range(2):
@@ -1557,8 +1567,10 @@
                 y, x = lax.rem(me.y + a, 2), lax.rem(me.x + b, 2)
             for z in range(me.Z):
                 at = ((z * 2 + y) * 2 + x) * 2 + me.c
-                gsib[a, b, z] = gcol[0, at] + gcol[1, at]
+                gsib[a, b, z, :, 128:] = gcol[0, at] + gcol[1, at]
     comm.begin(GAIN)
+    comm.first(KV)
+    comm.second(D2)
     comm.second(Q)
 
     need_mixed = fetch(1, mixed_in, acc)
@@ -1584,14 +1596,18 @@
             acc[at, :] = acc[at, :] + plain_dot(fac_a[j % 2, at, :], wd[j % 2])
 
         over_rows(add_down, 256)
+        if j == 0:
+            comm.third(U1)
         if j == 1:
+            comm.second(KV)
+        if j == 2:
             comm.first(GAIN)
+        if j == 3:
             comm.third(O)
             comm.third(D2)
-        if j == 2:
-            comm.second(KV)
         if j == 4:
             comm.third(Q)
+        if j == 5:
             comm.second(GAIN)
 
     def round_result(at):
@@ -1679,7 +1695,7 @@
     any_space = pl.BlockSpec(memory_space=pl.ANY)
     in_vmem = pl.BlockSpec(memory_space=pltpu.VMEM)
     scratch = sum([four(r, half) for _ in range(3)], [])
-    scratch += four(rd, d_wide) + four(rd, d_wide) + four(r, 128)
+    scratch += four(rd, d_wide) + four(rd, d_wide) + four(r, 256)
     scratch += [
         vmem((2, Z * rd, 2 * tokens), bf),
         vmem((4 * Z * r, 2 * tokens), bf),
@@ -1713,8 +1729,8 @@
         dma((11, 2 + Z)),
         dma((11, 2 + Z)),
         pltpu.SemaphoreType.REGULAR((5,)),
-        dma((12,)),
-        dma((12,)),
+        dma((15,)),
+        dma((15,)),
         dma((2 * (features // wide),)),
         dma((2 * (features // wide),)),
         dma((12,)),

time: 561 us -> 530 us (0.945)
  the two profiles are of different devices: /device:TPU:4 before, /device:TPU:0 now
where the time goes in v7:
time: 530 us; the launch traced here: 520 us
  Pallas kernels  496 us (94%)
  local copies, waits for them, and re-layouts  17.1 us (3%)
  other arithmetic  5.58 us (1%)
    pallas_call x1, Pallas kernels, backward(): pl.pallas_call(functools.partial(backward_kernel, (batches, rows, kv_head...  279 us
    pallas_call x1, Pallas kernels, forward(): pl.pallas_call(functools.partial(forward_kernel, (batches, rows, kv_heads...  218 us

profile of v7, /device:TPU:0, one launch (start us, length us, event | category | flops | bytes accessed | tf_op | source)
XLA Modules:
  0.0 520.1 jit_solution(7675034442875722758)
XLA Ops:
  0.6 0.6 compare_reduce_fusion.1
  1.3 0.6 compare_reduce_fusion
  1.9 1.3 fusion.1
  3.2 1.3 fusion
  4.6 0.6 broadcast_in_dim_tile.3.refs_7_
  5.2 0.1 copy.27
  5.3 0.1 copy.28
  5.4 0.1 scatter.9
  5.5 0.9 reshape.125
  6.4 0.9 reshape.126
  7.2 0.1 pad_maximum_fusion.1
  7.3 1.6 pad_maximum_fusion.refs_0_
  8.9 1.5 copy.29.refs_6_
  10.4 217.6 %shard_map.203 = (bf16[32,40,2048]{2,1,0:T(8,128)(2,1)}, bf16[32,40,1280]{2,1,0:T(8,128)(2,1)}, bf16[32,40,3584]{2,1,0:T(8,128)(2,1)}, bf16[32,40,3584]{2,1,0:T(...) custom-call(bf16[40,2048]{1,0:T(8,128)(2,1)} %pad_maximum_fusion.ref, ...), custom_call_target="tpu_custom_call" | custom-call | flops 13589544960 | bytes 71434240 | tf_op jit(solution)/shard_map/pallas_call | solution.py:573
  228.0 278.6 %shard_map.204 = (bf16[512,1280]{1,0:T(8,128)(2,1)}, bf16[512,1280]{1,0:T(8,128)(2,1)}, f32[40,2048]{1,0:T(8,128)}, f32[40,1280]{1,0:T(8,128)}, f32[40,3584]{1,0...) custom-call(bf16[512,1280]{1,0:T(8,128)(2,1)} %bitcast.26, ...), custom_call_target="tpu_custom_call" | custom-call | tf_op jit(solution)/shard_map/pallas_call | solution.py:1742
  506.7 0.0 copy-start
  506.7 1.5 slice_reduce_fusion.2
  508.2 0.9 slice.49
  509.1 1.6 slice.48
  510.7 0.2 reshape.139
  510.9 0.6 slice_reduce_fusion
  511.5 0.7 reshape_squeeze.7
  512.2 0.7 reshape_squeeze.6
  512.9 0.0 copy-start.4
  512.9 0.0 copy-start.3
  512.9 2.5 copy.42
  515.4 0.0 copy-done
  515.4 0.0 copy-start.2
  515.4 0.0 copy-start.1
  515.4 1.1 copy.43
  516.5 0.0 copy-done.4
  516.5 0.7 copy.44
  517.2 0.0 copy-done.3
  517.2 0.8 copy.45
  518.0 0.0 copy-done.2
  518.0 0.8 copy.46
  518.8 0.0 copy-done.1
  518.8 0.8 copy.47
  (4 shorter events, 0.0 us)
Async XLA Ops:
  506.7 8.8 %copy-start = (bf16[512,1280]{1,0:T(8,128)(2,1)S(1)}, bf16[512,1280]{1,0:T(8,128)(2,1)}, u32[]{:S(2)}) copy-start(bf16[512,1280]{1,0:T(8,128)(2,1)} %get-tuple-element.81) | copy-start | bytes 3932164
  512.9 3.6 copy-start.4
  512.9 4.3 copy-start.3
  515.4 2.6 copy-start.2
  515.4 3.4 copy-start.1

commit v8 on v7

--- a/solution.py
+++ b/solution.py
@@ -305,7 +305,6 @@
     comm.step(2, 0)
     comm.step(1, 1)
     comm.step(0, 2)
-    comm.begin(4)
     comm.step(3, 0)
     comm.step(2, 1)
     comm.step(1, 2)
@@ -325,7 +324,6 @@
         normed[at, :] = (x * inverse * gains[0:1, :]).astype(jnp.bfloat16)
 
     over_rows(norm_one)
-    comm.step(4, 0)
 
     def turn(flat, kind, put, step=256):
         def body(at):
@@ -366,7 +364,7 @@
     to_x = share(0, 0, "x")
     to_c = share(1, 0, "c")
     comm.step(3, 1)
-    comm.begin(5)
+    comm.begin(4)
     for j in range(queries.shape[1] // tile):
         raw, flat = ((raw_b, w_b), (raw_a, w_a))[j % 2]
         if (j + 1) * tile < queries.shape[1]:
@@ -380,6 +378,7 @@
         turn(flat, 0, put_query)
         if j == 0:
             comm.step(2, 2)
+            comm.begin(5)
     store(3, queries, q_out)
     turn_rows(normed, nor_t, 0, width)
     store(12, nor_t, nor_turned)
@@ -421,7 +420,7 @@
         return carry
 
     count = batches * kv_heads
-    pumps = [(5, 0), (4, 1), (3, 2), (2, 3), (5, 1), (4, 2)]
+    pumps = [(3, 2), (4, 0), (2, 3), (5, 0), (4, 1), (5, 1)]
     done = 0
     for i in range(6):
         upto = (2, 4, 6, 8, 9, 10)[i] * count // 10
@@ -464,7 +463,7 @@
 
     wide = 512
     features = hidden.shape[1]
-    pumps = {2: (5, 2), 5: (4, 3)}
+    pumps = {1: (4, 2), 3: (5, 2), 5: (4, 3)}
     load(gate_w, raw_a, 0, wide, 0).start()
     load(up_w, raw_b, 0, wide, 1).start()
     for j in range(features // wide):
@@ -488,12 +487,13 @@
 
         over_rows(units, 256)
         turn_rows(hidden, hid_t, j * wide, wide)
+        cols = pl.ds(j * wide, wide)
+        store(16 + 4 * j, hidden.at[:, cols], hidden_out.at[:, cols])
+        store(17 + 4 * j, silu.at[:, cols], silu_out.at[:, cols])
+        store(18 + 4 * j, slope.at[:, cols], slope_out.at[:, cols])
+        store(19 + 4 * j, hid_t.at[cols, :], hid_turned.at[cols, :])
         if j in pumps:
             comm.step(*pumps[j])
-    store(9, hidden, hidden_out)
-    store(10, silu, silu_out)
-    store(11, slope, slope_out)
-    store(15, hid_t, hid_turned)
     comm.step(5, 3)
     for copy in (to_x, to_c, to_far):
         copy.wait_send()
@@ -566,7 +566,7 @@
         pltpu.SemaphoreType.DMA((3,)),
         pltpu.SemaphoreType.DMA((3,)),
         pltpu.SemaphoreType.DMA((2,)),
-        pltpu.SemaphoreType.DMA((16,)),
+        pltpu.SemaphoreType.DMA((16 + 4 * (features // 512),)),
     ]
     any_space = pl.BlockSpec(memory_space=pl.ANY)
     in_vmem = pl.BlockSpec(memory_space=pltpu.VMEM)

time: 530 us -> 515 us (0.972)
  Pallas kernels: 496 us -> 481 us
    pallas_call x1, Pallas kernels: 218 us -> 207 us  [forward(): pl.pallas_call(functools.partial(forward_kernel, (batches, rows, kv_heads...]
where the time goes in v8:
time: 515 us; the launch traced here: 505 us
  Pallas kernels  481 us (93%)
  local copies, waits for them, and re-layouts  17.1 us (3%)
  other arithmetic  5.58 us (1%)
    pallas_call x1, Pallas kernels, backward(): pl.pallas_call(functools.partial(backward_kernel, (batches, rows, kv_head...  274 us
    pallas_call x1, Pallas kernels, forward(): pl.pallas_call(functools.partial(forward_kernel, (batches, rows, kv_heads...  207 us

profile of v8, /device:TPU:0, one launch (start us, length us, event | category | flops | bytes accessed | tf_op | source)
XLA Modules:
  0.0 505.1 jit_solution(18234439254603303757)
XLA Ops:
  0.6 0.6 compare_reduce_fusion.1
  1.3 0.6 compare_reduce_fusion
  1.9 1.3 fusion.1
  3.2 1.3 fusion
  4.6 0.6 broadcast_in_dim_tile.3.refs_7_
  5.2 0.1 copy.27
  5.3 0.1 copy.28
  5.4 0.1 scatter.9
  5.5 0.9 reshape.125
  6.4 0.9 reshape.126
  7.2 0.1 pad_maximum_fusion.1
  7.3 1.6 pad_maximum_fusion.refs_0_
  8.9 1.5 copy.29.refs_6_
  10.4 207.2 %shard_map.203 = (bf16[32,40,2048]{2,1,0:T(8,128)(2,1)}, bf16[32,40,1280]{2,1,0:T(8,128)(2,1)}, bf16[32,40,3584]{2,1,0:T(8,128)(2,1)}, bf16[32,40,3584]{2,1,0:T(...) custom-call(bf16[40,2048]{1,0:T(8,128)(2,1)} %pad_maximum_fusion.ref, ...), custom_call_target="tpu_custom_call" | custom-call | flops 13589544960 | bytes 71434240 | tf_op jit(solution)/shard_map/pallas_call | solution.py:573
  217.7 274.0 %shard_map.204 = (bf16[512,1280]{1,0:T(8,128)(2,1)}, bf16[512,1280]{1,0:T(8,128)(2,1)}, f32[40,2048]{1,0:T(8,128)}, f32[40,1280]{1,0:T(8,128)}, f32[40,3584]{1,0...) custom-call(bf16[512,1280]{1,0:T(8,128)(2,1)} %bitcast.26, ...), custom_call_target="tpu_custom_call" | custom-call | tf_op jit(solution)/shard_map/pallas_call | solution.py:1742
  491.7 0.0 copy-start
  491.7 1.5 slice_reduce_fusion.2
  493.3 0.9 slice.49
  494.2 1.6 slice.48
  495.8 0.2 reshape.139
  496.0 0.6 slice_reduce_fusion
  496.5 0.7 reshape_squeeze.7
  497.3 0.7 reshape_squeeze.6
  498.0 0.0 copy-start.4
  498.0 0.0 copy-start.3
  498.0 2.5 copy.42
  500.5 0.0 copy-done
  500.5 0.0 copy-start.2
  500.5 0.0 copy-start.1
  500.5 1.1 copy.43
  501.6 0.0 copy-done.4
  501.6 0.7 copy.44
  502.2 0.0 copy-done.3
  502.2 0.8 copy.45
  503.0 0.0 copy-done.2
  503.1 0.8 copy.46
  503.9 0.0 copy-done.1
  503.9 0.8 copy.47
  (4 shorter events, 0.0 us)
Async XLA Ops:
  491.7 8.8 %copy-start = (bf16[512,1280]{1,0:T(8,128)(2,1)S(1)}, bf16[512,1280]{1,0:T(8,128)(2,1)}, u32[]{:S(2)}) copy-start(bf16[512,1280]{1,0:T(8,128)(2,1)} %get-tuple-element.81) | copy-start | bytes 3932164
  498.0 3.6 copy-start.4
  498.0 4.3 copy-start.3
  500.5 2.6 copy-start.2
  500.5 3.4 copy-start.1

commit v9 on v8

--- a/solution.py
+++ b/solution.py
@@ -1364,7 +1364,6 @@
         over_rows(back_out, 256)
     comm.second(D0)
     comm.first(G0)
-    comm.second(D1)
 
     need_q.wait()
     need_kv.wait()
@@ -1469,16 +1468,17 @@
 
     count = batches * kv_heads
     lax.fori_loop(0, 2, head, 0)
+    comm.second(D1)
     comm.first(U0)
-    comm.third(D0)
     own_low.wait()
     got_low.wait_recv()
     lax.fori_loop(2, 5, head, 0)
-    comm.third(D1)
+    comm.third(D0)
     comm.second(G0)
     handed = to_sibling(0)
     comm.first(G1)
     lax.fori_loop(5, 8, head, 0)
+    comm.third(D1)
     comm.second(U0)
     comm.third(G0)
     comm.reuse(0)

time: 515 us -> 510 us (level)
    pallas_call x1, Pallas kernels: 274 us -> 268 us  [backward(): pl.pallas_call(functools.partial(backward_kernel, (batches, rows, kv_head...]
where the time goes in v9:
time: 510 us; the launch traced here: 500 us
  Pallas kernels  476 us (93%)
  local copies, waits for them, and re-layouts  17.1 us (3%)
  other arithmetic  5.58 us (1%)
    pallas_call x1, Pallas kernels, backward(): pl.pallas_call(functools.partial(backward_kernel, (batches, rows, kv_head...  268 us
    pallas_call x1, Pallas kernels, forward(): pl.pallas_call(functools.partial(forward_kernel, (batches, rows, kv_heads...  207 us

profile of v9, /device:TPU:0, one launch (start us, length us, event | category | flops | bytes accessed | tf_op | source)
XLA Modules:
  0.0 499.5 jit_solution(16405909932324674041)
XLA Ops:
  0.6 0.6 compare_reduce_fusion.1
  1.3 0.6 compare_reduce_fusion
  1.9 1.3 fusion.1
  3.2 1.3 fusion
  4.6 0.6 broadcast_in_dim_tile.3.refs_7_
  5.2 0.1 copy.27
  5.3 0.1 copy.28
  5.4 0.1 scatter.9
  5.5 0.9 reshape.125
  6.4 0.9 reshape.126
  7.2 0.1 pad_maximum_fusion.1
  7.3 1.6 pad_maximum_fusion.refs_0_
  8.9 1.5 copy.29.refs_6_
  10.4 207.2 %shard_map.203 = (bf16[32,40,2048]{2,1,0:T(8,128)(2,1)}, bf16[32,40,1280]{2,1,0:T(8,128)(2,1)}, bf16[32,40,3584]{2,1,0:T(8,128)(2,1)}, bf16[32,40,3584]{2,1,0:T(...) custom-call(bf16[40,2048]{1,0:T(8,128)(2,1)} %pad_maximum_fusion.ref, ...), custom_call_target="tpu_custom_call" | custom-call | flops 13589544960 | bytes 71434240 | tf_op jit(solution)/shard_map/pallas_call | solution.py:573
  217.7 268.4 %shard_map.204 = (bf16[512,1280]{1,0:T(8,128)(2,1)}, bf16[512,1280]{1,0:T(8,128)(2,1)}, f32[40,2048]{1,0:T(8,128)}, f32[40,1280]{1,0:T(8,128)}, f32[40,3584]{1,0...) custom-call(bf16[512,1280]{1,0:T(8,128)(2,1)} %bitcast.26, ...), custom_call_target="tpu_custom_call" | custom-call | tf_op jit(solution)/shard_map/pallas_call | solution.py:1742
  486.1 0.0 copy-start
  486.1 1.5 slice_reduce_fusion.2
  487.7 0.9 slice.49
  488.6 1.6 slice.48
  490.2 0.2 reshape.139
  490.4 0.6 slice_reduce_fusion
  491.0 0.7 reshape_squeeze.7
  491.7 0.7 reshape_squeeze.6
  492.4 0.0 copy-start.4
  492.4 0.0 copy-start.3
  492.4 2.5 copy.42
  494.9 0.0 copy-done
  494.9 0.0 copy-start.2
  494.9 0.0 copy-start.1
  494.9 1.1 copy.43
  496.0 0.0 copy-done.4
  496.0 0.7 copy.44
  496.6 0.0 copy-done.3
  496.7 0.8 copy.45
  497.5 0.0 copy-done.2
  497.5 0.8 copy.46
  498.3 0.0 copy-done.1
  498.3 0.8 copy.47
  (4 shorter events, 0.0 us)
Async XLA Ops:
  486.1 8.8 %copy-start = (bf16[512,1280]{1,0:T(8,128)(2,1)S(1)}, bf16[512,1280]{1,0:T(8,128)(2,1)}, u32[]{:S(2)}) copy-start(bf16[512,1280]{1,0:T(8,128)(2,1)} %get-tuple-element.81) | copy-start | bytes 3932164
  492.4 3.6 copy-start.4
  492.4 4.3 copy-start.3
  494.9 2.6 copy-start.2
  494.9 3.4 copy-start.1
